TPU v7x, 32 devices: a whole 2x2x4 slice. The times are simulated.
32 devices in a mesh: band: 4 (over y, x), expert: 8 (over z, core).
Axes of the slice: x: 2, y: 2, z: 4, core: 2. Of those that a mesh axis runs over, the one named last changes fastest.
Arguments:
- features: bfloat16 [8, 32, 64, 512], P('expert', None, 'band'), may hold values from -18 to 18
- routes: int32 [8, 4, 32, 16, 1], P('expert', 'band'), may hold values from 0 to 7; in each aligned block of 512 rows (0 to 511, 512 to 1023, ..., all dimensions but the last counted through in order) at most 128 rows name the same one
- qkv_regular: bfloat16 [512, 1536], replicated, may hold values from -0.25 to 0.25
- proj_regular: bfloat16 [512, 512], replicated, may hold values from -0.25 to 0.25
- table_regular: float32 [225, 16], replicated, may hold values from -4 to 4
- gain_regular: float32 [512], replicated, may hold values from 0.5 to 1.5
- mlp_up: bfloat16 [512, 2048], replicated, may hold values from -0.25 to 0.25
- mlp_down: bfloat16 [2048, 512], replicated, may hold values from -0.125 to 0.125
- gain_mlp: float32 [512], replicated, may hold values from 0.5 to 1.5
- qkv_shifted: bfloat16 [512, 1536], replicated, may hold values from -0.25 to 0.25
- proj_shifted: bfloat16 [512, 512], replicated, may hold values from -0.25 to 0.25
- table_shifted: float32 [225, 16], replicated, may hold values from -4 to 4
- gain_shifted: float32 [512], replicated, may hold values from 0.5 to 1.5
- expert_in: bfloat16 [8, 512, 2048], P('expert', None, 'band'), may hold values from -0.25 to 0.25
- expert_out: bfloat16 [8, 2048, 512], P('expert', 'band'), may hold values from -0.125 to 0.125
- gain_expert: float32 [512], replicated, may hold values from 0.5 to 1.5
Outputs:
- encoded: bfloat16 [8, 32, 64, 512], P('expert', None, 'band')
Inputs may be any that keep to these rules, and one draw needn't show every extreme that they name: `routes`: within one crop and one band (an aligned block of 512 tokens) no expert is named by more than 128 tokens, a bound that some block reaches.
All inputs are finite; a program needn't handle non-finite values.
Results may differ from a plain program's by a relative error of at most 0.015.
Values may be sent and summed in bfloat16 or wider, within the bound.
No kernel may reach another device: no remote copies, remote signals or barrier semaphores. Data moves between devices by JAX's collectives and lax.ppermute only.
A program may use at most 128 MiB of HBM per device.

v0:
```python
import functools
import math

import jax
import jax.numpy as jnp
from jax import lax
from jax.experimental import pallas as pl
from jax.experimental.pallas import tpu as pltpu
from jax.sharding import PartitionSpec as P

HEADS = 16
WIN = 8
HALF = WIN // 2
SPAN = 2 * WIN - 1
LANES = 128
LOG2E = math.log2(math.e)
CLOSED = -1e30
MASKED = -100.0 * LOG2E
BF = jnp.bfloat16
F32 = jnp.float32
I32 = jnp.int32

NN = (((1,), (0,)), ((), ()))
NT = (((1,), (1,)), ((), ()))


def dot(a, b, dims=NN):
    return lax.dot_general(a, b, dims, preferred_element_type=F32)


def iota(shape, dim):
    return lax.broadcasted_iota(I32, shape, dim)


def gelu(x):
    return 0.5 * x * (1.0 + lax.erf(x * math.sqrt(0.5)))


def layer_norm(values, gain):
    centre = jnp.mean(values, axis=-1, keepdims=True)
    offsets = values - centre
    spread = jnp.mean(offsets * offsets, axis=-1, keepdims=True)
    return offsets * lax.rsqrt(spread + 1e-05) * gain


def pick(row, idx):
    low = jnp.broadcast_to(row[:, :LANES], idx.shape)
    high = jnp.broadcast_to(row[:, LANES:], idx.shape)
    from_low = jnp.take_along_axis(
        low, jnp.minimum(idx, LANES - 1), axis=1, mode="promise_in_bounds"
    )
    from_high = jnp.take_along_axis(
        high, jnp.maximum(idx - LANES, 0), axis=1, mode="promise_in_bounds"
    )
    return jnp.where(idx < LANES, from_low, from_high)


def offset_index(row_p, col_p, row_q, col_q):
    return (row_p - row_q + WIN - 1) * SPAN + (col_p - col_q + WIN - 1)


def own_bias(tab_ref, first_head, bias_ref, band_width, shift):
    strip = WIN * band_width
    p, q = iota((strip, strip), 0), iota((strip, strip), 1)
    row_p, col_p = lax.div(p, band_width), lax.rem(p, band_width) + shift
    row_q, col_q = lax.div(q, band_width), lax.rem(q, band_width) + shift
    idx = offset_index(row_p, lax.rem(col_p, WIN), row_q, lax.rem(col_q, WIN))
    same = lax.div(col_p, WIN) == lax.div(col_q, WIN)
    for h in range(HEADS):
        row = tab_ref[first_head + h : first_head + h + 1, :]
        tile, part = divmod(h, 4)
        bias_ref[tile, :, part * strip : (part + 1) * strip] = jnp.where(
            same, pick(row, idx), CLOSED
        )


def halo_places(band_width):
    strip, halo = WIN * band_width, 2 * WIN * HALF
    p, q = iota((strip, 2 * halo), 0), iota((strip, 2 * halo), 1)
    row_p, col_p = lax.div(p, band_width), lax.rem(p, band_width) + HALF
    key = lax.rem(q, halo)
    right = key >= WIN * HALF
    cell = lax.rem(key, WIN * HALF)
    row_q = lax.div(cell, HALF)
    col_q = lax.rem(cell, HALF) + jnp.where(right, band_width + HALF, 0)
    return row_p, col_p, row_q, col_q, right, q < halo


def halo_bias(tab_ref, first_head, bias_ref, band_width, at_first, at_last):
    row_p, col_p, row_q, col_q, right, front = halo_places(band_width)
    idx = offset_index(row_p, lax.rem(col_p, WIN), row_q, lax.rem(col_q, WIN))
    same = lax.div(col_p, WIN) == lax.div(col_q, WIN)
    edge = jnp.where(right, at_last, at_first) > 0
    wide = front.shape[1]
    for pair in range(HEADS // 2):
        h = first_head + 2 * pair
        value = jnp.where(
            front, pick(tab_ref[h : h + 1, :], idx), pick(tab_ref[h + 1 : h + 2, :], idx)
        )
        value = jnp.where(same, value + jnp.where(edge, MASKED, 0.0), CLOSED)
        tile, part = divmod(pair, 2)
        bias_ref[tile, :, part * wide : (part + 1) * wide] = value


def head_masks(parts):
    lane_head = lax.div(iota((1, LANES), 1), LANES // parts)
    return [jnp.where(lane_head == h, 1.0, 0.0).astype(BF) for h in range(parts)]


def sum_columns(keys, parts):
    shape = (parts * keys, LANES)
    return jnp.where(
        lax.div(iota(shape, 0), keys) == lax.div(iota(shape, 1), LANES // parts), 1.0, 0.0
    ).astype(BF)


def by_head(block, masks):
    return jnp.concatenate([block * mask for mask in masks], axis=0)


def front_kernel(
    band_width,
    x_ref,
    wqkv_ref,
    wproj_ref,
    tab_ref,
    gain_ref,
    up_ref,
    down_ref,
    gain_mlp_ref,
    out_ref,
    left_ref,
    right_ref,
    qkv,
    bias,
    heads,
    second,
):
    rows, width = x_ref.shape
    strip = WIN * band_width
    head_dim = width // HEADS
    parts = LANES // head_dim
    x = x_ref[...]
    for part in range(3):
        cols = slice(part * width, (part + 1) * width)
        product = dot(x, wqkv_ref[:, cols])
        if part == 0:
            product = product * (LOG2E * head_dim**-0.5)
        qkv[:, cols] = product.astype(BF)
    own_bias(tab_ref, 0, bias, band_width, 0)
    masks = head_masks(parts)
    ones = sum_columns(strip, parts)

    def tile_step(t, carry):
        lanes = pl.ds(pl.multiple_of(t * LANES, LANES), LANES)
        lanes_k = pl.ds(pl.multiple_of(width + t * LANES, LANES), LANES)
        lanes_v = pl.ds(pl.multiple_of(2 * width + t * LANES, LANES), LANES)
        bias_tile = bias.at[t]
        for g in range(rows // strip):
            tokens = slice(g * strip, (g + 1) * strip)
            keys = by_head(qkv[tokens, lanes_k], masks)
            scores = dot(qkv[tokens, lanes], keys, NT) + bias_tile[...]
            probs = []
            for h in range(parts):
                s = scores[:, h * strip : (h + 1) * strip]
                probs.append(jnp.exp2(s - jnp.max(s, axis=-1, keepdims=True)).astype(BF))
            values = jnp.concatenate([by_head(qkv[tokens, lanes_v], masks), ones], axis=1)
            both = dot(jnp.concatenate(probs, axis=1), values)
            heads[tokens, lanes] = (both[:, :LANES] / both[:, LANES:]).astype(BF)
        return carry

    lax.fori_loop(0, width // LANES, tile_step, 0)

    half = rows // 2
    hidden = up_ref.shape[1]
    for r in range(2):
        tokens = slice(r * half, (r + 1) * half)
        projected = dot(heads[tokens, :], wproj_ref[...])
        first = (x_ref[tokens, :].astype(F32) + layer_norm(projected, gain_ref[...])).astype(BF)
        total = jnp.zeros((half, width), F32)
        for f in range(hidden // width):
            cols = slice(f * width, (f + 1) * width)
            act = gelu(dot(first, up_ref[:, cols])).astype(BF)
            total = total + dot(act, down_ref[cols, :])
        second[tokens, :] = (first.astype(F32) + layer_norm(total, gain_mlp_ref[...])).astype(BF)
    turn = HALF * band_width
    rolled = jnp.concatenate([second[turn:, :], second[:turn, :]], axis=0)
    out_ref[...] = rolled
    sent = left_ref.shape[0]
    r, t = iota((sent, rows), 0), iota((sent, rows), 1)
    place = lax.div(r, HALF) * band_width + lax.rem(r, HALF)
    left_ref[...] = dot(jnp.where(t == place, 1.0, 0.0).astype(BF), rolled).astype(BF)
    place = place + (band_width - HALF)
    right_ref[...] = dot(jnp.where(t == place, 1.0, 0.0).astype(BF), rolled).astype(BF)


def middle_kernel(
    band_width,
    experts,
    capacity,
    info_ref,
    x_ref,
    wqkv_ref,
    tab_ref,
    routes_ref,
    qkv_ref,
    bias_ref,
    bias_halo_ref,
    slot_row_ref,
    slot_col_ref,
):
    rows, width = x_ref.shape
    head_dim = width // HEADS
    x = x_ref[...]
    for part in range(3):
        cols = slice(part * width, (part + 1) * width)
        product = dot(x, wqkv_ref[:, cols])
        if part == 0:
            product = product * (LOG2E * head_dim**-0.5)
        qkv_ref[:, cols] = product.astype(BF)
    own_bias(tab_ref, HEADS, bias_ref, band_width, HALF)
    halo_bias(tab_ref, HEADS, bias_halo_ref, band_width, info_ref[0], info_ref[1])
    routes = routes_ref[...]
    named = jnp.where(iota((experts, rows), 0) == routes, 1.0, 0.0)
    a, b = iota((rows, rows), 0), iota((rows, rows), 1)
    upto = jnp.where(a <= b, 1.0, 0.0).astype(BF)
    count = dot(named.astype(BF), upto)
    base = iota((experts, rows), 0).astype(F32) * capacity - 1.0
    slot = jnp.sum(named * (count + base), axis=0, keepdims=True)
    slot_row_ref[...] = jnp.broadcast_to(slot, slot_row_ref.shape).astype(I32)
    same = jnp.where(a == b, 1.0, 0.0).astype(BF)
    named_col = dot(same, named.astype(BF), NT)
    before = jnp.where(a >= b, 1.0, 0.0).astype(BF)
    count_col = dot(before, named_col.astype(BF))
    base_col = iota((rows, experts), 1).astype(F32) * capacity - 1.0
    slot_col = jnp.sum(named_col * (count_col + base_col), axis=1, keepdims=True)
    slot_col_ref[...] = jnp.broadcast_to(slot_col, slot_col_ref.shape).astype(I32)


def shifted_kernel(
    band_width,
    capacity,
    info_ref,
    qkv_ref,
    x_ref,
    from_left_ref,
    from_right_ref,
    wqkv_ref,
    bias_ref,
    bias_halo_ref,
    wproj_ref,
    gain_ref,
    slot_row_ref,
    *rest,
):
    third_ref, *out_refs, halo_kv, heads = rest
    rows, width = x_ref.shape
    strip = WIN * band_width
    side = WIN * HALF
    halo = 2 * side
    groups = rows // strip
    head_dim = width // HEADS
    parts = LANES // head_dim
    arrived = jnp.concatenate(
        [
            ref[g * side : (g + 1) * side, :]
            for g in range(groups)
            for ref in (from_left_ref, from_right_ref)
        ],
        axis=0,
    )
    halo_kv[...] = dot(arrived, wqkv_ref[:, width:]).astype(BF)
    masks = head_masks(parts)
    ones = jnp.concatenate([sum_columns(strip, parts), sum_columns(halo, parts)], axis=0)
    p, q = iota((strip, strip), 0), iota((strip, strip), 1)
    turned = HALF * band_width
    apart = jnp.where((p < turned) != (q < turned), MASKED, 0.0)
    row_p, _, row_q, _, right, front = halo_places(band_width)
    edge = jnp.where(right, info_ref[1], info_ref[0]) > 0
    crossed = (row_p < HALF) != (row_q < HALF)
    apart_halo = jnp.where(jnp.logical_and(crossed, jnp.logical_not(edge)), MASKED, 0.0)
    wide = 2 * halo

    def tile_step(t, carry):
        lanes = pl.ds(pl.multiple_of(t * LANES, LANES), LANES)
        lanes_k = pl.ds(pl.multiple_of(width + t * LANES, LANES), LANES)
        lanes_v = pl.ds(pl.multiple_of(2 * width + t * LANES, LANES), LANES)
        bias_tile = bias_ref.at[t]
        bias_halo_tile = bias_halo_ref.at[t]
        for g in range(groups):
            tokens = slice(g * strip, (g + 1) * strip)
            outside = slice(g * halo, (g + 1) * halo)
            queries = qkv_ref[tokens, lanes]
            scores = dot(queries, by_head(qkv_ref[tokens, lanes_k], masks), NT)
            scores = scores + bias_tile[...]
            scores_halo = dot(queries, by_head(halo_kv[outside, lanes], masks), NT)
            scores_halo = scores_halo + bias_halo_tile[...]
            probs, probs_halo = [], []
            for pair in range(parts // 2):
                s_halo = scores_halo[:, pair * wide : (pair + 1) * wide]
                if g == groups - 1:
                    s_halo = s_halo + apart_halo
                tops = []
                for k in range(2):
                    h = 2 * pair + k
                    s = scores[:, h * strip : (h + 1) * strip]
                    if g == groups - 1:
                        s = s + apart
                    mine = front if k == 0 else jnp.logical_not(front)
                    top = jnp.max(
                        jnp.maximum(s, jnp.where(mine, s_halo, CLOSED)), axis=-1, keepdims=True
                    )
                    tops.append(top)
                    probs.append(jnp.exp2(s - top).astype(BF))
                probs_halo.append(
                    jnp.exp2(s_halo - jnp.where(front, tops[0], tops[1])).astype(BF)
                )
            values = jnp.concatenate(
                [by_head(qkv_ref[tokens, lanes_v], masks), by_head(halo_kv[outside, lanes_k], masks)],
                axis=0,
            )
            both = dot(
                jnp.concatenate(probs + probs_halo, axis=1),
                jnp.concatenate([values, ones], axis=1),
            )
            heads[tokens, lanes] = (both[:, :LANES] / both[:, LANES:]).astype(BF)
        return carry

    lax.fori_loop(0, width // LANES, tile_step, 0)
    projected = dot(heads[...], wproj_ref[...])
    third = (x_ref[...].astype(F32) + layer_norm(projected, gain_ref[...])).astype(BF)
    third_ref[...] = third
    slot = slot_row_ref[0:1, :]
    for s, ref in enumerate(out_refs):
        places = iota((capacity, rows), 0) + s * capacity
        ref[...] = dot(jnp.where(places == slot, 1.0, 0.0).astype(BF), third).astype(BF)


def expert_kernel(amount, quarters, *refs):
    x_refs, rest = refs[:amount], refs[amount:]
    in_refs, rest = rest[:quarters], rest[quarters:]
    out_w_refs, out_refs = rest[:quarters], rest[quarters:]
    x = jnp.concatenate([ref[...] for ref in x_refs], axis=0)
    total = jnp.zeros(x.shape, F32)
    for w_in, w_out in zip(in_refs, out_w_refs):
        total = total + dot(gelu(dot(x, w_in[...])).astype(BF), w_out[...])
    each = x_refs[0].shape[0]
    for k, ref in enumerate(out_refs):
        ref[...] = total[k * each : (k + 1) * each, :].astype(BF)


def final_kernel(band_width, capacity, third_ref, slot_col_ref, gain_ref, *rest):
    *result_refs, out_ref = rest
    rows, width = third_ref.shape
    results = jnp.concatenate([ref[...] for ref in result_refs], axis=0)
    slot = slot_col_ref[...]
    chosen = jnp.concatenate(
        [
            jnp.where(slot == iota(slot.shape, 1) + k * LANES, 1.0, 0.0).astype(BF)
            for k in range(results.shape[0] // LANES)
        ],
        axis=1,
    )
    picked = dot(chosen, results)
    encoded = (third_ref[...].astype(F32) + layer_norm(picked, gain_ref[...])).astype(BF)
    turn = HALF * band_width
    out_ref[turn:, :] = encoded[: rows - turn, :]
    out_ref[:turn, :] = encoded[rows - turn :, :]


def call(kernel, outs, ins, scratch=(), scalars=0, limit=32, flops=0):
    vmem = pl.BlockSpec(memory_space=pltpu.VMEM)
    smem = pl.BlockSpec(memory_space=pltpu.SMEM)
    size = sum(math.prod(a.shape) * a.dtype.itemsize for a in list(ins) + list(outs))
    return pl.pallas_call(
        kernel,
        out_shape=outs,
        in_specs=[smem] * scalars + [vmem] * (len(ins) - scalars),
        out_specs=[vmem] * len(outs),
        scratch_shapes=list(scratch),
        compiler_params=pltpu.CompilerParams(vmem_limit_bytes=limit << 20),
        cost_estimate=pl.CostEstimate(flops=flops, bytes_accessed=size, transcendentals=0),
    )(*ins)


def shape_of(*dims, dtype=BF):
    return jax.ShapeDtypeStruct(dims, dtype)


def swap(block, axis, bits):
    return lax.ppermute(block, axis, [(i, i ^ bits) for i in range(lax.axis_size(axis))])


def gather_blocks(block, axis, steps):
    blocks = {0: block}
    for bit in steps:
        blocks.update({at ^ bit: swap(held, axis, bit) for at, held in list(blocks.items())})
    return [blocks[at] for at in range(len(blocks))]


def local(
    features,
    routes,
    qkv_regular,
    proj_regular,
    table_regular,
    gain_regular,
    mlp_up,
    mlp_down,
    gain_mlp,
    qkv_shifted,
    proj_shifted,
    table_shifted,
    gain_shifted,
    expert_in,
    expert_out,
    gain_expert,
):
    crop_count, height, band_width, width = features.shape
    rows = height * band_width
    band_count = lax.axis_size("band")
    band_index = lax.axis_index("band")
    experts = lax.axis_size("expert")
    capacity = 2 * rows // experts
    hidden = mlp_up.shape[1]
    strip = WIN * band_width
    tiles = width // LANES
    wide = LANES // (width // HEADS) * strip
    wide_halo = LANES // (width // HEADS) * 2 * WIN * HALF
    sent = height * HALF

    steps = [1 << k for k in range(band_count.bit_length() - 1)]
    weights_in = gather_blocks(expert_in[0], "band", steps)
    weights_out = gather_blocks(expert_out[0], "band", steps[::-1])

    tables = jnp.concatenate([table_regular, table_shifted], axis=1).T * LOG2E
    tables = jnp.pad(tables, ((0, 0), (0, 2 * LANES - tables.shape[1])))
    info = jnp.stack([band_index == 0, band_index == band_count - 1]).astype(I32)
    turn = HALF * band_width
    route_row = jnp.roll(routes.reshape(1, rows), -turn, axis=1) ^ lax.axis_index("expert")

    second, to_left, to_right = call(
        functools.partial(front_kernel, band_width),
        [shape_of(rows, width), shape_of(sent, width), shape_of(sent, width)],
        [
            features.reshape(rows, width),
            qkv_regular,
            proj_regular,
            tables,
            gain_regular.reshape(1, width),
            mlp_up,
            mlp_down,
            gain_mlp.reshape(1, width),
        ],
        [
            pltpu.VMEM((rows, 3 * width), BF),
            pltpu.VMEM((tiles, strip, wide), F32),
            pltpu.VMEM((rows, width), BF),
            pltpu.VMEM((rows, width), BF),
        ],
        flops=2 * rows * width * (4 * width + 2 * hidden),
    )
    ring = range(band_count)
    from_right = lax.ppermute(to_left, "band", [(i, (i - 1) % band_count) for i in ring])
    from_left = lax.ppermute(to_right, "band", [(i, (i + 1) % band_count) for i in ring])
    qkv, bias, bias_halo, slot_row, slot_col = call(
        functools.partial(middle_kernel, band_width, experts, capacity),
        [
            shape_of(rows, 3 * width),
            shape_of(tiles, strip, wide, dtype=F32),
            shape_of(tiles, strip, wide_halo, dtype=F32),
            shape_of(8, rows, dtype=I32),
            shape_of(rows, LANES, dtype=I32),
        ],
        [info, second, qkv_shifted, tables, route_row],
        scalars=1,
        flops=2 * rows * width * 3 * width,
    )
    third, *outgoing = call(
        functools.partial(shifted_kernel, band_width, capacity),
        [shape_of(rows, width)] + [shape_of(capacity, width)] * experts,
        [
            info,
            qkv,
            second,
            from_left,
            from_right,
            qkv_shifted,
            bias,
            bias_halo,
            proj_shifted,
            gain_shifted.reshape(1, width),
            slot_row,
        ],
        [
            pltpu.VMEM((2 * sent, 2 * width), BF),
            pltpu.VMEM((rows, width), BF),
        ],
        scalars=1,
        flops=2 * rows * width * 4 * width,
    )
    arrived = [outgoing[0]] + [swap(outgoing[s], "expert", s) for s in range(1, experts)]
    amount = experts // 4
    results = []
    for k in range(0, experts, amount):
        results += call(
            functools.partial(expert_kernel, amount, band_count),
            [shape_of(capacity, width)] * amount,
            arrived[k : k + amount] + weights_in + weights_out,
            flops=4 * amount * capacity * width * hidden,
        )
    returned = [results[0]] + [swap(results[s], "expert", s) for s in range(1, experts)]
    encoded = call(
        functools.partial(final_kernel, band_width, capacity),
        [shape_of(rows, width)],
        [third, slot_col, gain_expert.reshape(1, width)] + returned,
        flops=2 * rows * width * 2 * rows,
    )[0]
    return encoded.reshape(crop_count, height, band_width, width)


def solution(mesh):
    return jax.shard_map(
        local,
        mesh=mesh,
        in_specs=(
            P("expert", None, "band", None),
            P("expert", "band", None, None, None),
        )
        + (P(),) * 11
        + (
            P("expert", None, "band"),
            P("expert", "band", None),
            P(),
        ),
        out_specs=P("expert", None, "band", None),
        check_vma=False,
    )
```

profile of v0, /device:TPU:1, one launch (start us, length us, event | category | flops | bytes accessed | tf_op | source)
XLA Modules:
  0.0 102.8 jit_solution(10969353802314277523)
XLA Ops:
  0.0 2.0 %collective-permute-start.3 = (bf16[512,512]{1,0:T(8,128)(2,1)}, bf16[512,512]{1,0:T(8,128)(2,1)S(1)}, u32[]{:S(2)}, u32[]{:S(2)}) collective-permute-start(bf16[512,512]{1,0:T(8,128)(2,1)} %bitcast.16), channel_id=1, source_target_pairs={{0,8},{8,0},{16,24},{24,16},{1,9},{9,1},{17,25},{25,17},{2,10},{10... | collective-permute-start | bytes 1572872 | tf_op jit(solution)/shard_map/ppermute | solution.py:391
  2.0 1.2 %collective-permute-start.7 = (bf16[512,512]{1,0:T(8,128)(2,1)}, bf16[512,512]{1,0:T(8,128)(2,1)S(1)}, u32[]{:S(2)}, u32[]{:S(2)}) collective-permute-start(bf16[512,512]{1,0:T(8,128)(2,1)} %bitcast.22), channel_id=1, source_target_pairs={{0,16},{8,24},{16,0},{24,8},{1,17},{9,25},{17,1},{25,9},{2,18},{10... | collective-permute-start | bytes 1572872 | tf_op jit(solution)/shard_map/ppermute | solution.py:391
  3.3 0.7 fusion
  4.0 1.6 %copy-done.10 = bf16[512,2048]{1,0:T(8,128)(2,1)S(1)} copy-done((bf16[512,2048]{1,0:T(8,128)(2,1)S(1)}, bf16[512,2048]{1,0:T(8,128)(2,1)}, u32[]{:S(2)}) %copy-start.10) | copy-done | bytes 2097176
  5.6 1.6 %copy-done.11 = bf16[2048,512]{1,0:T(8,128)(2,1)S(1)} copy-done((bf16[2048,512]{1,0:T(8,128)(2,1)S(1)}, bf16[2048,512]{1,0:T(8,128)(2,1)}, u32[]{:S(2)}) %copy-start.11) | copy-done | bytes 2097176
  7.2 1.4 %copy-done.12 = bf16[512,1536]{1,0:T(8,128)(2,1)S(1)} copy-done((bf16[512,1536]{1,0:T(8,128)(2,1)S(1)}, bf16[512,1536]{1,0:T(8,128)(2,1)}, u32[]{:S(2)}) %copy-start.12) | copy-done | bytes 1572888
  8.6 1.0 %copy-done.13 = bf16[1,32,16,512]{3,2,1,0:T(8,128)(2,1)S(1)} copy-done((bf16[1,32,16,512]{3,2,1,0:T(8,128)(2,1)S(1)}, bf16[1,32,16,512]{3,2,1,0:T(8,128)(2,1)}, u32[]{:S(2)}) %copy-start.13) | copy-done | bytes 524312
  9.7 1.0 %copy-done.14 = bf16[512,512]{1,0:T(8,128)(2,1)S(1)} copy-done((bf16[512,512]{1,0:T(8,128)(2,1)S(1)}, bf16[512,512]{1,0:T(8,128)(2,1)}, u32[]{:S(2)}) %copy-start.14) | copy-done | bytes 524312
  10.7 0.7 copy-done.15
  11.4 0.7 copy-done.16
  12.1 9.2 %shard_map.154 = (bf16[512,512]{1,0:T(8,128)(2,1)S(1)}, bf16[128,512]{1,0:T(8,128)(2,1)S(1)}, bf16[128,512]{1,0:T(8,128)(2,1)}) custom-call(bf16[512,512]{1,0:T(8,128)(2,1)S(1)} %bitcast.30, bf16[512,1536]{1,0:T(8,128)(2,1)S(1)} %copy-done.12, bf16[512,512]{1,0:T(8,128)(2,1)S(1)} %copy-done.14, f32[32,256]{1,0:T(8,128)S(1)} %pad.4.tab_ref, ...), custom_call_target="tpu_custom_call" | custom-call | flops 3221225472 | bytes 7639040 | tf_op jit(solution)/shard_map/pallas_call | solution.py:375
  21.3 0.8 copy-done.5
  22.1 0.3 collective-permute-start
  22.4 2.4 %collective-permute-start.6 = (bf16[512,512]{1,0:T(8,128)(2,1)S(1)}, bf16[512,512]{1,0:T(8,128)(2,1)S(1)}, u32[]{:S(2)}, u32[]{:S(2)}) collective-permute-start(bf16[512,512]{1,0:T(8,128)(2,1)S(1)} %bitcast.23), channel_id=1, source_target_pairs={{0,8},{8,0},{16,24},{24,16},{1,9},{9,1},{17,25},{25,17},{2,10},{10... | collective-permute-start | bytes 1572872 | tf_op jit(solution)/shard_map/ppermute | solution.py:391
  24.8 0.1 reshape.52
  24.9 0.1 slice.10
  25.0 0.1 add_xor_fusion.routes_ref
  25.1 2.1 %collective-permute-done.from_left_ref = bf16[128,512]{1,0:T(8,128)(2,1)S(1)} collective-permute-done((bf16[128,512]{1,0:T(8,128)(2,1)}, bf16[128,512]{1,0:T(8,128)(2,1)S(1)}, u32[]{:S(2)}, u32[]{:S(2)}) %collective-permute-start) | collective-permute-done | bytes 131104 | tf_op jit(solution)/shard_map/ppermute | solution.py:465
  27.1 0.4 collective-permute-start.5
  27.6 1.3 %collective-permute-start.8 = (bf16[512,512]{1,0:T(8,128)(2,1)S(1)}, bf16[512,512]{1,0:T(8,128)(2,1)S(1)}, u32[]{:S(2)}, u32[]{:S(2)}) collective-permute-start(bf16[512,512]{1,0:T(8,128)(2,1)S(1)} %collective-permute-done.7.refs_8_), channel_id=1, source_target_pairs={{0,8},{8,0},{16,24},{24,16},{1,9},{9,1},{17,25},{25,17},{2,10},{10... | collective-permute-start | bytes 1572872 | tf_op jit(solution)/shard_map/ppermute | solution.py:391
  28.9 1.4 %copy-done.2 = bf16[512,1536]{1,0:T(8,128)(2,1)S(1)} copy-done((bf16[512,1536]{1,0:T(8,128)(2,1)S(1)}, bf16[512,1536]{1,0:T(8,128)(2,1)}, u32[]{:S(2)}) %copy-start.2) | copy-done | bytes 1572888
  30.3 1.0 %copy-done.6 = bf16[512,512]{1,0:T(8,128)(2,1)S(1)} copy-done((bf16[512,512]{1,0:T(8,128)(2,1)S(1)}, bf16[512,512]{1,0:T(8,128)(2,1)}, u32[]{:S(2)}) %copy-start.6) | copy-done | bytes 524312
  31.4 3.6 %shard_map.155 = (bf16[512,1536]{1,0:T(8,128)(2,1)S(1)}, f32[4,128,512]{2,1,0:T(8,128)S(1)}, f32[4,128,256]{2,1,0:T(8,128)S(1)}, s32[8,512]{1,0:T(8,128)S(1)}, s32[512,128]{1,0:T(8,128)S(1)}) custom-call(s32[2]{0:T(128)S(1)} %add_convert_fusion.info_ref, bf16[512,512]{1,0:T(8,128)(2,1)S(1)} %copy-done.6, bf16[512,1536]{1,0:T(8,128)(2,1)S(1)} %copy-done.2, ...), custom_call_target="tpu_custom_call" | custom-call | flops 805306368 | bytes 5556232 | tf_op jit(solution)/shard_map/pallas_call | solution.py:375
  35.0 5.1 %collective-permute-done.1.from_right_ref = bf16[128,512]{1,0:T(8,128)(2,1)S(1)} collective-permute-done((bf16[128,512]{1,0:T(8,128)(2,1)S(1)}, bf16[128,512]{1,0:T(8,128)(2,1)S(1)}, u32[]{:S(2)}, u32[]{:S(2)}) %collective-permute-start.1) | collective-permute-done | bytes 131104 | tf_op jit(solution)/shard_map/ppermute | solution.py:464
  40.1 6.3 %shard_map.156 = (bf16[512,512]{1,0:T(8,128)(2,1)S(1)}, bf16[128,512]{1,0:T(8,128)(2,1)S(1)}, bf16[128,512]{1,0:T(8,128)(2,1)S(1)}, bf16[128,512]{1,0:T(8,128)(2...) custom-call(s32[2]{0:T(128)S(1)} %add_convert_fusion.info_ref, ...), custom_call_target="tpu_custom_call" | custom-call | flops 1073741824 | bytes 7620616 | tf_op jit(solution)/shard_map/pallas_call | solution.py:375
  46.5 3.4 %collective-permute-start.18 = (bf16[128,512]{1,0:T(8,128)(2,1)S(1)}, bf16[128,512]{1,0:T(8,128)(2,1)S(1)}, u32[]{:S(2)}, u32[]{:S(2)}) collective-permute-start(bf16[128,512]{1,0:T(8,128)(2,1)S(1)} %get-tuple-element.51), channel_id=1, source_target_pairs={{0,6},{1,7},{2,4},{3,5},{4,2},{5,3},{6,0},{7,1},{8,14},{9,15},{10,... | collective-permute-start | bytes 393224 | tf_op jit(solution)/shard_map/ppermute | solution.py:391
  49.9 2.5 %collective-permute-done.18.refs_0_ = bf16[128,512]{1,0:T(8,128)(2,1)S(1)} collective-permute-done((bf16[128,512]{1,0:T(8,128)(2,1)S(1)}, bf16[128,512]{1,0:T(8,128)(2,1)S(1)}, u32[]{:S(2)}, u32[]{:S(2)}) %collective-permute-start.18) | collective-permute-done | bytes 131104 | tf_op jit(solution)/shard_map/ppermute | solution.py:391
  52.4 8.0 %collective-permute-start.19 = (bf16[128,512]{1,0:T(8,128)(2,1)S(1)}, bf16[128,512]{1,0:T(8,128)(2,1)S(1)}, u32[]{:S(2)}, u32[]{:S(2)}) collective-permute-start(bf16[128,512]{1,0:T(8,128)(2,1)S(1)} %get-tuple-element.52), channel_id=1, source_target_pairs={{0,7},{1,6},{2,5},{3,4},{4,3},{5,2},{6,1},{7,0},{8,15},{9,14},{10,... | collective-permute-start | bytes 393224 | tf_op jit(solution)/shard_map/ppermute | solution.py:391
  60.4 3.9 %collective-permute-done.19.refs_1_ = bf16[128,512]{1,0:T(8,128)(2,1)S(1)} collective-permute-done((bf16[128,512]{1,0:T(8,128)(2,1)S(1)}, bf16[128,512]{1,0:T(8,128)(2,1)S(1)}, u32[]{:S(2)}, u32[]{:S(2)}) %collective-permute-start.19) | collective-permute-done | bytes 131104 | tf_op jit(solution)/shard_map/ppermute | solution.py:391
  64.3 1.3 %collective-permute-start.14 = (bf16[128,512]{1,0:T(8,128)(2,1)S(1)}, bf16[128,512]{1,0:T(8,128)(2,1)S(1)}, u32[]{:S(2)}, u32[]{:S(2)}) collective-permute-start(bf16[128,512]{1,0:T(8,128)(2,1)S(1)} %get-tuple-element.47), channel_id=1, source_target_pairs={{0,4},{1,5},{2,6},{3,7},{4,0},{5,1},{6,2},{7,3},{8,12},{9,13},{10,... | collective-permute-start | bytes 393224 | tf_op jit(solution)/shard_map/ppermute | solution.py:391
  65.6 1.7 %collective-permute-start.15 = (bf16[128,512]{1,0:T(8,128)(2,1)S(1)}, bf16[128,512]{1,0:T(8,128)(2,1)S(1)}, u32[]{:S(2)}, u32[]{:S(2)}) collective-permute-start(bf16[128,512]{1,0:T(8,128)(2,1)S(1)} %get-tuple-element.48), channel_id=1, source_target_pairs={{0,5},{1,4},{2,7},{3,6},{4,1},{5,0},{6,3},{7,2},{8,13},{9,12},{10,... | collective-permute-start | bytes 393224 | tf_op jit(solution)/shard_map/ppermute | solution.py:391
  67.3 0.7 collective-permute-start.10
  67.9 0.8 collective-permute-start.11
  68.7 0.4 collective-permute-start.2
  69.1 1.6 %shard_map.160 = (bf16[128,512]{1,0:T(8,128)(2,1)S(1)}, bf16[128,512]{1,0:T(8,128)(2,1)S(1)}) custom-call(bf16[128,512]{1,0:T(8,128)(2,1)S(1)} %collective-permute-done.18.refs_0_, bf16[128,512]{1,0:T(8,128)(2,1)S(1)} %collective-permute-done.19.refs_1_, bf16[512,512]{1,0:T(8,128)(2,1)S(1)} %bitcast.18, bf16[512,512]{1,0:T(8,128)(2,1)S(1)} %collective-permute-done.3.refs_3_, ...), custom_call_target="tpu_custom_call" | custom-call | flops 1073741824 | bytes 4718592 | tf_op jit(solution)/shard_map/pallas_call | solution.py:375
  70.7 3.3 %collective-permute-done.14.refs_0_ = bf16[128,512]{1,0:T(8,128)(2,1)S(1)} collective-permute-done((bf16[128,512]{1,0:T(8,128)(2,1)S(1)}, bf16[128,512]{1,0:T(8,128)(2,1)S(1)}, u32[]{:S(2)}, u32[]{:S(2)}) %collective-permute-start.14) | collective-permute-done | bytes 131104 | tf_op jit(solution)/shard_map/ppermute | solution.py:391
  74.0 4.3 %collective-permute-done.15.refs_1_ = bf16[128,512]{1,0:T(8,128)(2,1)S(1)} collective-permute-done((bf16[128,512]{1,0:T(8,128)(2,1)S(1)}, bf16[128,512]{1,0:T(8,128)(2,1)S(1)}, u32[]{:S(2)}, u32[]{:S(2)}) %collective-permute-start.15) | collective-permute-done | bytes 131104 | tf_op jit(solution)/shard_map/ppermute | solution.py:391
  78.4 1.4 %collective-permute-start.21 = (bf16[128,512]{1,0:T(8,128)(2,1)S(1)}, bf16[128,512]{1,0:T(8,128)(2,1)S(1)}, u32[]{:S(2)}, u32[]{:S(2)}) collective-permute-start(bf16[128,512]{1,0:T(8,128)(2,1)S(1)} %get-tuple-element.54), channel_id=1, source_target_pairs={{0,7},{1,6},{2,5},{3,4},{4,3},{5,2},{6,1},{7,0},{8,15},{9,14},{10,... | collective-permute-start | bytes 393224 | tf_op jit(solution)/shard_map/ppermute | solution.py:391
  79.7 1.6 %shard_map.159 = (bf16[128,512]{1,0:T(8,128)(2,1)S(1)}, bf16[128,512]{1,0:T(8,128)(2,1)S(1)}) custom-call(bf16[128,512]{1,0:T(8,128)(2,1)S(1)} %collective-permute-done.14.refs_0_, bf16[128,512]{1,0:T(8,128)(2,1)S(1)} %collective-permute-done.15.refs_1_, bf16[512,512]{1,0:T(8,128)(2,1)S(1)} %bitcast.19, bf16[512,512]{1,0:T(8,128)(2,1)S(1)} %collective-permute-done.3.refs_3_, ...), custom_call_target="tpu_custom_call" | custom-call | flops 1073741824 | bytes 4718592 | tf_op jit(solution)/shard_map/pallas_call | solution.py:375
  81.3 0.6 collective-permute-start.16
  81.9 4.5 %collective-permute-start.17 = (bf16[128,512]{1,0:T(8,128)(2,1)S(1)}, bf16[128,512]{1,0:T(8,128)(2,1)S(1)}, u32[]{:S(2)}, u32[]{:S(2)}) collective-permute-start(bf16[128,512]{1,0:T(8,128)(2,1)S(1)} %get-tuple-element.50), channel_id=1, source_target_pairs={{0,5},{1,4},{2,7},{3,6},{4,1},{5,0},{6,3},{7,2},{8,13},{9,12},{10,... | collective-permute-start | bytes 393224 | tf_op jit(solution)/shard_map/ppermute | solution.py:391
  86.4 1.6 %shard_map.158 = (bf16[128,512]{1,0:T(8,128)(2,1)S(1)}, bf16[128,512]{1,0:T(8,128)(2,1)S(1)}) custom-call(bf16[128,512]{1,0:T(8,128)(2,1)S(1)} %collective-permute-done.10.refs_0_, bf16[128,512]{1,0:T(8,128)(2,1)S(1)} %collective-permute-done.11.refs_1_, bf16[512,512]{1,0:T(8,128)(2,1)S(1)} %bitcast.20, bf16[512,512]{1,0:T(8,128)(2,1)S(1)} %collective-permute-done.3.refs_3_, ...), custom_call_target="tpu_custom_call" | custom-call | flops 1073741824 | bytes 4718592 | tf_op jit(solution)/shard_map/pallas_call | solution.py:375
  88.1 1.6 %shard_map.157 = (bf16[128,512]{1,0:T(8,128)(2,1)S(1)}, bf16[128,512]{1,0:T(8,128)(2,1)S(1)}) custom-call(bf16[128,512]{1,0:T(8,128)(2,1)S(1)} %get-tuple-element.39.refs_0_, bf16[128,512]{1,0:T(8,128)(2,1)S(1)} %collective-permute-done.2.refs_1_, bf16[512,512]{1,0:T(8,128)(2,1)S(1)} %bitcast.21, bf16[512,512]{1,0:T(8,128)(2,1)S(1)} %collective-permute-done.3.refs_3_, ...), custom_call_target="tpu_custom_call" | custom-call | flops 1073741824 | bytes 4718592 | tf_op jit(solution)/shard_map/pallas_call | solution.py:375
  89.7 3.3 %collective-permute-start.13 = (bf16[128,512]{1,0:T(8,128)(2,1)S(1)}, bf16[128,512]{1,0:T(8,128)(2,1)S(1)}, u32[]{:S(2)}, u32[]{:S(2)}) collective-permute-start(bf16[128,512]{1,0:T(8,128)(2,1)S(1)} %get-tuple-element.46), channel_id=1, source_target_pairs={{0,3},{1,2},{2,1},{3,0},{4,7},{5,6},{6,5},{7,4},{8,11},{9,10},{10,... | collective-permute-start | bytes 393224 | tf_op jit(solution)/shard_map/ppermute | solution.py:391
  93.0 4.0 %collective-permute-done.16.rest_4_ = bf16[128,512]{1,0:T(8,128)(2,1)S(1)} collective-permute-done((bf16[128,512]{1,0:T(8,128)(2,1)S(1)}, bf16[128,512]{1,0:T(8,128)(2,1)S(1)}, u32[]{:S(2)}, u32[]{:S(2)}) %collective-permute-start.16) | collective-permute-done | bytes 131104 | tf_op jit(solution)/shard_map/ppermute | solution.py:391
  96.9 3.1 %collective-permute-done.17.rest_5_ = bf16[128,512]{1,0:T(8,128)(2,1)S(1)} collective-permute-done((bf16[128,512]{1,0:T(8,128)(2,1)S(1)}, bf16[128,512]{1,0:T(8,128)(2,1)S(1)}, u32[]{:S(2)}, u32[]{:S(2)}) %collective-permute-start.17) | collective-permute-done | bytes 131104 | tf_op jit(solution)/shard_map/ppermute | solution.py:391
  100.1 0.9 collective-permute-done.13.rest_3_
  101.0 1.8 %shard_map.161 = bf16[512,512]{1,0:T(8,128)(2,1)} custom-call(bf16[512,512]{1,0:T(8,128)(2,1)S(1)} %get-tuple-element.37.third_ref, s32[512,128]{1,0:T(8,128)S(1)} %get-tuple-element.38.slot_col_ref, f32[1,512]{1,0:T(1,128)S(1)} %bitcast.29, bf16[128,512]{1,0:T(8,128)(2,1)S(1)} %get-tuple-element.41.rest_0_, ...), custom_call_target="tpu_custom_call" | custom-call | flops 536870912 | bytes 2361344 | tf_op jit(solution)/shard_map/pallas_call | solution.py:375
  (48 shorter events, 0.4 us)
Async XLA Ops:
  0.0 27.1 %collective-permute-start.3 = (bf16[512,512]{1,0:T(8,128)(2,1)}, bf16[512,512]{1,0:T(8,128)(2,1)S(1)}, u32[]{:S(2)}, u32[]{:S(2)}) collective-permute-start(bf16[512,512]{1,0:T(8,128)(2,1)} %bitcast.16), channel_id=1, source_target_pairs={{0,8},{8,0},{16,24},{24,16},{1,9},{9,1},{17,25},{25,17},{2,10},{10... | collective-permute-start | bytes 1572872 | tf_op jit(solution)/shard_map/ppermute | solution.py:391
  2.0 25.5 %collective-permute-start.7 = (bf16[512,512]{1,0:T(8,128)(2,1)}, bf16[512,512]{1,0:T(8,128)(2,1)S(1)}, u32[]{:S(2)}, u32[]{:S(2)}) collective-permute-start(bf16[512,512]{1,0:T(8,128)(2,1)} %bitcast.22), channel_id=1, source_target_pairs={{0,16},{8,24},{16,0},{24,8},{1,17},{9,25},{17,1},{25,9},{2,18},{10... | collective-permute-start | bytes 1572872 | tf_op jit(solution)/shard_map/ppermute | solution.py:391
  4.0 1.6 %copy-start.10 = (bf16[512,2048]{1,0:T(8,128)(2,1)S(1)}, bf16[512,2048]{1,0:T(8,128)(2,1)}, u32[]{:S(2)}) copy-start(bf16[512,2048]{1,0:T(8,128)(2,1)} %up_ref.1) | copy-start | bytes 6291460
  5.6 1.6 %copy-start.11 = (bf16[2048,512]{1,0:T(8,128)(2,1)S(1)}, bf16[2048,512]{1,0:T(8,128)(2,1)}, u32[]{:S(2)}) copy-start(bf16[2048,512]{1,0:T(8,128)(2,1)} %down_ref.1) | copy-start | bytes 6291460
  7.2 1.4 %copy-start.12 = (bf16[512,1536]{1,0:T(8,128)(2,1)S(1)}, bf16[512,1536]{1,0:T(8,128)(2,1)}, u32[]{:S(2)}) copy-start(bf16[512,1536]{1,0:T(8,128)(2,1)} %wqkv_ref.3) | copy-start | bytes 4718596
  8.6 1.0 %copy-start.13 = (bf16[1,32,16,512]{3,2,1,0:T(8,128)(2,1)S(1)}, bf16[1,32,16,512]{3,2,1,0:T(8,128)(2,1)}, u32[]{:S(2)}) copy-start(bf16[1,32,16,512]{3,2,1,0:T(8,128)(2,1)} %param.16) | copy-start | bytes 1572868
  9.7 1.0 %copy-start.14 = (bf16[512,512]{1,0:T(8,128)(2,1)S(1)}, bf16[512,512]{1,0:T(8,128)(2,1)}, u32[]{:S(2)}) copy-start(bf16[512,512]{1,0:T(8,128)(2,1)} %wproj_ref.2) | copy-start | bytes 1572868
  10.7 0.7 copy-start.15
  11.4 0.7 copy-start.16
  12.1 10.3 %copy-start = (bf16[1,512,512]{2,1,0:T(8,128)(2,1)S(1)}, bf16[1,512,512]{2,1,0:T(8,128)(2,1)}, u32[]{:S(2)}) copy-start(bf16[1,512,512]{2,1,0:T(8,128)(2,1)} %param.29) | copy-start | bytes 1572868
  12.1 10.3 %copy-start.1 = (bf16[1,512,512]{2,1,0:T(8,128)(2,1)S(1)}, bf16[1,512,512]{2,1,0:T(8,128)(2,1)}, u32[]{:S(2)}) copy-start(bf16[1,512,512]{2,1,0:T(8,128)(2,1)} %param.30) | copy-start | bytes 1572868
  12.1 12.7 %copy-start.17 = (s32[1,1,32,16,1]{2,4,3,1,0:T(1,128)S(1)}, s32[1,1,32,16,1]{2,4,3,1,0:T(1,128)}, u32[]{:S(2)}) copy-start(s32[1,1,32,16,1]{2,4,3,1,0:T(1,128)} %param.17) | copy-start | bytes 6148
  21.3 0.8 copy-start.5
  22.1 18.0 %copy-start.8 = (f32[512]{0:T(512)S(1)}, f32[512]{0:T(512)}, u32[]{:S(2)}) copy-start(f32[512]{0:T(512)} %param.28) | copy-start | bytes 6148
  22.1 5.0 %collective-permute-start = (bf16[128,512]{1,0:T(8,128)(2,1)}, bf16[128,512]{1,0:T(8,128)(2,1)S(1)}, u32[]{:S(2)}, u32[]{:S(2)}) collective-permute-start(bf16[128,512]{1,0:T(8,128)(2,1)} %get-tuple-element.32), channel_id=1, source_target_pairs={{0,8},{8,16},{16,24},{24,0},{1,9},{9,17},{17,25},{25,1},{2,10},{10... | collective-permute-start | bytes 393224 | tf_op jit(solution)/shard_map/ppermute | solution.py:465
  22.3 43.2 %collective-permute-start.4 = (bf16[512,512]{1,0:T(8,128)(2,1)S(1)}, bf16[512,512]{1,0:T(8,128)(2,1)S(1)}, u32[]{:S(2)}, u32[]{:S(2)}) collective-permute-start(bf16[512,512]{1,0:T(8,128)(2,1)S(1)} %bitcast.17), channel_id=1, source_target_pairs={{0,16},{8,24},{16,0},{24,8},{1,17},{9,25},{17,1},{25,9},{2,18},{10... | collective-permute-start | bytes 1572872 | tf_op jit(solution)/shard_map/ppermute | solution.py:391
  22.4 44.9 %collective-permute-start.6 = (bf16[512,512]{1,0:T(8,128)(2,1)S(1)}, bf16[512,512]{1,0:T(8,128)(2,1)S(1)}, u32[]{:S(2)}, u32[]{:S(2)}) collective-permute-start(bf16[512,512]{1,0:T(8,128)(2,1)S(1)} %bitcast.23), channel_id=1, source_target_pairs={{0,8},{8,0},{16,24},{24,16},{1,9},{9,1},{17,25},{25,17},{2,10},{10... | collective-permute-start | bytes 1572872 | tf_op jit(solution)/shard_map/ppermute | solution.py:391
  27.1 13.0 %collective-permute-start.1 = (bf16[128,512]{1,0:T(8,128)(2,1)S(1)}, bf16[128,512]{1,0:T(8,128)(2,1)S(1)}, u32[]{:S(2)}, u32[]{:S(2)}) collective-permute-start(bf16[128,512]{1,0:T(8,128)(2,1)S(1)} %get-tuple-element.33), channel_id=1, source_target_pairs={{0,24},{8,0},{16,8},{24,16},{1,25},{9,1},{17,9},{25,17},{2,26},{10... | collective-permute-start | bytes 393224 | tf_op jit(solution)/shard_map/ppermute | solution.py:464
  27.1 40.8 %collective-permute-start.5 = (bf16[512,512]{1,0:T(8,128)(2,1)S(1)}, bf16[512,512]{1,0:T(8,128)(2,1)S(1)}, u32[]{:S(2)}, u32[]{:S(2)}) collective-permute-start(bf16[512,512]{1,0:T(8,128)(2,1)S(1)} %collective-permute-done.3.refs_3_), channel_id=1, source_target_pairs={{0,16},{8,24},{16,0},{24,8},{1,17},{9,25},{17,1},{25,9},{2,18},{10... | collective-permute-start | bytes 1572872 | tf_op jit(solution)/shard_map/ppermute | solution.py:391
  27.6 41.1 %collective-permute-start.8 = (bf16[512,512]{1,0:T(8,128)(2,1)S(1)}, bf16[512,512]{1,0:T(8,128)(2,1)S(1)}, u32[]{:S(2)}, u32[]{:S(2)}) collective-permute-start(bf16[512,512]{1,0:T(8,128)(2,1)S(1)} %collective-permute-done.7.refs_8_), channel_id=1, source_target_pairs={{0,8},{8,0},{16,24},{24,16},{1,9},{9,1},{17,25},{25,17},{2,10},{10... | collective-permute-start | bytes 1572872 | tf_op jit(solution)/shard_map/ppermute | solution.py:391
  28.9 1.4 %copy-start.2 = (bf16[512,1536]{1,0:T(8,128)(2,1)S(1)}, bf16[512,1536]{1,0:T(8,128)(2,1)}, u32[]{:S(2)}) copy-start(bf16[512,1536]{1,0:T(8,128)(2,1)} %wqkv_ref.5) | copy-start | bytes 4718596
  30.3 1.0 %copy-start.6 = (bf16[512,512]{1,0:T(8,128)(2,1)S(1)}, bf16[512,512]{1,0:T(8,128)(2,1)}, u32[]{:S(2)}) copy-start(bf16[512,512]{1,0:T(8,128)(2,1)} %copy-done.5) | copy-start | bytes 1572868
  31.4 8.8 %copy-start.3 = (bf16[512,1536]{1,0:T(8,128)(2,1)S(1)}, bf16[512,1536]{1,0:T(8,128)(2,1)}, u32[]{:S(2)}) copy-start(bf16[512,1536]{1,0:T(8,128)(2,1)} %wqkv_ref.5) | copy-start | bytes 4718596
  31.4 8.8 %copy-start.4 = (bf16[512,512]{1,0:T(8,128)(2,1)S(1)}, bf16[512,512]{1,0:T(8,128)(2,1)}, u32[]{:S(2)}) copy-start(bf16[512,512]{1,0:T(8,128)(2,1)} %wproj_ref.3) | copy-start | bytes 1572868
  31.4 8.8 %copy-start.7 = (bf16[512,512]{1,0:T(8,128)(2,1)S(1)}, bf16[512,512]{1,0:T(8,128)(2,1)}, u32[]{:S(2)}) copy-start(bf16[512,512]{1,0:T(8,128)(2,1)} %copy-done.5) | copy-start | bytes 1572868
  46.5 5.9 %collective-permute-start.18 = (bf16[128,512]{1,0:T(8,128)(2,1)S(1)}, bf16[128,512]{1,0:T(8,128)(2,1)S(1)}, u32[]{:S(2)}, u32[]{:S(2)}) collective-permute-start(bf16[128,512]{1,0:T(8,128)(2,1)S(1)} %get-tuple-element.51), channel_id=1, source_target_pairs={{0,6},{1,7},{2,4},{3,5},{4,2},{5,3},{6,0},{7,1},{8,14},{9,15},{10,... | collective-permute-start | bytes 393224 | tf_op jit(solution)/shard_map/ppermute | solution.py:391
  52.4 11.9 %collective-permute-start.19 = (bf16[128,512]{1,0:T(8,128)(2,1)S(1)}, bf16[128,512]{1,0:T(8,128)(2,1)S(1)}, u32[]{:S(2)}, u32[]{:S(2)}) collective-permute-start(bf16[128,512]{1,0:T(8,128)(2,1)S(1)} %get-tuple-element.52), channel_id=1, source_target_pairs={{0,7},{1,6},{2,5},{3,4},{4,3},{5,2},{6,1},{7,0},{8,15},{9,14},{10,... | collective-permute-start | bytes 393224 | tf_op jit(solution)/shard_map/ppermute | solution.py:391
  64.3 9.7 %collective-permute-start.14 = (bf16[128,512]{1,0:T(8,128)(2,1)S(1)}, bf16[128,512]{1,0:T(8,128)(2,1)S(1)}, u32[]{:S(2)}, u32[]{:S(2)}) collective-permute-start(bf16[128,512]{1,0:T(8,128)(2,1)S(1)} %get-tuple-element.47), channel_id=1, source_target_pairs={{0,4},{1,5},{2,6},{3,7},{4,0},{5,1},{6,2},{7,3},{8,12},{9,13},{10,... | collective-permute-start | bytes 393224 | tf_op jit(solution)/shard_map/ppermute | solution.py:391
  65.6 12.8 %collective-permute-start.15 = (bf16[128,512]{1,0:T(8,128)(2,1)S(1)}, bf16[128,512]{1,0:T(8,128)(2,1)S(1)}, u32[]{:S(2)}, u32[]{:S(2)}) collective-permute-start(bf16[128,512]{1,0:T(8,128)(2,1)S(1)} %get-tuple-element.48), channel_id=1, source_target_pairs={{0,5},{1,4},{2,7},{3,6},{4,1},{5,0},{6,3},{7,2},{8,13},{9,12},{10,... | collective-permute-start | bytes 393224 | tf_op jit(solution)/shard_map/ppermute | solution.py:391
  67.3 14.1 %collective-permute-start.10 = (bf16[128,512]{1,0:T(8,128)(2,1)S(1)}, bf16[128,512]{1,0:T(8,128)(2,1)S(1)}, u32[]{:S(2)}, u32[]{:S(2)}) collective-permute-start(bf16[128,512]{1,0:T(8,128)(2,1)S(1)} %get-tuple-element.43), channel_id=1, source_target_pairs={{0,2},{1,3},{2,0},{3,1},{4,6},{5,7},{6,4},{7,5},{8,10},{9,11},{10,... | collective-permute-start | bytes 393224 | tf_op jit(solution)/shard_map/ppermute | solution.py:391
  67.9 14.0 %collective-permute-start.11 = (bf16[128,512]{1,0:T(8,128)(2,1)S(1)}, bf16[128,512]{1,0:T(8,128)(2,1)S(1)}, u32[]{:S(2)}, u32[]{:S(2)}) collective-permute-start(bf16[128,512]{1,0:T(8,128)(2,1)S(1)} %get-tuple-element.44), channel_id=1, source_target_pairs={{0,3},{1,2},{2,1},{3,0},{4,7},{5,6},{6,5},{7,4},{8,11},{9,10},{10,... | collective-permute-start | bytes 393224 | tf_op jit(solution)/shard_map/ppermute | solution.py:391
  68.7 19.3 %collective-permute-start.2 = (bf16[128,512]{1,0:T(8,128)(2,1)S(1)}, bf16[128,512]{1,0:T(8,128)(2,1)S(1)}, u32[]{:S(2)}, u32[]{:S(2)}) collective-permute-start(bf16[128,512]{1,0:T(8,128)(2,1)S(1)} %get-tuple-element.40), channel_id=1, source_target_pairs={{0,1},{1,0},{2,3},{3,2},{4,5},{5,4},{6,7},{7,6},{8,9},{9,8},{10,11... | collective-permute-start | bytes 393224 | tf_op jit(solution)/shard_map/ppermute | solution.py:391
  74.0 15.6 %collective-permute-start.20 = (bf16[128,512]{1,0:T(8,128)(2,1)S(1)}, bf16[128,512]{1,0:T(8,128)(2,1)S(1)}, u32[]{:S(2)}, u32[]{:S(2)}) collective-permute-start(bf16[128,512]{1,0:T(8,128)(2,1)S(1)} %get-tuple-element.53), channel_id=1, source_target_pairs={{0,6},{1,7},{2,4},{3,5},{4,2},{5,3},{6,0},{7,1},{8,14},{9,15},{10,... | collective-permute-start | bytes 393224 | tf_op jit(solution)/shard_map/ppermute | solution.py:391
  78.4 14.6 %collective-permute-start.21 = (bf16[128,512]{1,0:T(8,128)(2,1)S(1)}, bf16[128,512]{1,0:T(8,128)(2,1)S(1)}, u32[]{:S(2)}, u32[]{:S(2)}) collective-permute-start(bf16[128,512]{1,0:T(8,128)(2,1)S(1)} %get-tuple-element.54), channel_id=1, source_target_pairs={{0,7},{1,6},{2,5},{3,4},{4,3},{5,2},{6,1},{7,0},{8,15},{9,14},{10,... | collective-permute-start | bytes 393224 | tf_op jit(solution)/shard_map/ppermute | solution.py:391
  81.3 15.6 %collective-permute-start.16 = (bf16[128,512]{1,0:T(8,128)(2,1)S(1)}, bf16[128,512]{1,0:T(8,128)(2,1)S(1)}, u32[]{:S(2)}, u32[]{:S(2)}) collective-permute-start(bf16[128,512]{1,0:T(8,128)(2,1)S(1)} %get-tuple-element.49), channel_id=1, source_target_pairs={{0,4},{1,5},{2,6},{3,7},{4,0},{5,1},{6,2},{7,3},{8,12},{9,13},{10,... | collective-permute-start | bytes 393224 | tf_op jit(solution)/shard_map/ppermute | solution.py:391
  81.9 18.2 %collective-permute-start.17 = (bf16[128,512]{1,0:T(8,128)(2,1)S(1)}, bf16[128,512]{1,0:T(8,128)(2,1)S(1)}, u32[]{:S(2)}, u32[]{:S(2)}) collective-permute-start(bf16[128,512]{1,0:T(8,128)(2,1)S(1)} %get-tuple-element.50), channel_id=1, source_target_pairs={{0,5},{1,4},{2,7},{3,6},{4,1},{5,0},{6,3},{7,2},{8,13},{9,12},{10,... | collective-permute-start | bytes 393224 | tf_op jit(solution)/shard_map/ppermute | solution.py:391
  88.0 12.1 %collective-permute-start.12 = (bf16[128,512]{1,0:T(8,128)(2,1)S(1)}, bf16[128,512]{1,0:T(8,128)(2,1)S(1)}, u32[]{:S(2)}, u32[]{:S(2)}) collective-permute-start(bf16[128,512]{1,0:T(8,128)(2,1)S(1)} %get-tuple-element.45), channel_id=1, source_target_pairs={{0,2},{1,3},{2,0},{3,1},{4,6},{5,7},{6,4},{7,5},{8,10},{9,11},{10,... | collective-permute-start | bytes 393224 | tf_op jit(solution)/shard_map/ppermute | solution.py:391
  88.1 12.9 %copy-start.9 = (f32[512]{0:T(512)S(1)}, f32[512]{0:T(512)}, u32[]{:S(2)}) copy-start(f32[512]{0:T(512)} %param.31) | copy-start | bytes 6148
  89.7 11.3 %collective-permute-start.13 = (bf16[128,512]{1,0:T(8,128)(2,1)S(1)}, bf16[128,512]{1,0:T(8,128)(2,1)S(1)}, u32[]{:S(2)}, u32[]{:S(2)}) collective-permute-start(bf16[128,512]{1,0:T(8,128)(2,1)S(1)} %get-tuple-element.46), channel_id=1, source_target_pairs={{0,3},{1,2},{2,1},{3,0},{4,7},{5,6},{6,5},{7,4},{8,11},{9,10},{10,... | collective-permute-start | bytes 393224 | tf_op jit(solution)/shard_map/ppermute | solution.py:391
  93.0 8.1 %collective-permute-start.9 = (bf16[128,512]{1,0:T(8,128)(2,1)S(1)}, bf16[128,512]{1,0:T(8,128)(2,1)S(1)}, u32[]{:S(2)}, u32[]{:S(2)}) collective-permute-start(bf16[128,512]{1,0:T(8,128)(2,1)S(1)} %get-tuple-element.42), channel_id=1, source_target_pairs={{0,1},{1,0},{2,3},{3,2},{4,5},{5,4},{6,7},{7,6},{8,9},{9,8},{10,11... | collective-permute-start | bytes 393224 | tf_op jit(solution)/shard_map/ppermute | solution.py:391
where the time goes:
time: 103 us
  starting transfers between devices  33.6 us (33%)
  waiting for transfers between devices  29.3 us (28%)
  Pallas kernels  27.3 us (27%)
  local copies, waits for them, and re-layouts  11.5 us (11%)
    ppermute x20, starting transfers between devices, swap(): lax.ppermute(block, axis, [(i, i ^ bits) for i in range(lax.axis_size(axi...  33.4 us
    pallas_call x8, Pallas kernels, call(): pl.pallas_call(kernel, out_shape=outs, in_specs=[smem] * scalars + [vmem]...  27.3 us
    ppermute x20, waiting for transfers between devices, swap(): lax.ppermute(block, axis, [(i, i ^ bits) for i in range(lax.axis_size(axi...  22.1 us
    unnamed x37, local copies, waits for them, and re-layouts  11.4 us
    ppermute x1, waiting for transfers between devices, local(): lax.ppermute(to_left, 'band', [(i, (i - 1) % band_count) for i in ring])  5.14 us
    ppermute x1, waiting for transfers between devices, local(): lax.ppermute(to_right, 'band', [(i, (i + 1) % band_count) for i in ring])  2.06 us
  transfers between devices with their start and end apart: 22, of which 9 were waited for; matrix products, arithmetic and copies ran while one was open for 1% of the time, Pallas kernels for 25%

commit v1 on v0

--- a/solution.py
+++ b/solution.py
@@ -55,11 +55,15 @@
     return jnp.where(idx < LANES, from_low, from_high)
 
 
+def head_rows(table_ref, tab_ref):
+    tab_ref[:, : table_ref.shape[1]] = table_ref[...] * LOG2E
+
+
 def offset_index(row_p, col_p, row_q, col_q):
     return (row_p - row_q + WIN - 1) * SPAN + (col_p - col_q + WIN - 1)
 
 
-def own_bias(tab_ref, first_head, bias_ref, band_width, shift):
+def own_bias(tab_ref, bias_ref, band_width, shift):
     strip = WIN * band_width
     p, q = iota((strip, strip), 0), iota((strip, strip), 1)
     row_p, col_p = lax.div(p, band_width), lax.rem(p, band_width) + shift
@@ -67,7 +71,7 @@
     idx = offset_index(row_p, lax.rem(col_p, WIN), row_q, lax.rem(col_q, WIN))
     same = lax.div(col_p, WIN) == lax.div(col_q, WIN)
     for h in range(HEADS):
-        row = tab_ref[first_head + h : first_head + h + 1, :]
+        row = tab_ref[h : h + 1, :]
         tile, part = divmod(h, 4)
         bias_ref[tile, :, part * strip : (part + 1) * strip] = jnp.where(
             same, pick(row, idx), CLOSED
@@ -86,14 +90,14 @@
     return row_p, col_p, row_q, col_q, right, q < halo
 
 
-def halo_bias(tab_ref, first_head, bias_ref, band_width, at_first, at_last):
+def halo_bias(tab_ref, bias_ref, band_width, at_first, at_last):
     row_p, col_p, row_q, col_q, right, front = halo_places(band_width)
     idx = offset_index(row_p, lax.rem(col_p, WIN), row_q, lax.rem(col_q, WIN))
     same = lax.div(col_p, WIN) == lax.div(col_q, WIN)
     edge = jnp.where(right, at_last, at_first) > 0
     wide = front.shape[1]
     for pair in range(HEADS // 2):
-        h = first_head + 2 * pair
+        h = 2 * pair
         value = jnp.where(
             front, pick(tab_ref[h : h + 1, :], idx), pick(tab_ref[h + 1 : h + 2, :], idx)
         )
@@ -118,28 +122,65 @@
     return jnp.concatenate([block * mask for mask in masks], axis=0)
 
 
+def fetch(sems, *pairs):
+    copies = [pltpu.make_async_copy(a, b, sems.at[i]) for i, (a, b) in enumerate(pairs)]
+    for copy in copies:
+        copy.start()
+    return copies
+
+
 def front_kernel(
     band_width,
+    table_hbm,
+    x_hbm,
+    wqkv_hbm,
+    wproj_hbm,
+    gain_hbm,
+    up_hbm,
+    down_hbm,
+    gain_mlp_hbm,
+    out_ref,
+    left_ref,
+    right_ref,
     x_ref,
     wqkv_ref,
     wproj_ref,
-    tab_ref,
     gain_ref,
     up_ref,
     down_ref,
     gain_mlp_ref,
-    out_ref,
-    left_ref,
-    right_ref,
+    table_ref,
+    sems,
+    tab_ref,
     qkv,
     bias,
     heads,
+    act,
     second,
 ):
     rows, width = x_ref.shape
     strip = WIN * band_width
     head_dim = width // HEADS
     parts = LANES // head_dim
+    copies = fetch(
+        sems,
+        (table_hbm, table_ref),
+        (x_hbm, x_ref),
+        (wqkv_hbm, wqkv_ref),
+    )
+    copies[0].wait()
+    head_rows(table_ref, tab_ref)
+    own_bias(tab_ref, bias, band_width, 0)
+    copies[1].wait()
+    copies[2].wait()
+    copies = fetch(
+        sems.at[3:],
+        (wproj_hbm, wproj_ref),
+        (gain_hbm, gain_ref),
+        (up_hbm, up_ref),
+        (down_hbm, down_ref),
+        (gain_mlp_hbm, gain_mlp_ref),
+    )
     x = x_ref[...]
     for part in range(3):
         cols = slice(part * width, (part + 1) * width)
@@ -147,7 +188,6 @@
         if part == 0:
             product = product * (LOG2E * head_dim**-0.5)
         qkv[:, cols] = product.astype(BF)
-    own_bias(tab_ref, 0, bias, band_width, 0)
     masks = head_masks(parts)
     ones = sum_columns(strip, parts)
 
@@ -170,19 +210,13 @@
         return carry
 
     lax.fori_loop(0, width // LANES, tile_step, 0)
-
-    half = rows // 2
-    hidden = up_ref.shape[1]
-    for r in range(2):
-        tokens = slice(r * half, (r + 1) * half)
-        projected = dot(heads[tokens, :], wproj_ref[...])
-        first = (x_ref[tokens, :].astype(F32) + layer_norm(projected, gain_ref[...])).astype(BF)
-        total = jnp.zeros((half, width), F32)
-        for f in range(hidden // width):
-            cols = slice(f * width, (f + 1) * width)
-            act = gelu(dot(first, up_ref[:, cols])).astype(BF)
-            total = total + dot(act, down_ref[cols, :])
-        second[tokens, :] = (first.astype(F32) + layer_norm(total, gain_mlp_ref[...])).astype(BF)
+    for copy in copies:
+        copy.wait()
+    projected = dot(heads[...], wproj_ref[...])
+    first = (x_ref[...].astype(F32) + layer_norm(projected, gain_ref[...])).astype(BF)
+    act[...] = gelu(dot(first, up_ref[...])).astype(BF)
+    dense = layer_norm(dot(act[...], down_ref[...]), gain_mlp_ref[...])
+    second[...] = (first.astype(F32) + dense).astype(BF)
     turn = HALF * band_width
     rolled = jnp.concatenate([second[turn:, :], second[:turn, :]], axis=0)
     out_ref[...] = rolled
@@ -200,26 +234,40 @@
     capacity,
     info_ref,
     x_ref,
-    wqkv_ref,
-    tab_ref,
     routes_ref,
+    table_hbm,
+    wqkv_hbm,
+    in_hbm,
+    in_next,
+    out_hbm,
+    out_next,
     qkv_ref,
     bias_ref,
     bias_halo_ref,
     slot_row_ref,
     slot_col_ref,
+    wqkv_ref,
+    in_pair,
+    out_pair,
+    table_ref,
+    sems,
+    tab_ref,
 ):
     rows, width = x_ref.shape
     head_dim = width // HEADS
-    x = x_ref[...]
-    for part in range(3):
-        cols = slice(part * width, (part + 1) * width)
-        product = dot(x, wqkv_ref[:, cols])
-        if part == 0:
-            product = product * (LOG2E * head_dim**-0.5)
-        qkv_ref[:, cols] = product.astype(BF)
-    own_bias(tab_ref, HEADS, bias_ref, band_width, HALF)
-    halo_bias(tab_ref, HEADS, bias_halo_ref, band_width, info_ref[0], info_ref[1])
+    copies = fetch(
+        sems,
+        (table_hbm, table_ref),
+        (wqkv_hbm, wqkv_ref),
+        (in_hbm, in_pair.at[0]),
+        (in_next, in_pair.at[1]),
+        (out_hbm, out_pair.at[0]),
+        (out_next, out_pair.at[1]),
+    )
+    copies[0].wait()
+    head_rows(table_ref, tab_ref)
+    own_bias(tab_ref, bias_ref, band_width, HALF)
+    halo_bias(tab_ref, bias_halo_ref, band_width, info_ref[0], info_ref[1])
     routes = routes_ref[...]
     named = jnp.where(iota((experts, rows), 0) == routes, 1.0, 0.0)
     a, b = iota((rows, rows), 0), iota((rows, rows), 1)
@@ -235,6 +283,16 @@
     base_col = iota((rows, experts), 1).astype(F32) * capacity - 1.0
     slot_col = jnp.sum(named_col * (count_col + base_col), axis=1, keepdims=True)
     slot_col_ref[...] = jnp.broadcast_to(slot_col, slot_col_ref.shape).astype(I32)
+    copies[1].wait()
+    x = x_ref[...]
+    for part in range(3):
+        cols = slice(part * width, (part + 1) * width)
+        product = dot(x, wqkv_ref[:, cols])
+        if part == 0:
+            product = product * (LOG2E * head_dim**-0.5)
+        qkv_ref[:, cols] = product.astype(BF)
+    for copy in copies[2:]:
+        copy.wait()
 
 
 def shifted_kernel(
@@ -248,12 +306,13 @@
     wqkv_ref,
     bias_ref,
     bias_halo_ref,
-    wproj_ref,
-    gain_ref,
     slot_row_ref,
+    wproj_hbm,
+    gain_hbm,
     *rest,
 ):
-    third_ref, *out_refs, halo_kv, heads = rest
+    third_ref, *out_refs, halo_kv, heads, wproj_ref, gain_ref, sems = rest
+    copies = fetch(sems, (wproj_hbm, wproj_ref), (gain_hbm, gain_ref))
     rows, width = x_ref.shape
     strip = WIN * band_width
     side = WIN * HALF
@@ -327,6 +386,8 @@
         return carry
 
     lax.fori_loop(0, width // LANES, tile_step, 0)
+    for copy in copies:
+        copy.wait()
     projected = dot(heads[...], wproj_ref[...])
     third = (x_ref[...].astype(F32) + layer_norm(projected, gain_ref[...])).astype(BF)
     third_ref[...] = third
@@ -336,10 +397,14 @@
         ref[...] = dot(jnp.where(places == slot, 1.0, 0.0).astype(BF), third).astype(BF)
 
 
-def expert_kernel(amount, quarters, *refs):
-    x_refs, rest = refs[:amount], refs[amount:]
-    in_refs, rest = rest[:quarters], rest[quarters:]
-    out_w_refs, out_refs = rest[:quarters], rest[quarters:]
+def expert_kernel(amount, *refs):
+    x_refs, (in_own, in_far, out_own, out_far), out_refs = (
+        refs[:amount],
+        refs[amount : amount + 4],
+        refs[amount + 4 :],
+    )
+    in_refs = (in_own.at[0], in_own.at[1], in_far.at[0], in_far.at[1])
+    out_w_refs = (out_own.at[0], out_far.at[0], out_own.at[1], out_far.at[1])
     x = jnp.concatenate([ref[...] for ref in x_refs], axis=0)
     total = jnp.zeros(x.shape, F32)
     for w_in, w_out in zip(in_refs, out_w_refs):
@@ -349,8 +414,9 @@
         ref[...] = total[k * each : (k + 1) * each, :].astype(BF)
 
 
-def final_kernel(band_width, capacity, third_ref, slot_col_ref, gain_ref, *rest):
-    *result_refs, out_ref = rest
+def final_kernel(band_width, capacity, third_ref, slot_col_ref, gain_hbm, *rest):
+    *result_refs, out_ref, gain_ref, sems = rest
+    copies = fetch(sems, (gain_hbm, gain_ref))
     rows, width = third_ref.shape
     results = jnp.concatenate([ref[...] for ref in result_refs], axis=0)
     slot = slot_col_ref[...]
@@ -362,25 +428,27 @@
         axis=1,
     )
     picked = dot(chosen, results)
+    copies[0].wait()
     encoded = (third_ref[...].astype(F32) + layer_norm(picked, gain_ref[...])).astype(BF)
     turn = HALF * band_width
     out_ref[turn:, :] = encoded[: rows - turn, :]
     out_ref[:turn, :] = encoded[rows - turn :, :]
 
 
-def call(kernel, outs, ins, scratch=(), scalars=0, limit=32, flops=0):
-    vmem = pl.BlockSpec(memory_space=pltpu.VMEM)
-    smem = pl.BlockSpec(memory_space=pltpu.SMEM)
-    size = sum(math.prod(a.shape) * a.dtype.itemsize for a in list(ins) + list(outs))
-    return pl.pallas_call(
+def call(kernel, outs, ins, places, scratch=(), limit=32, flops=0, size=None):
+    spaces = {"s": pltpu.SMEM, "v": pltpu.VMEM, "h": pltpu.HBM, "a": pl.ANY}
+    if size is None:
+        size = sum(math.prod(a.shape) * a.dtype.itemsize for a in list(ins) + list(outs))
+    results = pl.pallas_call(
         kernel,
         out_shape=outs,
-        in_specs=[smem] * scalars + [vmem] * (len(ins) - scalars),
-        out_specs=[vmem] * len(outs),
+        in_specs=[pl.BlockSpec(memory_space=spaces[p]) for p in places],
+        out_specs=[pl.BlockSpec(memory_space=pltpu.VMEM)] * len(outs),
         scratch_shapes=list(scratch),
         compiler_params=pltpu.CompilerParams(vmem_limit_bytes=limit << 20),
         cost_estimate=pl.CostEstimate(flops=flops, bytes_accessed=size, transcendentals=0),
     )(*ins)
+    return list(results)
 
 
 def shape_of(*dims, dtype=BF):
@@ -389,13 +457,6 @@
 
 def swap(block, axis, bits):
     return lax.ppermute(block, axis, [(i, i ^ bits) for i in range(lax.axis_size(axis))])
-
-
-def gather_blocks(block, axis, steps):
-    blocks = {0: block}
-    for bit in steps:
-        blocks.update({at ^ bit: swap(held, axis, bit) for at, held in list(blocks.items())})
-    return [blocks[at] for at in range(len(blocks))]
 
 
 def local(
@@ -429,12 +490,9 @@
     wide_halo = LANES // (width // HEADS) * 2 * WIN * HALF
     sent = height * HALF
 
-    steps = [1 << k for k in range(band_count.bit_length() - 1)]
-    weights_in = gather_blocks(expert_in[0], "band", steps)
-    weights_out = gather_blocks(expert_out[0], "band", steps[::-1])
-
-    tables = jnp.concatenate([table_regular, table_shifted], axis=1).T * LOG2E
-    tables = jnp.pad(tables, ((0, 0), (0, 2 * LANES - tables.shape[1])))
+    in_next = swap(expert_in[0], "band", 1)
+    out_next = swap(expert_out[0], "band", 2)
+
     info = jnp.stack([band_index == 0, band_index == band_count - 1]).astype(I32)
     turn = HALF * band_width
     route_row = jnp.roll(routes.reshape(1, rows), -turn, axis=1) ^ lax.axis_index("expert")
@@ -443,27 +501,40 @@
         functools.partial(front_kernel, band_width),
         [shape_of(rows, width), shape_of(sent, width), shape_of(sent, width)],
         [
+            table_regular.T,
             features.reshape(rows, width),
             qkv_regular,
             proj_regular,
-            tables,
             gain_regular.reshape(1, width),
             mlp_up,
             mlp_down,
             gain_mlp.reshape(1, width),
         ],
-        [
+        "hhhhhhhh",
+        [
+            pltpu.VMEM((rows, width), BF),
+            pltpu.VMEM((width, 3 * width), BF),
+            pltpu.VMEM((width, width), BF),
+            pltpu.VMEM((1, width), F32),
+            pltpu.VMEM((width, hidden), BF),
+            pltpu.VMEM((hidden, width), BF),
+            pltpu.VMEM((1, width), F32),
+            pltpu.VMEM(table_regular.shape[::-1], F32),
+            pltpu.SemaphoreType.DMA((8,)),
+            pltpu.VMEM((HEADS, 2 * LANES), F32),
             pltpu.VMEM((rows, 3 * width), BF),
             pltpu.VMEM((tiles, strip, wide), F32),
             pltpu.VMEM((rows, width), BF),
+            pltpu.VMEM((rows, hidden), BF),
             pltpu.VMEM((rows, width), BF),
         ],
+        limit=60,
         flops=2 * rows * width * (4 * width + 2 * hidden),
     )
     ring = range(band_count)
     from_right = lax.ppermute(to_left, "band", [(i, (i - 1) % band_count) for i in ring])
     from_left = lax.ppermute(to_right, "band", [(i, (i + 1) % band_count) for i in ring])
-    qkv, bias, bias_halo, slot_row, slot_col = call(
+    qkv, bias, bias_halo, slot_row, slot_col, wqkv, in_own, out_own = call(
         functools.partial(middle_kernel, band_width, experts, capacity),
         [
             shape_of(rows, 3 * width),
@@ -471,11 +542,34 @@
             shape_of(tiles, strip, wide_halo, dtype=F32),
             shape_of(8, rows, dtype=I32),
             shape_of(rows, LANES, dtype=I32),
-        ],
-        [info, second, qkv_shifted, tables, route_row],
-        scalars=1,
+            shape_of(width, 3 * width),
+            shape_of(2, *expert_in.shape[1:]),
+            shape_of(2, *expert_out.shape[1:]),
+        ],
+        [
+            info,
+            second,
+            route_row,
+            table_shifted.T,
+            qkv_shifted,
+            expert_in[0],
+            in_next,
+            expert_out[0],
+            out_next,
+        ],
+        "svvhhhaha",
+        [
+            pltpu.VMEM(table_shifted.shape[::-1], F32),
+            pltpu.SemaphoreType.DMA((6,)),
+            pltpu.VMEM((HEADS, 2 * LANES), F32),
+        ],
         flops=2 * rows * width * 3 * width,
     )
+    from_left, from_right, in_own, out_own = lax.optimization_barrier(
+        (from_left, from_right, in_own, out_own)
+    )
+    in_far = swap(in_own, "band", 2)
+    out_far = swap(out_own, "band", 1)
     third, *outgoing = call(
         functools.partial(shifted_kernel, band_width, capacity),
         [shape_of(rows, width)] + [shape_of(capacity, width)] * experts,
@@ -485,35 +579,62 @@
             second,
             from_left,
             from_right,
-            qkv_shifted,
+            wqkv,
             bias,
             bias_halo,
+            slot_row,
             proj_shifted,
             gain_shifted.reshape(1, width),
-            slot_row,
-        ],
+        ],
+        "svvvvvvvvhh",
         [
             pltpu.VMEM((2 * sent, 2 * width), BF),
             pltpu.VMEM((rows, width), BF),
-        ],
-        scalars=1,
+            pltpu.VMEM((width, width), BF),
+            pltpu.VMEM((1, width), F32),
+            pltpu.SemaphoreType.DMA((2,)),
+        ],
         flops=2 * rows * width * 4 * width,
     )
-    arrived = [outgoing[0]] + [swap(outgoing[s], "expert", s) for s in range(1, experts)]
-    amount = experts // 4
-    results = []
-    for k in range(0, experts, amount):
-        results += call(
-            functools.partial(expert_kernel, amount, band_count),
-            [shape_of(capacity, width)] * amount,
-            arrived[k : k + amount] + weights_in + weights_out,
-            flops=4 * amount * capacity * width * hidden,
+    weights = [in_own, in_far, out_own, out_far]
+
+    def send(blocks, first):
+        return [swap(block, "expert", first + k) for k, block in enumerate(blocks)]
+
+    def compute(blocks):
+        return call(
+            functools.partial(expert_kernel, len(blocks)),
+            [shape_of(capacity, width)] * len(blocks),
+            blocks + weights,
+            "v" * (len(blocks) + 4),
+            flops=4 * len(blocks) * capacity * width * hidden,
         )
-    returned = [results[0]] + [swap(results[s], "expert", s) for s in range(1, experts)]
+
+    far, most = experts // 2, 3 * experts // 4
+    third_part = send(outgoing[far:most], far)
+    *third_part, = lax.optimization_barrier((*third_part, *outgoing[most:]))
+    fourth_part = send(third_part[most - far :], most)
+    third_part = compute(third_part[: most - far])
+    *third_part, = lax.optimization_barrier((*third_part, *outgoing[:far]))
+    near = third_part[most - far :]
+    near = near[:1] + send(near[1:], 1)
+    back_third = send(third_part[: most - far], far)
+    back_fourth = send(compute(fourth_part), most)
+    half = far // 2
+    first_part, second_part = compute(near[:half]), compute(near[half:])
+    returned = (
+        first_part[:1]
+        + send(first_part[1:], 1)
+        + send(second_part, half)
+        + back_third
+        + back_fourth
+    )
     encoded = call(
         functools.partial(final_kernel, band_width, capacity),
         [shape_of(rows, width)],
         [third, slot_col, gain_expert.reshape(1, width)] + returned,
+        "vvh" + "v" * experts,
+        [pltpu.VMEM((1, width), F32), pltpu.SemaphoreType.DMA((1,))],
         flops=2 * rows * width * 2 * rows,
     )[0]
     return encoded.reshape(crop_count, height, band_width, width)

time: 103 us -> 82.3 us (0.80)
  local copies, waits for them, and re-layouts: 11.5 us -> 1.3 us
  starting transfers between devices: 33.6 us -> 27.1 us
  waiting for transfers between devices: 29.3 us -> 23.2 us
  Pallas kernels: 27.3 us -> 30 us
    unnamed x37 -> x19, local copies, waits for them, and re-layouts: 11.4 us -> 1.14 us
    ppermute x20 -> x18, starting transfers between devices: 33.4 us -> 24.7 us  [swap(): lax.ppermute(block, axis, [(i, i ^ bits) for i in range(lax.axis_size(axi...]
    ppermute x1, waiting for transfers between devices: 5.14 us -> 0.01 us  [local(): lax.ppermute(to_left, 'band', [(i, (i - 1) % band_count) for i in ring])]
    pallas_call x8, Pallas kernels: 27.3 us -> 30 us  [call(): pl.pallas_call(kernel, out_shape=outs, in_specs=[pl.BlockSpec(memory_spac...]
    ppermute x1, starting transfers between devices: 0.01 us -> 2.12 us  [local(): lax.ppermute(to_left, 'band', [(i, (i - 1) % band_count) for i in ring])]
    ppermute x1, waiting for transfers between devices: 2.06 us -> 0.01 us  [local(): lax.ppermute(to_right, 'band', [(i, (i + 1) % band_count) for i in ring])]
    ppermute x20 -> x18, waiting for transfers between devices: 22.1 us -> 23.2 us  [swap(): lax.ppermute(block, axis, [(i, i ^ bits) for i in range(lax.axis_size(axi...]
  transfers between devices with their start and end apart: 22 -> 20, of which waited for: 9 -> 7; matrix products, arithmetic and copies ran while one was open for 1% -> 0% of each run, Pallas kernels for 25% -> 34%
where the time goes in v1:
time: 82.3 us; the launch traced here: 82.2 us
  Pallas kernels  30 us (36%)
  starting transfers between devices  27.1 us (33%)
  waiting for transfers between devices  23.2 us (28%)
  local copies, waits for them, and re-layouts  1.3 us (2%)
    pallas_call x8, Pallas kernels, call(): pl.pallas_call(kernel, out_shape=outs, in_specs=[pl.BlockSpec(memory_spac...  30 us
    ppermute x18, starting transfers between devices, swap(): lax.ppermute(block, axis, [(i, i ^ bits) for i in range(lax.axis_size(axi...  24.7 us
    ppermute x18, waiting for transfers between devices, swap(): lax.ppermute(block, axis, [(i, i ^ bits) for i in range(lax.axis_size(axi...  23.2 us
    ppermute x1, starting transfers between devices, local(): lax.ppermute(to_left, 'band', [(i, (i - 1) % band_count) for i in ring])  2.12 us
  transfers between devices with their start and end apart: 20, of which 7 were waited for; matrix products, arithmetic and copies ran while one was open for 0% of the time, Pallas kernels for 34%

profile of v1, /device:TPU:1, one launch (start us, length us, event | category | flops | bytes accessed | tf_op | source)
XLA Modules:
  0.0 82.2 jit_solution(1530307520097062703)
XLA Ops:
  0.0 2.0 %collective-permute-start = (bf16[512,512]{1,0:T(8,128)(2,1)}, bf16[512,512]{1,0:T(8,128)(2,1)S(1)}, u32[]{:S(2)}, u32[]{:S(2)}) collective-permute-start(bf16[512,512]{1,0:T(8,128)(2,1)} %bitcast.16), channel_id=1, source_target_pairs={{0,8},{8,0},{16,24},{24,16},{1,9},{9,1},{17,25},{25,17},{2,10},{10... | collective-permute-start | bytes 1572872 | tf_op jit(solution)/shard_map/ppermute | solution.py:459
  2.0 1.2 %collective-permute-start.1 = (bf16[512,512]{1,0:T(8,128)(2,1)}, bf16[512,512]{1,0:T(8,128)(2,1)}, u32[]{:S(2)}, u32[]{:S(2)}) collective-permute-start(bf16[512,512]{1,0:T(8,128)(2,1)} %bitcast.18), channel_id=1, source_target_pairs={{0,16},{8,24},{16,0},{24,8},{1,17},{9,25},{17,1},{25,9},{2,18},{10... | collective-permute-start | bytes 1572872 | tf_op jit(solution)/shard_map/ppermute | solution.py:459
  3.3 10.2 %shard_map.154 = (bf16[512,512]{1,0:T(8,128)(2,1)}, bf16[128,512]{1,0:T(8,128)(2,1)}, bf16[128,512]{1,0:T(8,128)(2,1)}) custom-call(f32[16,225]{1,0:T(8,128)} %bitcast.24, bf16[512,512]{1,0:T(8,128)(2,1)} %bitcast.23, bf16[512,1536]{1,0:T(8,128)(2,1)} %wqkv_hbm.2, bf16[512,512]{1,0:T(8,128)(2,1)} %wproj_hbm.2, f32[1,512]{1,0:T(1,128)} %bitcast.25, ...), custom_call_target="tpu_custom_call" | custom-call | flops 3221225472 | bytes 7620672 | tf_op jit(solution)/shard_map/pallas_call | solution.py:442
  13.6 0.3 collective-permute-start.2
  13.8 2.1 %collective-permute-start.3 = (bf16[128,512]{1,0:T(8,128)(2,1)}, bf16[128,512]{1,0:T(8,128)(2,1)S(1)}, u32[]{:S(2)}, u32[]{:S(2)}) collective-permute-start(bf16[128,512]{1,0:T(8,128)(2,1)} %get-tuple-element.50), channel_id=1, source_target_pairs={{0,24},{8,0},{16,8},{24,16},{1,25},{9,1},{17,9},{25,17},{2,26},{10... | collective-permute-start | bytes 393224 | tf_op jit(solution)/shard_map/ppermute | solution.py:535
  16.0 0.1 copy.18
  16.0 0.1 reshape.52
  16.1 0.1 slice.10
  16.2 0.1 add_xor_fusion.routes_ref
  16.3 0.1 add_convert_fusion.info_ref
  16.4 0.0 collective-permute-done.in_next
  16.4 0.0 collective-permute-done.1.out_next
  16.4 0.0 copy-done.1
  16.4 0.0 copy-start
  16.4 1.0 %copy-done = bf16[512,512]{1,0:T(8,128)(2,1)S(1)} copy-done((bf16[512,512]{1,0:T(8,128)(2,1)S(1)}, bf16[512,512]{1,0:T(8,128)(2,1)}, u32[]{:S(2)}) %copy-start) | copy-done | bytes 524312
  17.5 4.9 %shard_map.155 = (bf16[512,1536]{1,0:T(8,128)(2,1)S(1)}, f32[4,128,512]{2,1,0:T(8,128)S(1)}, f32[4,128,256]{2,1,0:T(8,128)S(1)}, s32[8,512]{1,0:T(8,128)S(1)}, s...) custom-call(s32[2]{0:T(128)S(1)} %add_convert_fusion.info_ref, ...), custom_call_target="tpu_custom_call" | custom-call | flops 805306368 | bytes 11305032 | tf_op jit(solution)/shard_map/pallas_call | solution.py:442
  22.4 0.0 collective-permute-done.2.from_left_ref
  22.4 0.3 collective-permute-start.6
  22.7 0.1 collective-permute-start.7
  22.8 6.5 %shard_map.156 = (bf16[512,512]{1,0:T(8,128)(2,1)S(1)}, bf16[128,512]{1,0:T(8,128)(2,1)S(1)}, bf16[128,512]{1,0:T(8,128)(2,1)S(1)}, bf16[128,512]{1,0:T(8,128)(2...) custom-call(s32[2]{0:T(128)S(1)} %add_convert_fusion.info_ref, ...), custom_call_target="tpu_custom_call" | custom-call | flops 1073741824 | bytes 7620616 | tf_op jit(solution)/shard_map/pallas_call | solution.py:442
  29.3 2.4 %collective-permute-start.4 = (bf16[128,512]{1,0:T(8,128)(2,1)S(1)}, bf16[128,512]{1,0:T(8,128)(2,1)S(1)}, u32[]{:S(2)}, u32[]{:S(2)}) collective-permute-start(bf16[128,512]{1,0:T(8,128)(2,1)S(1)} %get-tuple-element.61), channel_id=1, source_target_pairs={{0,4},{1,5},{2,6},{3,7},{4,0},{5,1},{6,2},{7,3},{8,12},{9,13},{10,... | collective-permute-start | bytes 393224 | tf_op jit(solution)/shard_map/ppermute | solution.py:459
  31.7 2.5 %collective-permute-start.5 = (bf16[128,512]{1,0:T(8,128)(2,1)S(1)}, bf16[128,512]{1,0:T(8,128)(2,1)S(1)}, u32[]{:S(2)}, u32[]{:S(2)}) collective-permute-start(bf16[128,512]{1,0:T(8,128)(2,1)S(1)} %get-tuple-element.62), channel_id=1, source_target_pairs={{0,5},{1,4},{2,7},{3,6},{4,1},{5,0},{6,3},{7,2},{8,13},{9,12},{10,... | collective-permute-start | bytes 393224 | tf_op jit(solution)/shard_map/ppermute | solution.py:459
  34.2 1.6 %collective-permute-done.4.refs_0_ = bf16[128,512]{1,0:T(8,128)(2,1)S(1)} collective-permute-done((bf16[128,512]{1,0:T(8,128)(2,1)S(1)}, bf16[128,512]{1,0:T(8,128)(2,1)S(1)}, u32[]{:S(2)}, u32[]{:S(2)}) %collective-permute-start.4) | collective-permute-done | bytes 131104 | tf_op jit(solution)/shard_map/ppermute | solution.py:459
  35.8 8.1 %collective-permute-done.5.refs_1_ = bf16[128,512]{1,0:T(8,128)(2,1)S(1)} collective-permute-done((bf16[128,512]{1,0:T(8,128)(2,1)S(1)}, bf16[128,512]{1,0:T(8,128)(2,1)S(1)}, u32[]{:S(2)}, u32[]{:S(2)}) %collective-permute-start.5) | collective-permute-done | bytes 131104 | tf_op jit(solution)/shard_map/ppermute | solution.py:459
  44.0 3.9 %collective-permute-start.16 = (bf16[128,512]{1,0:T(8,128)(2,1)S(1)}, bf16[128,512]{1,0:T(8,128)(2,1)S(1)}, u32[]{:S(2)}, u32[]{:S(2)}) collective-permute-start(bf16[128,512]{1,0:T(8,128)(2,1)S(1)} %get-tuple-element.85), channel_id=1, source_target_pairs={{0,6},{1,7},{2,4},{3,5},{4,2},{5,3},{6,0},{7,1},{8,14},{9,15},{10,... | collective-permute-start | bytes 393224 | tf_op jit(solution)/shard_map/ppermute | solution.py:459
  47.9 1.6 %shard_map.157 = (bf16[128,512]{1,0:T(8,128)(2,1)S(1)}, bf16[128,512]{1,0:T(8,128)(2,1)S(1)}) custom-call(bf16[128,512]{1,0:T(8,128)(2,1)S(1)} %collective-permute-done.4.refs_0_, bf16[128,512]{1,0:T(8,128)(2,1)S(1)} %collective-permute-done.5.refs_1_, bf16[2,512,512]{2,1,0:T(8,128)(2,1)S(1)} %get-tuple-element.67.refs_2_, ...), custom_call_target="tpu_custom_call" | custom-call | flops 1073741824 | bytes 4718592 | tf_op jit(solution)/shard_map/pallas_call | solution.py:442
  49.5 0.5 collective-permute-start.8
  49.9 1.3 %collective-permute-start.10 = (bf16[128,512]{1,0:T(8,128)(2,1)S(1)}, bf16[128,512]{1,0:T(8,128)(2,1)S(1)}, u32[]{:S(2)}, u32[]{:S(2)}) collective-permute-start(bf16[128,512]{1,0:T(8,128)(2,1)S(1)} %get-tuple-element.79), channel_id=1, source_target_pairs={{0,2},{1,3},{2,0},{3,1},{4,6},{5,7},{6,4},{7,5},{8,10},{9,11},{10,... | collective-permute-start | bytes 393224 | tf_op jit(solution)/shard_map/ppermute | solution.py:459
  51.2 0.4 collective-permute-start.11
  51.7 0.3 collective-permute-done.16.refs_0_
  51.9 2.0 %collective-permute-start.14 = (bf16[128,512]{1,0:T(8,128)(2,1)S(1)}, bf16[128,512]{1,0:T(8,128)(2,1)S(1)}, u32[]{:S(2)}, u32[]{:S(2)}) collective-permute-start(bf16[128,512]{1,0:T(8,128)(2,1)S(1)} %get-tuple-element.83), channel_id=1, source_target_pairs={{0,4},{1,5},{2,6},{3,7},{4,0},{5,1},{6,2},{7,3},{8,12},{9,13},{10,... | collective-permute-start | bytes 393224 | tf_op jit(solution)/shard_map/ppermute | solution.py:459
  54.0 0.7 collective-permute-done.17.refs_1_
  54.6 4.2 %collective-permute-start.15 = (bf16[128,512]{1,0:T(8,128)(2,1)S(1)}, bf16[128,512]{1,0:T(8,128)(2,1)S(1)}, u32[]{:S(2)}, u32[]{:S(2)}) collective-permute-start(bf16[128,512]{1,0:T(8,128)(2,1)S(1)} %get-tuple-element.84), channel_id=1, source_target_pairs={{0,5},{1,4},{2,7},{3,6},{4,1},{5,0},{6,3},{7,2},{8,13},{9,12},{10,... | collective-permute-start | bytes 393224 | tf_op jit(solution)/shard_map/ppermute | solution.py:459
  58.8 1.6 %shard_map.160 = (bf16[128,512]{1,0:T(8,128)(2,1)S(1)}, bf16[128,512]{1,0:T(8,128)(2,1)S(1)}) custom-call(bf16[128,512]{1,0:T(8,128)(2,1)S(1)} %collective-permute-done.16.refs_0_, bf16[128,512]{1,0:T(8,128)(2,1)S(1)} %collective-permute-done.17.refs_1_, bf16[2,512,512]{2,1,0:T(8,128)(2,1)S(1)} %get-tuple-element.67.refs_2_, ...), custom_call_target="tpu_custom_call" | custom-call | flops 1073741824 | bytes 4718592 | tf_op jit(solution)/shard_map/pallas_call | solution.py:442
  60.4 0.9 %collective-permute-start.18 = (bf16[128,512]{1,0:T(8,128)(2,1)S(1)}, bf16[128,512]{1,0:T(8,128)(2,1)S(1)}, u32[]{:S(2)}, u32[]{:S(2)}) collective-permute-start(bf16[128,512]{1,0:T(8,128)(2,1)S(1)} %get-tuple-element.87), channel_id=1, source_target_pairs={{0,6},{1,7},{2,4},{3,5},{4,2},{5,3},{6,0},{7,1},{8,14},{9,15},{10,... | collective-permute-start | bytes 393224 | tf_op jit(solution)/shard_map/ppermute | solution.py:459
  61.3 1.6 %shard_map.158 = (bf16[128,512]{1,0:T(8,128)(2,1)S(1)}, bf16[128,512]{1,0:T(8,128)(2,1)S(1)}) custom-call(bf16[128,512]{1,0:T(8,128)(2,1)S(1)} %get-tuple-element.75.refs_0_, bf16[128,512]{1,0:T(8,128)(2,1)S(1)} %collective-permute-done.8.refs_1_, bf16[2,512,512]{2,1,0:T(8,128)(2,1)S(1)} %get-tuple-element.67.refs_2_, ...), custom_call_target="tpu_custom_call" | custom-call | flops 1073741824 | bytes 4718592 | tf_op jit(solution)/shard_map/pallas_call | solution.py:442
  62.9 0.0 collective-permute-done.10.refs_0_
  62.9 2.4 %collective-permute-start.19 = (bf16[128,512]{1,0:T(8,128)(2,1)S(1)}, bf16[128,512]{1,0:T(8,128)(2,1)S(1)}, u32[]{:S(2)}, u32[]{:S(2)}) collective-permute-start(bf16[128,512]{1,0:T(8,128)(2,1)S(1)} %get-tuple-element.88), channel_id=1, source_target_pairs={{0,7},{1,6},{2,5},{3,4},{4,3},{5,2},{6,1},{7,0},{8,15},{9,14},{10,... | collective-permute-start | bytes 393224 | tf_op jit(solution)/shard_map/ppermute | solution.py:459
  65.3 0.0 collective-permute-done.11.refs_1_
  65.3 0.5 collective-permute-start.9
  65.8 1.6 %shard_map.159 = (bf16[128,512]{1,0:T(8,128)(2,1)S(1)}, bf16[128,512]{1,0:T(8,128)(2,1)S(1)}) custom-call(bf16[128,512]{1,0:T(8,128)(2,1)S(1)} %collective-permute-done.10.refs_0_, bf16[128,512]{1,0:T(8,128)(2,1)S(1)} %collective-permute-done.11.refs_1_, bf16[2,512,512]{2,1,0:T(8,128)(2,1)S(1)} %get-tuple-element.67.refs_2_, ...), custom_call_target="tpu_custom_call" | custom-call | flops 1073741824 | bytes 4718592 | tf_op jit(solution)/shard_map/pallas_call | solution.py:442
  67.4 0.0 collective-permute-done.14.rest_4_
  67.5 0.1 collective-permute-start.12
  67.5 7.4 %collective-permute-done.15.rest_5_ = bf16[128,512]{1,0:T(8,128)(2,1)S(1)} collective-permute-done((bf16[128,512]{1,0:T(8,128)(2,1)S(1)}, bf16[128,512]{1,0:T(8,128)(2,1)S(1)}, u32[]{:S(2)}, u32[]{:S(2)}) %collective-permute-start.15) | collective-permute-done | bytes 131104 | tf_op jit(solution)/shard_map/ppermute | solution.py:459
  74.9 0.0 collective-permute-done.18.rest_6_
  75.0 1.2 %collective-permute-done.12.rest_2_ = bf16[128,512]{1,0:T(8,128)(2,1)S(1)} collective-permute-done((bf16[128,512]{1,0:T(8,128)(2,1)S(1)}, bf16[128,512]{1,0:T(8,128)(2,1)S(1)}, u32[]{:S(2)}, u32[]{:S(2)}) %collective-permute-start.12) | collective-permute-done | bytes 131104 | tf_op jit(solution)/shard_map/ppermute | solution.py:459
  76.2 3.9 %collective-permute-done.13.rest_3_ = bf16[128,512]{1,0:T(8,128)(2,1)S(1)} collective-permute-done((bf16[128,512]{1,0:T(8,128)(2,1)S(1)}, bf16[128,512]{1,0:T(8,128)(2,1)S(1)}, u32[]{:S(2)}, u32[]{:S(2)}) %collective-permute-start.13) | collective-permute-done | bytes 131104 | tf_op jit(solution)/shard_map/ppermute | solution.py:459
  80.1 1.9 %shard_map.161 = bf16[512,512]{1,0:T(8,128)(2,1)} custom-call(bf16[512,512]{1,0:T(8,128)(2,1)S(1)} %get-tuple-element.59.third_ref, s32[512,128]{1,0:T(8,128)S(1)} %get-tuple-element.60.slot_col_ref, f32[1,512]{1,0:T(1,128)S(1)} %bitcast.22, bf16[128,512]{1,0:T(8,128)(2,1)S(1)} %get-tuple-element.77.rest_0_, ...), custom_call_target="tpu_custom_call" | custom-call | flops 536870912 | bytes 2361344 | tf_op jit(solution)/shard_map/pallas_call | solution.py:442
  (24 shorter events, 0.1 us)
Async XLA Ops:
  0.0 16.4 %collective-permute-start = (bf16[512,512]{1,0:T(8,128)(2,1)}, bf16[512,512]{1,0:T(8,128)(2,1)S(1)}, u32[]{:S(2)}, u32[]{:S(2)}) collective-permute-start(bf16[512,512]{1,0:T(8,128)(2,1)} %bitcast.16), channel_id=1, source_target_pairs={{0,8},{8,0},{16,24},{24,16},{1,9},{9,1},{17,25},{25,17},{2,10},{10... | collective-permute-start | bytes 1572872 | tf_op jit(solution)/shard_map/ppermute | solution.py:459
  2.0 14.3 %collective-permute-start.1 = (bf16[512,512]{1,0:T(8,128)(2,1)}, bf16[512,512]{1,0:T(8,128)(2,1)}, u32[]{:S(2)}, u32[]{:S(2)}) collective-permute-start(bf16[512,512]{1,0:T(8,128)(2,1)} %bitcast.18), channel_id=1, source_target_pairs={{0,16},{8,24},{16,0},{24,8},{1,17},{9,25},{17,1},{25,9},{2,18},{10... | collective-permute-start | bytes 1572872 | tf_op jit(solution)/shard_map/ppermute | solution.py:459
  3.3 12.7 %copy-start.8 = (s32[1,1,32,16,1]{2,4,3,1,0:T(1,128)S(1)}, s32[1,1,32,16,1]{2,4,3,1,0:T(1,128)}, u32[]{:S(2)}) copy-start(s32[1,1,32,16,1]{2,4,3,1,0:T(1,128)} %param.17) | copy-start | bytes 6148
  3.3 13.1 %copy-start.1 = (bf16[512,1536]{1,0:T(8,128)(2,1)S(1)}, bf16[512,1536]{1,0:T(8,128)(2,1)}, u32[]{:S(2)}) copy-start(bf16[512,1536]{1,0:T(8,128)(2,1)} %wqkv_hbm.3) | copy-start | bytes 4718596
  3.3 13.1 %copy-start.3 = (bf16[1,512,512]{2,1,0:T(8,128)(2,1)S(1)}, bf16[1,512,512]{2,1,0:T(8,128)(2,1)}, u32[]{:S(2)}) copy-start(bf16[1,512,512]{2,1,0:T(8,128)(2,1)} %param.29) | copy-start | bytes 1572868
  3.3 13.1 %copy-start.4 = (bf16[1,512,512]{2,1,0:T(8,128)(2,1)S(1)}, bf16[1,512,512]{2,1,0:T(8,128)(2,1)}, u32[]{:S(2)}) copy-start(bf16[1,512,512]{2,1,0:T(8,128)(2,1)} %param.30) | copy-start | bytes 1572868
  3.3 13.1 %copy-start.5 = (f32[225,16]{0,1:T(8,128)S(1)}, f32[225,16]{0,1:T(8,128)}, u32[]{:S(2)}) copy-start(f32[225,16]{0,1:T(8,128)} %param.27) | copy-start | bytes 43204
  13.6 8.8 %collective-permute-start.2 = (bf16[128,512]{1,0:T(8,128)(2,1)}, bf16[128,512]{1,0:T(8,128)(2,1)S(1)}, u32[]{:S(2)}, u32[]{:S(2)}) collective-permute-start(bf16[128,512]{1,0:T(8,128)(2,1)} %get-tuple-element.49), channel_id=1, source_target_pairs={{0,8},{8,16},{16,24},{24,0},{1,9},{9,17},{17,25},{25,1},{2,10},{10... | collective-permute-start | bytes 393224 | tf_op jit(solution)/shard_map/ppermute | solution.py:536
  13.8 8.6 %collective-permute-start.3 = (bf16[128,512]{1,0:T(8,128)(2,1)}, bf16[128,512]{1,0:T(8,128)(2,1)S(1)}, u32[]{:S(2)}, u32[]{:S(2)}) collective-permute-start(bf16[128,512]{1,0:T(8,128)(2,1)} %get-tuple-element.50), channel_id=1, source_target_pairs={{0,24},{8,0},{16,8},{24,16},{1,25},{9,1},{17,9},{25,17},{2,26},{10... | collective-permute-start | bytes 393224 | tf_op jit(solution)/shard_map/ppermute | solution.py:535
  16.4 1.0 %copy-start = (bf16[512,512]{1,0:T(8,128)(2,1)S(1)}, bf16[512,512]{1,0:T(8,128)(2,1)}, u32[]{:S(2)}) copy-start(bf16[512,512]{1,0:T(8,128)(2,1)} %get-tuple-element.47.x_ref) | copy-start | bytes 1572868
  17.5 5.3 %copy-start.2 = (bf16[512,512]{1,0:T(8,128)(2,1)S(1)}, bf16[512,512]{1,0:T(8,128)(2,1)}, u32[]{:S(2)}) copy-start(bf16[512,512]{1,0:T(8,128)(2,1)} %wproj_hbm.3) | copy-start | bytes 1572868
  17.5 5.3 %copy-start.6 = (f32[512]{0:T(512)S(1)}, f32[512]{0:T(512)}, u32[]{:S(2)}) copy-start(f32[512]{0:T(512)} %param.28) | copy-start | bytes 6148
  22.4 25.4 %collective-permute-start.6 = (bf16[2,512,512]{2,1,0:T(8,128)(2,1)S(1)}, bf16[2,512,512]{2,1,0:T(8,128)(2,1)S(1)}, u32[]{:S(2)}, u32[]{:S(2)}) collective-permute-start(bf16[2,512,512]{2,1,0:T(8,128)(2,1)S(1)} %get-tuple-element.67.refs_2_), channel_id=1, source_target_pairs={{0,16},{8,24},{16,0},{24,8},{1,17},{9,25},{17,1},{25,9},{2,18},{10... | collective-permute-start | bytes 3145736 | tf_op jit(solution)/shard_map/ppermute | solution.py:459
  22.7 25.1 %collective-permute-start.7 = (bf16[2,512,512]{2,1,0:T(8,128)(2,1)S(1)}, bf16[2,512,512]{2,1,0:T(8,128)(2,1)S(1)}, u32[]{:S(2)}, u32[]{:S(2)}) collective-permute-start(bf16[2,512,512]{2,1,0:T(8,128)(2,1)S(1)} %get-tuple-element.68.refs_4_), channel_id=1, source_target_pairs={{0,8},{8,0},{16,24},{24,16},{1,9},{9,1},{17,25},{25,17},{2,10},{10... | collective-permute-start | bytes 3145736 | tf_op jit(solution)/shard_map/ppermute | solution.py:459
  29.3 6.5 %collective-permute-start.4 = (bf16[128,512]{1,0:T(8,128)(2,1)S(1)}, bf16[128,512]{1,0:T(8,128)(2,1)S(1)}, u32[]{:S(2)}, u32[]{:S(2)}) collective-permute-start(bf16[128,512]{1,0:T(8,128)(2,1)S(1)} %get-tuple-element.61), channel_id=1, source_target_pairs={{0,4},{1,5},{2,6},{3,7},{4,0},{5,1},{6,2},{7,3},{8,12},{9,13},{10,... | collective-permute-start | bytes 393224 | tf_op jit(solution)/shard_map/ppermute | solution.py:459
  31.7 12.3 %collective-permute-start.5 = (bf16[128,512]{1,0:T(8,128)(2,1)S(1)}, bf16[128,512]{1,0:T(8,128)(2,1)S(1)}, u32[]{:S(2)}, u32[]{:S(2)}) collective-permute-start(bf16[128,512]{1,0:T(8,128)(2,1)S(1)} %get-tuple-element.62), channel_id=1, source_target_pairs={{0,5},{1,4},{2,7},{3,6},{4,1},{5,0},{6,3},{7,2},{8,13},{9,12},{10,... | collective-permute-start | bytes 393224 | tf_op jit(solution)/shard_map/ppermute | solution.py:459
  44.0 8.0 %collective-permute-start.16 = (bf16[128,512]{1,0:T(8,128)(2,1)S(1)}, bf16[128,512]{1,0:T(8,128)(2,1)S(1)}, u32[]{:S(2)}, u32[]{:S(2)}) collective-permute-start(bf16[128,512]{1,0:T(8,128)(2,1)S(1)} %get-tuple-element.85), channel_id=1, source_target_pairs={{0,6},{1,7},{2,4},{3,5},{4,2},{5,3},{6,0},{7,1},{8,14},{9,15},{10,... | collective-permute-start | bytes 393224 | tf_op jit(solution)/shard_map/ppermute | solution.py:459
  47.8 6.8 %collective-permute-start.17 = (bf16[128,512]{1,0:T(8,128)(2,1)S(1)}, bf16[128,512]{1,0:T(8,128)(2,1)S(1)}, u32[]{:S(2)}, u32[]{:S(2)}) collective-permute-start(bf16[128,512]{1,0:T(8,128)(2,1)S(1)} %get-tuple-element.86), channel_id=1, source_target_pairs={{0,7},{1,6},{2,5},{3,4},{4,3},{5,2},{6,1},{7,0},{8,15},{9,14},{10,... | collective-permute-start | bytes 393224 | tf_op jit(solution)/shard_map/ppermute | solution.py:459
  49.5 11.0 %collective-permute-start.8 = (bf16[128,512]{1,0:T(8,128)(2,1)S(1)}, bf16[128,512]{1,0:T(8,128)(2,1)S(1)}, u32[]{:S(2)}, u32[]{:S(2)}) collective-permute-start(bf16[128,512]{1,0:T(8,128)(2,1)S(1)} %get-tuple-element.76), channel_id=1, source_target_pairs={{0,1},{1,0},{2,3},{3,2},{4,5},{5,4},{6,7},{7,6},{8,9},{9,8},{10,11... | collective-permute-start | bytes 393224 | tf_op jit(solution)/shard_map/ppermute | solution.py:459
  49.9 13.0 %collective-permute-start.10 = (bf16[128,512]{1,0:T(8,128)(2,1)S(1)}, bf16[128,512]{1,0:T(8,128)(2,1)S(1)}, u32[]{:S(2)}, u32[]{:S(2)}) collective-permute-start(bf16[128,512]{1,0:T(8,128)(2,1)S(1)} %get-tuple-element.79), channel_id=1, source_target_pairs={{0,2},{1,3},{2,0},{3,1},{4,6},{5,7},{6,4},{7,5},{8,10},{9,11},{10,... | collective-permute-start | bytes 393224 | tf_op jit(solution)/shard_map/ppermute | solution.py:459
  51.2 14.1 %collective-permute-start.11 = (bf16[128,512]{1,0:T(8,128)(2,1)S(1)}, bf16[128,512]{1,0:T(8,128)(2,1)S(1)}, u32[]{:S(2)}, u32[]{:S(2)}) collective-permute-start(bf16[128,512]{1,0:T(8,128)(2,1)S(1)} %get-tuple-element.80), channel_id=1, source_target_pairs={{0,3},{1,2},{2,1},{3,0},{4,7},{5,6},{6,5},{7,4},{8,11},{9,10},{10,... | collective-permute-start | bytes 393224 | tf_op jit(solution)/shard_map/ppermute | solution.py:459
  51.9 15.5 %collective-permute-start.14 = (bf16[128,512]{1,0:T(8,128)(2,1)S(1)}, bf16[128,512]{1,0:T(8,128)(2,1)S(1)}, u32[]{:S(2)}, u32[]{:S(2)}) collective-permute-start(bf16[128,512]{1,0:T(8,128)(2,1)S(1)} %get-tuple-element.83), channel_id=1, source_target_pairs={{0,4},{1,5},{2,6},{3,7},{4,0},{5,1},{6,2},{7,3},{8,12},{9,13},{10,... | collective-permute-start | bytes 393224 | tf_op jit(solution)/shard_map/ppermute | solution.py:459
  54.6 20.3 %collective-permute-start.15 = (bf16[128,512]{1,0:T(8,128)(2,1)S(1)}, bf16[128,512]{1,0:T(8,128)(2,1)S(1)}, u32[]{:S(2)}, u32[]{:S(2)}) collective-permute-start(bf16[128,512]{1,0:T(8,128)(2,1)S(1)} %get-tuple-element.84), channel_id=1, source_target_pairs={{0,5},{1,4},{2,7},{3,6},{4,1},{5,0},{6,3},{7,2},{8,13},{9,12},{10,... | collective-permute-start | bytes 393224 | tf_op jit(solution)/shard_map/ppermute | solution.py:459
  60.4 14.5 %collective-permute-start.18 = (bf16[128,512]{1,0:T(8,128)(2,1)S(1)}, bf16[128,512]{1,0:T(8,128)(2,1)S(1)}, u32[]{:S(2)}, u32[]{:S(2)}) collective-permute-start(bf16[128,512]{1,0:T(8,128)(2,1)S(1)} %get-tuple-element.87), channel_id=1, source_target_pairs={{0,6},{1,7},{2,4},{3,5},{4,2},{5,3},{6,0},{7,1},{8,14},{9,15},{10,... | collective-permute-start | bytes 393224 | tf_op jit(solution)/shard_map/ppermute | solution.py:459
  62.9 12.0 %collective-permute-start.19 = (bf16[128,512]{1,0:T(8,128)(2,1)S(1)}, bf16[128,512]{1,0:T(8,128)(2,1)S(1)}, u32[]{:S(2)}, u32[]{:S(2)}) collective-permute-start(bf16[128,512]{1,0:T(8,128)(2,1)S(1)} %get-tuple-element.88), channel_id=1, source_target_pairs={{0,7},{1,6},{2,5},{3,4},{4,3},{5,2},{6,1},{7,0},{8,15},{9,14},{10,... | collective-permute-start | bytes 393224 | tf_op jit(solution)/shard_map/ppermute | solution.py:459
  65.3 14.8 %copy-start.7 = (f32[512]{0:T(512)S(1)}, f32[512]{0:T(512)}, u32[]{:S(2)}) copy-start(f32[512]{0:T(512)} %param.31) | copy-start | bytes 6148
  65.3 9.6 %collective-permute-start.9 = (bf16[128,512]{1,0:T(8,128)(2,1)S(1)}, bf16[128,512]{1,0:T(8,128)(2,1)S(1)}, u32[]{:S(2)}, u32[]{:S(2)}) collective-permute-start(bf16[128,512]{1,0:T(8,128)(2,1)S(1)} %get-tuple-element.78), channel_id=1, source_target_pairs={{0,1},{1,0},{2,3},{3,2},{4,5},{5,4},{6,7},{7,6},{8,9},{9,8},{10,11... | collective-permute-start | bytes 393224 | tf_op jit(solution)/shard_map/ppermute | solution.py:459
  67.5 8.7 %collective-permute-start.12 = (bf16[128,512]{1,0:T(8,128)(2,1)S(1)}, bf16[128,512]{1,0:T(8,128)(2,1)S(1)}, u32[]{:S(2)}, u32[]{:S(2)}) collective-permute-start(bf16[128,512]{1,0:T(8,128)(2,1)S(1)} %get-tuple-element.81), channel_id=1, source_target_pairs={{0,2},{1,3},{2,0},{3,1},{4,6},{5,7},{6,4},{7,5},{8,10},{9,11},{10,... | collective-permute-start | bytes 393224 | tf_op jit(solution)/shard_map/ppermute | solution.py:459
  74.9 5.1 %collective-permute-start.13 = (bf16[128,512]{1,0:T(8,128)(2,1)S(1)}, bf16[128,512]{1,0:T(8,128)(2,1)S(1)}, u32[]{:S(2)}, u32[]{:S(2)}) collective-permute-start(bf16[128,512]{1,0:T(8,128)(2,1)S(1)} %get-tuple-element.82), channel_id=1, source_target_pairs={{0,3},{1,2},{2,1},{3,0},{4,7},{5,6},{6,5},{7,4},{8,11},{9,10},{10,... | collective-permute-start | bytes 393224 | tf_op jit(solution)/shard_map/ppermute | solution.py:459

commit v2 on v1

--- a/solution.py
+++ b/solution.py
@@ -209,7 +209,7 @@
             heads[tokens, lanes] = (both[:, :LANES] / both[:, LANES:]).astype(BF)
         return carry
 
-    lax.fori_loop(0, width // LANES, tile_step, 0)
+    lax.fori_loop(0, width // LANES, tile_step, 0, unroll=True)
     for copy in copies:
         copy.wait()
     projected = dot(heads[...], wproj_ref[...])
@@ -228,12 +228,25 @@
     right_ref[...] = dot(jnp.where(t == place, 1.0, 0.0).astype(BF), rolled).astype(BF)
 
 
+def column_kernel(slot_row_ref, slot_col_ref):
+    rows = slot_row_ref.shape[1]
+    slot = slot_row_ref[...]
+    digit = iota(slot.shape, 0)
+    parts = jnp.where(
+        digit == 0, lax.rem(slot, LANES), jnp.where(digit == 1, lax.div(slot, LANES), 0)
+    )
+    same = jnp.where(iota((rows, rows), 0) == iota((rows, rows), 1), 1.0, 0.0).astype(BF)
+    turned = dot(same, parts.astype(F32).astype(BF), NT)
+    column = turned[:, 0:1] + turned[:, 1:2] * LANES
+    slot_col_ref[...] = jnp.broadcast_to(column, slot_col_ref.shape).astype(I32)
+
+
 def middle_kernel(
     band_width,
     experts,
     capacity,
     info_ref,
-    x_ref,
+    x_any,
     routes_ref,
     table_hbm,
     wqkv_hbm,
@@ -245,11 +258,11 @@
     bias_ref,
     bias_halo_ref,
     slot_row_ref,
-    slot_col_ref,
     wqkv_ref,
     in_pair,
     out_pair,
     table_ref,
+    x_ref,
     sems,
     tab_ref,
 ):
@@ -259,10 +272,7 @@
         sems,
         (table_hbm, table_ref),
         (wqkv_hbm, wqkv_ref),
-        (in_hbm, in_pair.at[0]),
-        (in_next, in_pair.at[1]),
-        (out_hbm, out_pair.at[0]),
-        (out_next, out_pair.at[1]),
+        (x_any, x_ref),
     )
     copies[0].wait()
     head_rows(table_ref, tab_ref)
@@ -276,14 +286,15 @@
     base = iota((experts, rows), 0).astype(F32) * capacity - 1.0
     slot = jnp.sum(named * (count + base), axis=0, keepdims=True)
     slot_row_ref[...] = jnp.broadcast_to(slot, slot_row_ref.shape).astype(I32)
-    same = jnp.where(a == b, 1.0, 0.0).astype(BF)
-    named_col = dot(same, named.astype(BF), NT)
-    before = jnp.where(a >= b, 1.0, 0.0).astype(BF)
-    count_col = dot(before, named_col.astype(BF))
-    base_col = iota((rows, experts), 1).astype(F32) * capacity - 1.0
-    slot_col = jnp.sum(named_col * (count_col + base_col), axis=1, keepdims=True)
-    slot_col_ref[...] = jnp.broadcast_to(slot_col, slot_col_ref.shape).astype(I32)
     copies[1].wait()
+    copies[2].wait()
+    copies = fetch(
+        sems.at[3:],
+        (in_hbm, in_pair.at[0]),
+        (in_next, in_pair.at[1]),
+        (out_hbm, out_pair.at[0]),
+        (out_next, out_pair.at[1]),
+    )
     x = x_ref[...]
     for part in range(3):
         cols = slice(part * width, (part + 1) * width)
@@ -291,7 +302,7 @@
         if part == 0:
             product = product * (LOG2E * head_dim**-0.5)
         qkv_ref[:, cols] = product.astype(BF)
-    for copy in copies[2:]:
+    for copy in copies:
         copy.wait()
 
 
@@ -385,16 +396,19 @@
             heads[tokens, lanes] = (both[:, :LANES] / both[:, LANES:]).astype(BF)
         return carry
 
-    lax.fori_loop(0, width // LANES, tile_step, 0)
+    lax.fori_loop(0, width // LANES, tile_step, 0, unroll=True)
     for copy in copies:
         copy.wait()
     projected = dot(heads[...], wproj_ref[...])
     third = (x_ref[...].astype(F32) + layer_norm(projected, gain_ref[...])).astype(BF)
     third_ref[...] = third
     slot = slot_row_ref[0:1, :]
-    for s, ref in enumerate(out_refs):
-        places = iota((capacity, rows), 0) + s * capacity
-        ref[...] = dot(jnp.where(places == slot, 1.0, 0.0).astype(BF), third).astype(BF)
+    group = max(1, 2 * LANES // capacity)
+    for s in range(0, len(out_refs), group):
+        places = iota((group * capacity, rows), 0) + s * capacity
+        sent = dot(jnp.where(places == slot, 1.0, 0.0).astype(BF), third).astype(BF)
+        for k in range(group):
+            out_refs[s + k][...] = sent[k * capacity : (k + 1) * capacity, :]
 
 
 def expert_kernel(amount, *refs):
@@ -418,16 +432,19 @@
     *result_refs, out_ref, gain_ref, sems = rest
     copies = fetch(sems, (gain_hbm, gain_ref))
     rows, width = third_ref.shape
-    results = jnp.concatenate([ref[...] for ref in result_refs], axis=0)
     slot = slot_col_ref[...]
-    chosen = jnp.concatenate(
-        [
-            jnp.where(slot == iota(slot.shape, 1) + k * LANES, 1.0, 0.0).astype(BF)
-            for k in range(results.shape[0] // LANES)
-        ],
-        axis=1,
-    )
-    picked = dot(chosen, results)
+    group = max(1, 2 * LANES // capacity)
+    picked = jnp.zeros((rows, width), F32)
+    for s in range(0, len(result_refs), group):
+        results = jnp.concatenate([ref[...] for ref in result_refs[s : s + group]], axis=0)
+        chosen = jnp.concatenate(
+            [
+                jnp.where(slot == iota(slot.shape, 1) + base, 1.0, 0.0).astype(BF)
+                for base in range(s * capacity, (s + group) * capacity, LANES)
+            ],
+            axis=1,
+        )
+        picked = picked + dot(chosen, results)
     copies[0].wait()
     encoded = (third_ref[...].astype(F32) + layer_norm(picked, gain_ref[...])).astype(BF)
     turn = HALF * band_width
@@ -534,14 +551,13 @@
     ring = range(band_count)
     from_right = lax.ppermute(to_left, "band", [(i, (i - 1) % band_count) for i in ring])
     from_left = lax.ppermute(to_right, "band", [(i, (i + 1) % band_count) for i in ring])
-    qkv, bias, bias_halo, slot_row, slot_col, wqkv, in_own, out_own = call(
+    qkv, bias, bias_halo, slot_row, wqkv, in_own, out_own = call(
         functools.partial(middle_kernel, band_width, experts, capacity),
         [
             shape_of(rows, 3 * width),
             shape_of(tiles, strip, wide, dtype=F32),
             shape_of(tiles, strip, wide_halo, dtype=F32),
             shape_of(8, rows, dtype=I32),
-            shape_of(rows, LANES, dtype=I32),
             shape_of(width, 3 * width),
             shape_of(2, *expert_in.shape[1:]),
             shape_of(2, *expert_out.shape[1:]),
@@ -557,10 +573,11 @@
             expert_out[0],
             out_next,
         ],
-        "svvhhhaha",
+        "savhhhaha",
         [
             pltpu.VMEM(table_shifted.shape[::-1], F32),
-            pltpu.SemaphoreType.DMA((6,)),
+            pltpu.VMEM((rows, width), BF),
+            pltpu.SemaphoreType.DMA((7,)),
             pltpu.VMEM((HEADS, 2 * LANES), F32),
         ],
         flops=2 * rows * width * 3 * width,
@@ -612,7 +629,10 @@
 
     far, most = experts // 2, 3 * experts // 4
     third_part = send(outgoing[far:most], far)
-    *third_part, = lax.optimization_barrier((*third_part, *outgoing[most:]))
+    slot_row, *third_part = lax.optimization_barrier(
+        (slot_row, *third_part, *outgoing[most:])
+    )
+    slot_col = call(column_kernel, [shape_of(rows, LANES, dtype=I32)], [slot_row], "v")[0]
     fourth_part = send(third_part[most - far :], most)
     third_part = compute(third_part[: most - far])
     *third_part, = lax.optimization_barrier((*third_part, *outgoing[:far]))

time: 82.3 us -> 82 us (level)
  starting transfers between devices: 27.1 us -> 29 us
  Pallas kernels: 30 us -> 28.3 us
    ppermute x18, starting transfers between devices: 24.7 us -> 26.6 us  [swap(): lax.ppermute(block, axis, [(i, i ^ bits) for i in range(lax.axis_size(axi...]
    pallas_call x8 -> x9, Pallas kernels: 30 us -> 28.3 us  [call(): pl.pallas_call(kernel, out_shape=outs, in_specs=[pl.BlockSpec(memory_spac...]
  transfers between devices with their start and end apart: 20 -> 20, of which waited for: 7 -> 5; matrix products, arithmetic and copies ran while one was open for 0% -> 0% of each run, Pallas kernels for 34% -> 32%
where the time goes in v2:
time: 82 us; the launch traced here: 81.7 us
  starting transfers between devices  29 us (35%)
  Pallas kernels  28.3 us (35%)
  waiting for transfers between devices  22.6 us (28%)
  local copies, waits for them, and re-layouts  1.3 us (2%)
    pallas_call x9, Pallas kernels, call(): pl.pallas_call(kernel, out_shape=outs, in_specs=[pl.BlockSpec(memory_spac...  28.3 us
    ppermute x18, starting transfers between devices, swap(): lax.ppermute(block, axis, [(i, i ^ bits) for i in range(lax.axis_size(axi...  26.6 us
    ppermute x18, waiting for transfers between devices, swap(): lax.ppermute(block, axis, [(i, i ^ bits) for i in range(lax.axis_size(axi...  22.6 us
    ppermute x1, starting transfers between devices, local(): lax.ppermute(to_left, 'band', [(i, (i - 1) % band_count) for i in ring])  2.12 us
  transfers between devices with their start and end apart: 20, of which 5 were waited for; matrix products, arithmetic and copies ran while one was open for 0% of the time, Pallas kernels for 32%

profile of v2, /device:TPU:1, one launch (start us, length us, event | category | flops | bytes accessed | tf_op | source)
XLA Modules:
  0.0 81.7 jit_solution(10144469913424255742)
XLA Ops:
  0.0 2.0 %collective-permute-start = (bf16[512,512]{1,0:T(8,128)(2,1)}, bf16[512,512]{1,0:T(8,128)(2,1)S(1)}, u32[]{:S(2)}, u32[]{:S(2)}) collective-permute-start(bf16[512,512]{1,0:T(8,128)(2,1)} %bitcast.16), channel_id=1, source_target_pairs={{0,8},{8,0},{16,24},{24,16},{1,9},{9,1},{17,25},{25,17},{2,10},{10... | collective-permute-start | bytes 1572872 | tf_op jit(solution)/shard_map/ppermute | solution.py:476
  2.0 1.2 %collective-permute-start.1 = (bf16[512,512]{1,0:T(8,128)(2,1)}, bf16[512,512]{1,0:T(8,128)(2,1)}, u32[]{:S(2)}, u32[]{:S(2)}) collective-permute-start(bf16[512,512]{1,0:T(8,128)(2,1)} %bitcast.18), channel_id=1, source_target_pairs={{0,16},{8,24},{16,0},{24,8},{1,17},{9,25},{17,1},{25,9},{2,18},{10... | collective-permute-start | bytes 1572872 | tf_op jit(solution)/shard_map/ppermute | solution.py:476
  3.3 9.1 %shard_map.154 = (bf16[512,512]{1,0:T(8,128)(2,1)}, bf16[128,512]{1,0:T(8,128)(2,1)}, bf16[128,512]{1,0:T(8,128)(2,1)}) custom-call(f32[16,225]{1,0:T(8,128)} %bitcast.24, bf16[512,512]{1,0:T(8,128)(2,1)} %bitcast.23, bf16[512,1536]{1,0:T(8,128)(2,1)} %wqkv_hbm.2, bf16[512,512]{1,0:T(8,128)(2,1)} %wproj_hbm.2, f32[1,512]{1,0:T(1,128)} %bitcast.25, ...), custom_call_target="tpu_custom_call" | custom-call | flops 3221225472 | bytes 7620672 | tf_op jit(solution)/shard_map/pallas_call | solution.py:459
  12.4 0.3 collective-permute-start.2
  12.7 2.1 %collective-permute-start.3 = (bf16[128,512]{1,0:T(8,128)(2,1)}, bf16[128,512]{1,0:T(8,128)(2,1)S(1)}, u32[]{:S(2)}, u32[]{:S(2)}) collective-permute-start(bf16[128,512]{1,0:T(8,128)(2,1)} %get-tuple-element.50), channel_id=1, source_target_pairs={{0,24},{8,0},{16,8},{24,16},{1,25},{9,1},{17,9},{25,17},{2,26},{10... | collective-permute-start | bytes 393224 | tf_op jit(solution)/shard_map/ppermute | solution.py:552
  14.8 0.1 copy.18
  14.9 0.1 reshape.52
  15.0 0.1 slice.10
  15.1 0.1 add_xor_fusion.routes_ref
  15.1 0.1 add_convert_fusion.info_ref
  15.2 0.0 collective-permute-done.in_next
  15.2 0.0 collective-permute-done.1.out_next
  15.2 0.0 copy-done.1
  15.3 0.0 copy-start
  15.3 1.0 %copy-done = bf16[512,512]{1,0:T(8,128)(2,1)S(1)} copy-done((bf16[512,512]{1,0:T(8,128)(2,1)S(1)}, bf16[512,512]{1,0:T(8,128)(2,1)}, u32[]{:S(2)}) %copy-start) | copy-done | bytes 524312
  16.3 5.0 %shard_map.155 = (bf16[512,1536]{1,0:T(8,128)(2,1)S(1)}, f32[4,128,512]{2,1,0:T(8,128)S(1)}, f32[4,128,256]{2,1,0:T(8,128)S(1)}, s32[8,512]{1,0:T(8,128)S(1)}, b...) custom-call(s32[2]{0:T(128)S(1)} %add_convert_fusion.info_ref, ...), custom_call_target="tpu_custom_call" | custom-call | flops 805306368 | bytes 11042888 | tf_op jit(solution)/shard_map/pallas_call | solution.py:459
  21.4 0.0 collective-permute-done.2.from_left_ref
  21.4 0.0 collective-permute-done.3.from_right_ref
  21.4 0.9 %collective-permute-start.6 = (bf16[2,512,512]{2,1,0:T(8,128)(2,1)S(1)}, bf16[2,512,512]{2,1,0:T(8,128)(2,1)S(1)}, u32[]{:S(2)}, u32[]{:S(2)}) collective-permute-start(bf16[2,512,512]{2,1,0:T(8,128)(2,1)S(1)} %get-tuple-element.67.refs_2_), channel_id=1, source_target_pairs={{0,16},{8,24},{16,0},{24,8},{1,17},{9,25},{17,1},{25,9},{2,18},{10... | collective-permute-start | bytes 3145736 | tf_op jit(solution)/shard_map/ppermute | solution.py:476
  22.3 0.3 collective-permute-start.7
  22.6 5.5 %shard_map.156 = (bf16[512,512]{1,0:T(8,128)(2,1)S(1)}, bf16[128,512]{1,0:T(8,128)(2,1)S(1)}, bf16[128,512]{1,0:T(8,128)(2,1)S(1)}, bf16[128,512]{1,0:T(8,128)(2...) custom-call(s32[2]{0:T(128)S(1)} %add_convert_fusion.info_ref, ...), custom_call_target="tpu_custom_call" | custom-call | flops 1073741824 | bytes 7620616 | tf_op jit(solution)/shard_map/pallas_call | solution.py:459
  28.1 2.4 %collective-permute-start.4 = (bf16[128,512]{1,0:T(8,128)(2,1)S(1)}, bf16[128,512]{1,0:T(8,128)(2,1)S(1)}, u32[]{:S(2)}, u32[]{:S(2)}) collective-permute-start(bf16[128,512]{1,0:T(8,128)(2,1)S(1)} %get-tuple-element.60), channel_id=1, source_target_pairs={{0,4},{1,5},{2,6},{3,7},{4,0},{5,1},{6,2},{7,3},{8,12},{9,13},{10,... | collective-permute-start | bytes 393224 | tf_op jit(solution)/shard_map/ppermute | solution.py:476
  30.5 4.0 %collective-permute-start.5 = (bf16[128,512]{1,0:T(8,128)(2,1)S(1)}, bf16[128,512]{1,0:T(8,128)(2,1)S(1)}, u32[]{:S(2)}, u32[]{:S(2)}) collective-permute-start(bf16[128,512]{1,0:T(8,128)(2,1)S(1)} %get-tuple-element.61), channel_id=1, source_target_pairs={{0,5},{1,4},{2,7},{3,6},{4,1},{5,0},{6,3},{7,2},{8,13},{9,12},{10,... | collective-permute-start | bytes 393224 | tf_op jit(solution)/shard_map/ppermute | solution.py:476
  34.5 9.7 %collective-permute-done.5.refs_1_ = bf16[128,512]{1,0:T(8,128)(2,1)S(1)} collective-permute-done((bf16[128,512]{1,0:T(8,128)(2,1)S(1)}, bf16[128,512]{1,0:T(8,128)(2,1)S(1)}, u32[]{:S(2)}, u32[]{:S(2)}) %collective-permute-start.5) | collective-permute-done | bytes 131104 | tf_op jit(solution)/shard_map/ppermute | solution.py:476
  44.2 3.1 %collective-permute-start.16 = (bf16[128,512]{1,0:T(8,128)(2,1)S(1)}, bf16[128,512]{1,0:T(8,128)(2,1)S(1)}, u32[]{:S(2)}, u32[]{:S(2)}) collective-permute-start(bf16[128,512]{1,0:T(8,128)(2,1)S(1)} %get-tuple-element.85), channel_id=1, source_target_pairs={{0,6},{1,7},{2,4},{3,5},{4,2},{5,3},{6,0},{7,1},{8,14},{9,15},{10,... | collective-permute-start | bytes 393224 | tf_op jit(solution)/shard_map/ppermute | solution.py:476
  47.4 0.7 collective-permute-start.17
  48.1 0.0 collective-permute-done.6.refs_3_
  48.1 0.0 collective-permute-done.7.refs_5_
  48.1 1.6 %shard_map.158 = (bf16[128,512]{1,0:T(8,128)(2,1)S(1)}, bf16[128,512]{1,0:T(8,128)(2,1)S(1)}) custom-call(bf16[128,512]{1,0:T(8,128)(2,1)S(1)} %collective-permute-done.4.refs_0_, bf16[128,512]{1,0:T(8,128)(2,1)S(1)} %collective-permute-done.5.refs_1_, bf16[2,512,512]{2,1,0:T(8,128)(2,1)S(1)} %get-tuple-element.67.refs_2_, ...), custom_call_target="tpu_custom_call" | custom-call | flops 1073741824 | bytes 4718592 | tf_op jit(solution)/shard_map/pallas_call | solution.py:459
  49.7 0.1 collective-permute-start.8
  49.7 1.1 %collective-permute-start.10 = (bf16[128,512]{1,0:T(8,128)(2,1)S(1)}, bf16[128,512]{1,0:T(8,128)(2,1)S(1)}, u32[]{:S(2)}, u32[]{:S(2)}) collective-permute-start(bf16[128,512]{1,0:T(8,128)(2,1)S(1)} %get-tuple-element.79), channel_id=1, source_target_pairs={{0,2},{1,3},{2,0},{3,1},{4,6},{5,7},{6,4},{7,5},{8,10},{9,11},{10,... | collective-permute-start | bytes 393224 | tf_op jit(solution)/shard_map/ppermute | solution.py:476
  50.8 1.0 %collective-permute-start.11 = (bf16[128,512]{1,0:T(8,128)(2,1)S(1)}, bf16[128,512]{1,0:T(8,128)(2,1)S(1)}, u32[]{:S(2)}, u32[]{:S(2)}) collective-permute-start(bf16[128,512]{1,0:T(8,128)(2,1)S(1)} %get-tuple-element.80), channel_id=1, source_target_pairs={{0,3},{1,2},{2,1},{3,0},{4,7},{5,6},{6,5},{7,4},{8,11},{9,10},{10,... | collective-permute-start | bytes 393224 | tf_op jit(solution)/shard_map/ppermute | solution.py:476
  51.9 0.0 collective-permute-done.16.refs_0_
  51.9 1.7 %collective-permute-start.14 = (bf16[128,512]{1,0:T(8,128)(2,1)S(1)}, bf16[128,512]{1,0:T(8,128)(2,1)S(1)}, u32[]{:S(2)}, u32[]{:S(2)}) collective-permute-start(bf16[128,512]{1,0:T(8,128)(2,1)S(1)} %get-tuple-element.83), channel_id=1, source_target_pairs={{0,4},{1,5},{2,6},{3,7},{4,0},{5,1},{6,2},{7,3},{8,12},{9,13},{10,... | collective-permute-start | bytes 393224 | tf_op jit(solution)/shard_map/ppermute | solution.py:476
  53.5 0.7 collective-permute-done.17.refs_1_
  54.3 4.1 %collective-permute-start.15 = (bf16[128,512]{1,0:T(8,128)(2,1)S(1)}, bf16[128,512]{1,0:T(8,128)(2,1)S(1)}, u32[]{:S(2)}, u32[]{:S(2)}) collective-permute-start(bf16[128,512]{1,0:T(8,128)(2,1)S(1)} %get-tuple-element.84), channel_id=1, source_target_pairs={{0,5},{1,4},{2,7},{3,6},{4,1},{5,0},{6,3},{7,2},{8,13},{9,12},{10,... | collective-permute-start | bytes 393224 | tf_op jit(solution)/shard_map/ppermute | solution.py:476
  58.4 1.6 %shard_map.161 = (bf16[128,512]{1,0:T(8,128)(2,1)S(1)}, bf16[128,512]{1,0:T(8,128)(2,1)S(1)}) custom-call(bf16[128,512]{1,0:T(8,128)(2,1)S(1)} %collective-permute-done.16.refs_0_, bf16[128,512]{1,0:T(8,128)(2,1)S(1)} %collective-permute-done.17.refs_1_, bf16[2,512,512]{2,1,0:T(8,128)(2,1)S(1)} %get-tuple-element.67.refs_2_, ...), custom_call_target="tpu_custom_call" | custom-call | flops 1073741824 | bytes 4718592 | tf_op jit(solution)/shard_map/pallas_call | solution.py:459
  60.0 0.9 %collective-permute-start.18 = (bf16[128,512]{1,0:T(8,128)(2,1)S(1)}, bf16[128,512]{1,0:T(8,128)(2,1)S(1)}, u32[]{:S(2)}, u32[]{:S(2)}) collective-permute-start(bf16[128,512]{1,0:T(8,128)(2,1)S(1)} %get-tuple-element.87), channel_id=1, source_target_pairs={{0,6},{1,7},{2,4},{3,5},{4,2},{5,3},{6,0},{7,1},{8,14},{9,15},{10,... | collective-permute-start | bytes 393224 | tf_op jit(solution)/shard_map/ppermute | solution.py:476
  60.8 1.6 %shard_map.159 = (bf16[128,512]{1,0:T(8,128)(2,1)S(1)}, bf16[128,512]{1,0:T(8,128)(2,1)S(1)}) custom-call(bf16[128,512]{1,0:T(8,128)(2,1)S(1)} %get-tuple-element.75.refs_0_, bf16[128,512]{1,0:T(8,128)(2,1)S(1)} %collective-permute-done.8.refs_1_, bf16[2,512,512]{2,1,0:T(8,128)(2,1)S(1)} %get-tuple-element.67.refs_2_, ...), custom_call_target="tpu_custom_call" | custom-call | flops 1073741824 | bytes 4718592 | tf_op jit(solution)/shard_map/pallas_call | solution.py:459
  62.5 2.5 %collective-permute-start.19 = (bf16[128,512]{1,0:T(8,128)(2,1)S(1)}, bf16[128,512]{1,0:T(8,128)(2,1)S(1)}, u32[]{:S(2)}, u32[]{:S(2)}) collective-permute-start(bf16[128,512]{1,0:T(8,128)(2,1)S(1)} %get-tuple-element.88), channel_id=1, source_target_pairs={{0,7},{1,6},{2,5},{3,4},{4,3},{5,2},{6,1},{7,0},{8,15},{9,14},{10,... | collective-permute-start | bytes 393224 | tf_op jit(solution)/shard_map/ppermute | solution.py:476
  64.9 0.5 collective-permute-start.9
  65.4 1.6 %shard_map.160 = (bf16[128,512]{1,0:T(8,128)(2,1)S(1)}, bf16[128,512]{1,0:T(8,128)(2,1)S(1)}) custom-call(bf16[128,512]{1,0:T(8,128)(2,1)S(1)} %collective-permute-done.10.refs_0_, bf16[128,512]{1,0:T(8,128)(2,1)S(1)} %collective-permute-done.11.refs_1_, bf16[2,512,512]{2,1,0:T(8,128)(2,1)S(1)} %get-tuple-element.67.refs_2_, ...), custom_call_target="tpu_custom_call" | custom-call | flops 1073741824 | bytes 4718592 | tf_op jit(solution)/shard_map/pallas_call | solution.py:459
  67.0 0.1 collective-permute-start.12
  67.1 7.3 %collective-permute-done.15.rest_5_ = bf16[128,512]{1,0:T(8,128)(2,1)S(1)} collective-permute-done((bf16[128,512]{1,0:T(8,128)(2,1)S(1)}, bf16[128,512]{1,0:T(8,128)(2,1)S(1)}, u32[]{:S(2)}, u32[]{:S(2)}) %collective-permute-start.15) | collective-permute-done | bytes 131104 | tf_op jit(solution)/shard_map/ppermute | solution.py:476
  74.4 0.4 shard_map.157.slot_col_ref
  74.8 1.0 %collective-permute-done.12.rest_2_ = bf16[128,512]{1,0:T(8,128)(2,1)S(1)} collective-permute-done((bf16[128,512]{1,0:T(8,128)(2,1)S(1)}, bf16[128,512]{1,0:T(8,128)(2,1)S(1)}, u32[]{:S(2)}, u32[]{:S(2)}) %collective-permute-start.12) | collective-permute-done | bytes 131104 | tf_op jit(solution)/shard_map/ppermute | solution.py:476
  75.8 3.8 %collective-permute-done.13.rest_3_ = bf16[128,512]{1,0:T(8,128)(2,1)S(1)} collective-permute-done((bf16[128,512]{1,0:T(8,128)(2,1)S(1)}, bf16[128,512]{1,0:T(8,128)(2,1)S(1)}, u32[]{:S(2)}, u32[]{:S(2)}) %collective-permute-start.13) | collective-permute-done | bytes 131104 | tf_op jit(solution)/shard_map/ppermute | solution.py:476
  79.6 1.9 %shard_map.162 = bf16[512,512]{1,0:T(8,128)(2,1)} custom-call(bf16[512,512]{1,0:T(8,128)(2,1)S(1)} %get-tuple-element.59.third_ref, s32[512,128]{1,0:T(8,128)S(1)} %shard_map.157.slot_col_ref, f32[1,512]{1,0:T(1,128)S(1)} %bitcast.22, bf16[128,512]{1,0:T(8,128)(2,1)S(1)} %get-tuple-element.77.rest_0_, bf16[128,512]{1,0:T(8,128)(2,1)S(1)} %collective-permute-done.9.rest_1_, ...), custom_call_target="tpu_custom_call" | custom-call | flops 536870912 | bytes 2361344 | tf_op jit(solution)/shard_map/pallas_call | solution.py:459
  (25 shorter events, 0.1 us)
Async XLA Ops:
  0.0 15.2 %collective-permute-start = (bf16[512,512]{1,0:T(8,128)(2,1)}, bf16[512,512]{1,0:T(8,128)(2,1)S(1)}, u32[]{:S(2)}, u32[]{:S(2)}) collective-permute-start(bf16[512,512]{1,0:T(8,128)(2,1)} %bitcast.16), channel_id=1, source_target_pairs={{0,8},{8,0},{16,24},{24,16},{1,9},{9,1},{17,25},{25,17},{2,10},{10... | collective-permute-start | bytes 1572872 | tf_op jit(solution)/shard_map/ppermute | solution.py:476
  2.0 13.2 %collective-permute-start.1 = (bf16[512,512]{1,0:T(8,128)(2,1)}, bf16[512,512]{1,0:T(8,128)(2,1)}, u32[]{:S(2)}, u32[]{:S(2)}) collective-permute-start(bf16[512,512]{1,0:T(8,128)(2,1)} %bitcast.18), channel_id=1, source_target_pairs={{0,16},{8,24},{16,0},{24,8},{1,17},{9,25},{17,1},{25,9},{2,18},{10... | collective-permute-start | bytes 1572872 | tf_op jit(solution)/shard_map/ppermute | solution.py:476
  3.3 11.5 %copy-start.8 = (s32[1,1,32,16,1]{2,4,3,1,0:T(1,128)S(1)}, s32[1,1,32,16,1]{2,4,3,1,0:T(1,128)}, u32[]{:S(2)}) copy-start(s32[1,1,32,16,1]{2,4,3,1,0:T(1,128)} %param.17) | copy-start | bytes 6148
  3.3 11.9 %copy-start.1 = (bf16[512,1536]{1,0:T(8,128)(2,1)S(1)}, bf16[512,1536]{1,0:T(8,128)(2,1)}, u32[]{:S(2)}) copy-start(bf16[512,1536]{1,0:T(8,128)(2,1)} %wqkv_hbm.3) | copy-start | bytes 4718596
  3.3 12.0 %copy-start.3 = (bf16[1,512,512]{2,1,0:T(8,128)(2,1)S(1)}, bf16[1,512,512]{2,1,0:T(8,128)(2,1)}, u32[]{:S(2)}) copy-start(bf16[1,512,512]{2,1,0:T(8,128)(2,1)} %param.29) | copy-start | bytes 1572868
  3.3 12.0 %copy-start.4 = (bf16[1,512,512]{2,1,0:T(8,128)(2,1)S(1)}, bf16[1,512,512]{2,1,0:T(8,128)(2,1)}, u32[]{:S(2)}) copy-start(bf16[1,512,512]{2,1,0:T(8,128)(2,1)} %param.30) | copy-start | bytes 1572868
  3.3 12.0 %copy-start.5 = (f32[225,16]{0,1:T(8,128)S(1)}, f32[225,16]{0,1:T(8,128)}, u32[]{:S(2)}) copy-start(f32[225,16]{0,1:T(8,128)} %param.27) | copy-start | bytes 43204
  12.4 9.0 %collective-permute-start.2 = (bf16[128,512]{1,0:T(8,128)(2,1)}, bf16[128,512]{1,0:T(8,128)(2,1)S(1)}, u32[]{:S(2)}, u32[]{:S(2)}) collective-permute-start(bf16[128,512]{1,0:T(8,128)(2,1)} %get-tuple-element.49), channel_id=1, source_target_pairs={{0,8},{8,16},{16,24},{24,0},{1,9},{9,17},{17,25},{25,1},{2,10},{10... | collective-permute-start | bytes 393224 | tf_op jit(solution)/shard_map/ppermute | solution.py:553
  12.7 8.7 %collective-permute-start.3 = (bf16[128,512]{1,0:T(8,128)(2,1)}, bf16[128,512]{1,0:T(8,128)(2,1)S(1)}, u32[]{:S(2)}, u32[]{:S(2)}) collective-permute-start(bf16[128,512]{1,0:T(8,128)(2,1)} %get-tuple-element.50), channel_id=1, source_target_pairs={{0,24},{8,0},{16,8},{24,16},{1,25},{9,1},{17,9},{25,17},{2,26},{10... | collective-permute-start | bytes 393224 | tf_op jit(solution)/shard_map/ppermute | solution.py:552
  15.3 1.0 %copy-start = (bf16[512,512]{1,0:T(8,128)(2,1)S(1)}, bf16[512,512]{1,0:T(8,128)(2,1)}, u32[]{:S(2)}) copy-start(bf16[512,512]{1,0:T(8,128)(2,1)} %get-tuple-element.47.x_any.x_ref) | copy-start | bytes 1572868
  16.3 6.3 %copy-start.2 = (bf16[512,512]{1,0:T(8,128)(2,1)S(1)}, bf16[512,512]{1,0:T(8,128)(2,1)}, u32[]{:S(2)}) copy-start(bf16[512,512]{1,0:T(8,128)(2,1)} %wproj_hbm.3) | copy-start | bytes 1572868
  16.3 6.3 %copy-start.6 = (f32[512]{0:T(512)S(1)}, f32[512]{0:T(512)}, u32[]{:S(2)}) copy-start(f32[512]{0:T(512)} %param.28) | copy-start | bytes 6148
  21.4 26.7 %collective-permute-start.6 = (bf16[2,512,512]{2,1,0:T(8,128)(2,1)S(1)}, bf16[2,512,512]{2,1,0:T(8,128)(2,1)S(1)}, u32[]{:S(2)}, u32[]{:S(2)}) collective-permute-start(bf16[2,512,512]{2,1,0:T(8,128)(2,1)S(1)} %get-tuple-element.67.refs_2_), channel_id=1, source_target_pairs={{0,16},{8,24},{16,0},{24,8},{1,17},{9,25},{17,1},{25,9},{2,18},{10... | collective-permute-start | bytes 3145736 | tf_op jit(solution)/shard_map/ppermute | solution.py:476
  22.3 25.8 %collective-permute-start.7 = (bf16[2,512,512]{2,1,0:T(8,128)(2,1)S(1)}, bf16[2,512,512]{2,1,0:T(8,128)(2,1)S(1)}, u32[]{:S(2)}, u32[]{:S(2)}) collective-permute-start(bf16[2,512,512]{2,1,0:T(8,128)(2,1)S(1)} %get-tuple-element.68.refs_4_), channel_id=1, source_target_pairs={{0,8},{8,0},{16,24},{24,16},{1,9},{9,1},{17,25},{25,17},{2,10},{10... | collective-permute-start | bytes 3145736 | tf_op jit(solution)/shard_map/ppermute | solution.py:476
  28.1 6.4 %collective-permute-start.4 = (bf16[128,512]{1,0:T(8,128)(2,1)S(1)}, bf16[128,512]{1,0:T(8,128)(2,1)S(1)}, u32[]{:S(2)}, u32[]{:S(2)}) collective-permute-start(bf16[128,512]{1,0:T(8,128)(2,1)S(1)} %get-tuple-element.60), channel_id=1, source_target_pairs={{0,4},{1,5},{2,6},{3,7},{4,0},{5,1},{6,2},{7,3},{8,12},{9,13},{10,... | collective-permute-start | bytes 393224 | tf_op jit(solution)/shard_map/ppermute | solution.py:476
  30.5 13.8 %collective-permute-start.5 = (bf16[128,512]{1,0:T(8,128)(2,1)S(1)}, bf16[128,512]{1,0:T(8,128)(2,1)S(1)}, u32[]{:S(2)}, u32[]{:S(2)}) collective-permute-start(bf16[128,512]{1,0:T(8,128)(2,1)S(1)} %get-tuple-element.61), channel_id=1, source_target_pairs={{0,5},{1,4},{2,7},{3,6},{4,1},{5,0},{6,3},{7,2},{8,13},{9,12},{10,... | collective-permute-start | bytes 393224 | tf_op jit(solution)/shard_map/ppermute | solution.py:476
  44.2 7.6 %collective-permute-start.16 = (bf16[128,512]{1,0:T(8,128)(2,1)S(1)}, bf16[128,512]{1,0:T(8,128)(2,1)S(1)}, u32[]{:S(2)}, u32[]{:S(2)}) collective-permute-start(bf16[128,512]{1,0:T(8,128)(2,1)S(1)} %get-tuple-element.85), channel_id=1, source_target_pairs={{0,6},{1,7},{2,4},{3,5},{4,2},{5,3},{6,0},{7,1},{8,14},{9,15},{10,... | collective-permute-start | bytes 393224 | tf_op jit(solution)/shard_map/ppermute | solution.py:476
  47.4 6.9 %collective-permute-start.17 = (bf16[128,512]{1,0:T(8,128)(2,1)S(1)}, bf16[128,512]{1,0:T(8,128)(2,1)S(1)}, u32[]{:S(2)}, u32[]{:S(2)}) collective-permute-start(bf16[128,512]{1,0:T(8,128)(2,1)S(1)} %get-tuple-element.86), channel_id=1, source_target_pairs={{0,7},{1,6},{2,5},{3,4},{4,3},{5,2},{6,1},{7,0},{8,15},{9,14},{10,... | collective-permute-start | bytes 393224 | tf_op jit(solution)/shard_map/ppermute | solution.py:476
  49.7 10.3 %collective-permute-start.8 = (bf16[128,512]{1,0:T(8,128)(2,1)S(1)}, bf16[128,512]{1,0:T(8,128)(2,1)S(1)}, u32[]{:S(2)}, u32[]{:S(2)}) collective-permute-start(bf16[128,512]{1,0:T(8,128)(2,1)S(1)} %get-tuple-element.76), channel_id=1, source_target_pairs={{0,1},{1,0},{2,3},{3,2},{4,5},{5,4},{6,7},{7,6},{8,9},{9,8},{10,11... | collective-permute-start | bytes 393224 | tf_op jit(solution)/shard_map/ppermute | solution.py:476
  49.7 12.7 %collective-permute-start.10 = (bf16[128,512]{1,0:T(8,128)(2,1)S(1)}, bf16[128,512]{1,0:T(8,128)(2,1)S(1)}, u32[]{:S(2)}, u32[]{:S(2)}) collective-permute-start(bf16[128,512]{1,0:T(8,128)(2,1)S(1)} %get-tuple-element.79), channel_id=1, source_target_pairs={{0,2},{1,3},{2,0},{3,1},{4,6},{5,7},{6,4},{7,5},{8,10},{9,11},{10,... | collective-permute-start | bytes 393224 | tf_op jit(solution)/shard_map/ppermute | solution.py:476
  50.8 14.1 %collective-permute-start.11 = (bf16[128,512]{1,0:T(8,128)(2,1)S(1)}, bf16[128,512]{1,0:T(8,128)(2,1)S(1)}, u32[]{:S(2)}, u32[]{:S(2)}) collective-permute-start(bf16[128,512]{1,0:T(8,128)(2,1)S(1)} %get-tuple-element.80), channel_id=1, source_target_pairs={{0,3},{1,2},{2,1},{3,0},{4,7},{5,6},{6,5},{7,4},{8,11},{9,10},{10,... | collective-permute-start | bytes 393224 | tf_op jit(solution)/shard_map/ppermute | solution.py:476
  51.9 15.1 %collective-permute-start.14 = (bf16[128,512]{1,0:T(8,128)(2,1)S(1)}, bf16[128,512]{1,0:T(8,128)(2,1)S(1)}, u32[]{:S(2)}, u32[]{:S(2)}) collective-permute-start(bf16[128,512]{1,0:T(8,128)(2,1)S(1)} %get-tuple-element.83), channel_id=1, source_target_pairs={{0,4},{1,5},{2,6},{3,7},{4,0},{5,1},{6,2},{7,3},{8,12},{9,13},{10,... | collective-permute-start | bytes 393224 | tf_op jit(solution)/shard_map/ppermute | solution.py:476
  54.3 20.1 %collective-permute-start.15 = (bf16[128,512]{1,0:T(8,128)(2,1)S(1)}, bf16[128,512]{1,0:T(8,128)(2,1)S(1)}, u32[]{:S(2)}, u32[]{:S(2)}) collective-permute-start(bf16[128,512]{1,0:T(8,128)(2,1)S(1)} %get-tuple-element.84), channel_id=1, source_target_pairs={{0,5},{1,4},{2,7},{3,6},{4,1},{5,0},{6,3},{7,2},{8,13},{9,12},{10,... | collective-permute-start | bytes 393224 | tf_op jit(solution)/shard_map/ppermute | solution.py:476
  60.0 14.8 %collective-permute-start.18 = (bf16[128,512]{1,0:T(8,128)(2,1)S(1)}, bf16[128,512]{1,0:T(8,128)(2,1)S(1)}, u32[]{:S(2)}, u32[]{:S(2)}) collective-permute-start(bf16[128,512]{1,0:T(8,128)(2,1)S(1)} %get-tuple-element.87), channel_id=1, source_target_pairs={{0,6},{1,7},{2,4},{3,5},{4,2},{5,3},{6,0},{7,1},{8,14},{9,15},{10,... | collective-permute-start | bytes 393224 | tf_op jit(solution)/shard_map/ppermute | solution.py:476
  62.5 12.3 %collective-permute-start.19 = (bf16[128,512]{1,0:T(8,128)(2,1)S(1)}, bf16[128,512]{1,0:T(8,128)(2,1)S(1)}, u32[]{:S(2)}, u32[]{:S(2)}) collective-permute-start(bf16[128,512]{1,0:T(8,128)(2,1)S(1)} %get-tuple-element.88), channel_id=1, source_target_pairs={{0,7},{1,6},{2,5},{3,4},{4,3},{5,2},{6,1},{7,0},{8,15},{9,14},{10,... | collective-permute-start | bytes 393224 | tf_op jit(solution)/shard_map/ppermute | solution.py:476
  64.9 14.7 %copy-start.7 = (f32[512]{0:T(512)S(1)}, f32[512]{0:T(512)}, u32[]{:S(2)}) copy-start(f32[512]{0:T(512)} %param.31) | copy-start | bytes 6148
  64.9 9.9 %collective-permute-start.9 = (bf16[128,512]{1,0:T(8,128)(2,1)S(1)}, bf16[128,512]{1,0:T(8,128)(2,1)S(1)}, u32[]{:S(2)}, u32[]{:S(2)}) collective-permute-start(bf16[128,512]{1,0:T(8,128)(2,1)S(1)} %get-tuple-element.78), channel_id=1, source_target_pairs={{0,1},{1,0},{2,3},{3,2},{4,5},{5,4},{6,7},{7,6},{8,9},{9,8},{10,11... | collective-permute-start | bytes 393224 | tf_op jit(solution)/shard_map/ppermute | solution.py:476
  67.0 8.8 %collective-permute-start.12 = (bf16[128,512]{1,0:T(8,128)(2,1)S(1)}, bf16[128,512]{1,0:T(8,128)(2,1)S(1)}, u32[]{:S(2)}, u32[]{:S(2)}) collective-permute-start(bf16[128,512]{1,0:T(8,128)(2,1)S(1)} %get-tuple-element.81), channel_id=1, source_target_pairs={{0,2},{1,3},{2,0},{3,1},{4,6},{5,7},{6,4},{7,5},{8,10},{9,11},{10,... | collective-permute-start | bytes 393224 | tf_op jit(solution)/shard_map/ppermute | solution.py:476
  74.4 5.2 %collective-permute-start.13 = (bf16[128,512]{1,0:T(8,128)(2,1)S(1)}, bf16[128,512]{1,0:T(8,128)(2,1)S(1)}, u32[]{:S(2)}, u32[]{:S(2)}) collective-permute-start(bf16[128,512]{1,0:T(8,128)(2,1)S(1)} %get-tuple-element.82), channel_id=1, source_target_pairs={{0,3},{1,2},{2,1},{3,0},{4,7},{5,6},{6,5},{7,4},{8,11},{9,10},{10,... | collective-permute-start | bytes 393224 | tf_op jit(solution)/shard_map/ppermute | solution.py:476

commit v3 on v2

--- a/solution.py
+++ b/solution.py
@@ -116,6 +116,14 @@
     return jnp.where(
         lax.div(iota(shape, 0), keys) == lax.div(iota(shape, 1), LANES // parts), 1.0, 0.0
     ).astype(BF)
+
+
+def spread(tops):
+    lane_head = lax.div(iota((tops[0].shape[0], LANES), 1), LANES // len(tops))
+    spread_out = tops[-1]
+    for h in range(len(tops) - 2, -1, -1):
+        spread_out = jnp.where(lane_head == h, tops[h], spread_out)
+    return spread_out
 
 
 def by_head(block, masks):
@@ -241,6 +249,12 @@
     slot_col_ref[...] = jnp.broadcast_to(column, slot_col_ref.shape).astype(I32)
 
 
+def stack_kernel(in_first, in_second, out_first, out_second, in_pair, out_pair, sems):
+    places = (in_pair.at[0], in_pair.at[1], out_pair.at[0], out_pair.at[1])
+    for copy in fetch(sems, *zip((in_first, in_second, out_first, out_second), places)):
+        copy.wait()
+
+
 def middle_kernel(
     band_width,
     experts,
@@ -250,24 +264,23 @@
     routes_ref,
     table_hbm,
     wqkv_hbm,
-    in_hbm,
-    in_next,
-    out_hbm,
-    out_next,
     qkv_ref,
-    bias_ref,
+    sums_ref,
+    weights_ref,
+    tops_ref,
     bias_halo_ref,
     slot_row_ref,
     wqkv_ref,
-    in_pair,
-    out_pair,
     table_ref,
     x_ref,
     sems,
     tab_ref,
+    bias_ref,
 ):
     rows, width = x_ref.shape
     head_dim = width // HEADS
+    strip = WIN * band_width
+    parts = LANES // head_dim
     copies = fetch(
         sems,
         (table_hbm, table_ref),
@@ -288,13 +301,6 @@
     slot_row_ref[...] = jnp.broadcast_to(slot, slot_row_ref.shape).astype(I32)
     copies[1].wait()
     copies[2].wait()
-    copies = fetch(
-        sems.at[3:],
-        (in_hbm, in_pair.at[0]),
-        (in_next, in_pair.at[1]),
-        (out_hbm, out_pair.at[0]),
-        (out_next, out_pair.at[1]),
-    )
     x = x_ref[...]
     for part in range(3):
         cols = slice(part * width, (part + 1) * width)
@@ -302,8 +308,32 @@
         if part == 0:
             product = product * (LOG2E * head_dim**-0.5)
         qkv_ref[:, cols] = product.astype(BF)
-    for copy in copies:
-        copy.wait()
+    masks = head_masks(parts)
+    ones = sum_columns(strip, parts)
+    p, q = iota((strip, strip), 0), iota((strip, strip), 1)
+    turned = HALF * band_width
+    apart = jnp.where((p < turned) != (q < turned), MASKED, 0.0)
+    groups = rows // strip
+    for t in range(width // LANES):
+        lanes, lanes_k, lanes_v = (
+            slice(part * width + t * LANES, part * width + (t + 1) * LANES) for part in range(3)
+        )
+        for g in range(groups):
+            tokens = slice(g * strip, (g + 1) * strip)
+            keys = by_head(qkv_ref[tokens, lanes_k], masks)
+            scores = dot(qkv_ref[tokens, lanes], keys, NT) + bias_ref[t]
+            probs, tops = [], []
+            for h in range(parts):
+                s = scores[:, h * strip : (h + 1) * strip]
+                if g == groups - 1:
+                    s = s + apart
+                tops.append(jnp.max(s, axis=-1, keepdims=True))
+                probs.append(jnp.exp2(s - tops[h]).astype(BF))
+            values = jnp.concatenate([by_head(qkv_ref[tokens, lanes_v], masks), ones], axis=1)
+            both = dot(jnp.concatenate(probs, axis=1), values)
+            sums_ref[tokens, lanes] = both[:, :LANES]
+            weights_ref[tokens, lanes] = both[:, LANES:]
+            tops_ref[tokens, lanes] = spread(tops)
 
 
 def shifted_kernel(
@@ -315,7 +345,9 @@
     from_left_ref,
     from_right_ref,
     wqkv_ref,
-    bias_ref,
+    sums_ref,
+    weights_ref,
+    tops_ref,
     bias_halo_ref,
     slot_row_ref,
     wproj_hbm,
@@ -341,62 +373,38 @@
     )
     halo_kv[...] = dot(arrived, wqkv_ref[:, width:]).astype(BF)
     masks = head_masks(parts)
-    ones = jnp.concatenate([sum_columns(strip, parts), sum_columns(halo, parts)], axis=0)
-    p, q = iota((strip, strip), 0), iota((strip, strip), 1)
-    turned = HALF * band_width
-    apart = jnp.where((p < turned) != (q < turned), MASKED, 0.0)
+    ones = sum_columns(halo, parts)
     row_p, _, row_q, _, right, front = halo_places(band_width)
     edge = jnp.where(right, info_ref[1], info_ref[0]) > 0
     crossed = (row_p < HALF) != (row_q < HALF)
     apart_halo = jnp.where(jnp.logical_and(crossed, jnp.logical_not(edge)), MASKED, 0.0)
     wide = 2 * halo
-
-    def tile_step(t, carry):
-        lanes = pl.ds(pl.multiple_of(t * LANES, LANES), LANES)
-        lanes_k = pl.ds(pl.multiple_of(width + t * LANES, LANES), LANES)
-        lanes_v = pl.ds(pl.multiple_of(2 * width + t * LANES, LANES), LANES)
-        bias_tile = bias_ref.at[t]
-        bias_halo_tile = bias_halo_ref.at[t]
+    for t in range(width // LANES):
+        lanes, lanes_k = (
+            slice(part * width + t * LANES, part * width + (t + 1) * LANES) for part in range(2)
+        )
         for g in range(groups):
             tokens = slice(g * strip, (g + 1) * strip)
             outside = slice(g * halo, (g + 1) * halo)
-            queries = qkv_ref[tokens, lanes]
-            scores = dot(queries, by_head(qkv_ref[tokens, lanes_k], masks), NT)
-            scores = scores + bias_tile[...]
-            scores_halo = dot(queries, by_head(halo_kv[outside, lanes], masks), NT)
-            scores_halo = scores_halo + bias_halo_tile[...]
-            probs, probs_halo = [], []
+            keys = by_head(halo_kv[outside, lanes], masks)
+            scores = dot(qkv_ref[tokens, lanes], keys, NT) + bias_halo_ref[t]
+            probs, tops = [], []
             for pair in range(parts // 2):
-                s_halo = scores_halo[:, pair * wide : (pair + 1) * wide]
+                s = scores[:, pair * wide : (pair + 1) * wide]
                 if g == groups - 1:
-                    s_halo = s_halo + apart_halo
-                tops = []
-                for k in range(2):
-                    h = 2 * pair + k
-                    s = scores[:, h * strip : (h + 1) * strip]
-                    if g == groups - 1:
-                        s = s + apart
-                    mine = front if k == 0 else jnp.logical_not(front)
-                    top = jnp.max(
-                        jnp.maximum(s, jnp.where(mine, s_halo, CLOSED)), axis=-1, keepdims=True
-                    )
-                    tops.append(top)
-                    probs.append(jnp.exp2(s - top).astype(BF))
-                probs_halo.append(
-                    jnp.exp2(s_halo - jnp.where(front, tops[0], tops[1])).astype(BF)
-                )
-            values = jnp.concatenate(
-                [by_head(qkv_ref[tokens, lanes_v], masks), by_head(halo_kv[outside, lanes_k], masks)],
-                axis=0,
-            )
-            both = dot(
-                jnp.concatenate(probs + probs_halo, axis=1),
-                jnp.concatenate([values, ones], axis=1),
-            )
-            heads[tokens, lanes] = (both[:, :LANES] / both[:, LANES:]).astype(BF)
-        return carry
-
-    lax.fori_loop(0, width // LANES, tile_step, 0, unroll=True)
+                    s = s + apart_halo
+                first = jnp.max(jnp.where(front, s, CLOSED), axis=-1, keepdims=True)
+                second = jnp.max(jnp.where(front, CLOSED, s), axis=-1, keepdims=True)
+                tops += [first, second]
+                probs.append(jnp.exp2(s - jnp.where(front, first, second)).astype(BF))
+            values = jnp.concatenate([by_head(halo_kv[outside, lanes_k], masks), ones], axis=1)
+            both = dot(jnp.concatenate(probs, axis=1), values)
+            own_top, halo_top = tops_ref[tokens, lanes], spread(tops)
+            top = jnp.maximum(own_top, halo_top)
+            own, other = jnp.exp2(own_top - top), jnp.exp2(halo_top - top)
+            total = sums_ref[tokens, lanes] * own + both[:, :LANES] * other
+            weight = weights_ref[tokens, lanes] * own + both[:, LANES:] * other
+            heads[tokens, lanes] = (total / weight).astype(BF)
     for copy in copies:
         copy.wait()
     projected = dot(heads[...], wproj_ref[...])
@@ -462,7 +470,7 @@
         in_specs=[pl.BlockSpec(memory_space=spaces[p]) for p in places],
         out_specs=[pl.BlockSpec(memory_space=pltpu.VMEM)] * len(outs),
         scratch_shapes=list(scratch),
-        compiler_params=pltpu.CompilerParams(vmem_limit_bytes=limit << 20),
+        compiler_params=pltpu.CompilerParams(vmem_limit_bytes=int(limit * 2**20)),
         cost_estimate=pl.CostEstimate(flops=flops, bytes_accessed=size, transcendentals=0),
     )(*ins)
     return list(results)
@@ -551,16 +559,16 @@
     ring = range(band_count)
     from_right = lax.ppermute(to_left, "band", [(i, (i - 1) % band_count) for i in ring])
     from_left = lax.ppermute(to_right, "band", [(i, (i + 1) % band_count) for i in ring])
-    qkv, bias, bias_halo, slot_row, wqkv, in_own, out_own = call(
+    qkv, *own_heads, bias_halo, slot_row, wqkv = call(
         functools.partial(middle_kernel, band_width, experts, capacity),
         [
             shape_of(rows, 3 * width),
-            shape_of(tiles, strip, wide, dtype=F32),
+            shape_of(rows, width, dtype=F32),
+            shape_of(rows, width, dtype=F32),
+            shape_of(rows, width, dtype=F32),
             shape_of(tiles, strip, wide_halo, dtype=F32),
             shape_of(8, rows, dtype=I32),
             shape_of(width, 3 * width),
-            shape_of(2, *expert_in.shape[1:]),
-            shape_of(2, *expert_out.shape[1:]),
         ],
         [
             info,
@@ -568,22 +576,28 @@
             route_row,
             table_shifted.T,
             qkv_shifted,
-            expert_in[0],
-            in_next,
-            expert_out[0],
-            out_next,
-        ],
-        "savhhhaha",
+        ],
+        "savhh",
         [
             pltpu.VMEM(table_shifted.shape[::-1], F32),
             pltpu.VMEM((rows, width), BF),
-            pltpu.SemaphoreType.DMA((7,)),
+            pltpu.SemaphoreType.DMA((3,)),
             pltpu.VMEM((HEADS, 2 * LANES), F32),
-        ],
+            pltpu.VMEM((tiles, strip, wide), F32),
+        ],
+        limit=46.5,
         flops=2 * rows * width * 3 * width,
     )
-    from_left, from_right, in_own, out_own = lax.optimization_barrier(
-        (from_left, from_right, in_own, out_own)
+    from_left, from_right, bias_halo, in_next, out_next = lax.optimization_barrier(
+        (from_left, from_right, bias_halo, in_next, out_next)
+    )
+    in_own, out_own = call(
+        stack_kernel,
+        [shape_of(2, *expert_in.shape[1:]), shape_of(2, *expert_out.shape[1:])],
+        [expert_in[0], in_next, expert_out[0], out_next],
+        "vvvv",
+        [pltpu.SemaphoreType.DMA((4,))],
+        limit=8,
     )
     in_far = swap(in_own, "band", 2)
     out_far = swap(out_own, "band", 1)
@@ -597,13 +611,13 @@
             from_left,
             from_right,
             wqkv,
-            bias,
+            *own_heads,
             bias_halo,
             slot_row,
             proj_shifted,
             gain_shifted.reshape(1, width),
         ],
-        "svvvvvvvvhh",
+        "svvvvvvvvvvhh",
         [
             pltpu.VMEM((2 * sent, 2 * width), BF),
             pltpu.VMEM((rows, width), BF),

time: 82 us -> 80.6 us (0.983)
  starting transfers between devices: 29 us -> 27.7 us
    ppermute x18, starting transfers between devices: 26.6 us -> 25.2 us  [swap(): lax.ppermute(block, axis, [(i, i ^ bits) for i in range(lax.axis_size(axi...]
    pallas_call x9 -> x10, Pallas kernels: 28.3 us -> 28.5 us  [call(): pl.pallas_call(kernel, out_shape=outs, in_specs=[pl.BlockSpec(memory_spac...]
  transfers between devices with their start and end apart: 20 -> 20, of which waited for: 5 -> 5; matrix products, arithmetic and copies ran while one was open for 0% -> 0% of each run, Pallas kernels for 32% -> 33%
where the time goes in v3:
time: 80.6 us; the launch traced here: 80.3 us
  Pallas kernels  28.5 us (35%)
  starting transfers between devices  27.7 us (34%)
  waiting for transfers between devices  21.9 us (27%)
  local copies, waits for them, and re-layouts  1.72 us (2%)
    pallas_call x10, Pallas kernels, call(): pl.pallas_call(kernel, out_shape=outs, in_specs=[pl.BlockSpec(memory_spac...  28.5 us
    ppermute x18, starting transfers between devices, swap(): lax.ppermute(block, axis, [(i, i ^ bits) for i in range(lax.axis_size(axi...  25.2 us
    ppermute x18, waiting for transfers between devices, swap(): lax.ppermute(block, axis, [(i, i ^ bits) for i in range(lax.axis_size(axi...  21.9 us
    ppermute x1, starting transfers between devices, local(): lax.ppermute(to_left, 'band', [(i, (i - 1) % band_count) for i in ring])  2.1 us
  transfers between devices with their start and end apart: 20, of which 5 were waited for; matrix products, arithmetic and copies ran while one was open for 0% of the time, Pallas kernels for 33%

profile of v3, /device:TPU:1, one launch (start us, length us, event | category | flops | bytes accessed | tf_op | source)
XLA Modules:
  0.0 80.3 jit_solution(6269697105707333106)
XLA Ops:
  0.0 2.0 %collective-permute-start.2 = (bf16[512,512]{1,0:T(8,128)(2,1)}, bf16[512,512]{1,0:T(8,128)(2,1)S(1)}, u32[]{:S(2)}, u32[]{:S(2)}) collective-permute-start(bf16[512,512]{1,0:T(8,128)(2,1)} %bitcast.16), channel_id=1, source_target_pairs={{0,8},{8,0},{16,24},{24,16},{1,9},{9,1},{17,25},{25,17},{2,10},{10... | collective-permute-start | bytes 1572872 | tf_op jit(solution)/shard_map/ppermute | solution.py:484
  2.0 1.2 %collective-permute-start.3 = (bf16[512,512]{1,0:T(8,128)(2,1)}, bf16[512,512]{1,0:T(8,128)(2,1)S(1)}, u32[]{:S(2)}, u32[]{:S(2)}) collective-permute-start(bf16[512,512]{1,0:T(8,128)(2,1)} %bitcast.18), channel_id=1, source_target_pairs={{0,16},{8,24},{16,0},{24,8},{1,17},{9,25},{17,1},{25,9},{2,18},{10... | collective-permute-start | bytes 1572872 | tf_op jit(solution)/shard_map/ppermute | solution.py:484
  3.3 9.0 %shard_map.154 = (bf16[512,512]{1,0:T(8,128)(2,1)}, bf16[128,512]{1,0:T(8,128)(2,1)}, bf16[128,512]{1,0:T(8,128)(2,1)}) custom-call(f32[16,225]{1,0:T(8,128)} %bitcast.24, bf16[512,512]{1,0:T(8,128)(2,1)} %bitcast.23, bf16[512,1536]{1,0:T(8,128)(2,1)} %wqkv_hbm.2, bf16[512,512]{1,0:T(8,128)(2,1)} %wproj_hbm.2, f32[1,512]{1,0:T(1,128)} %bitcast.25, ...), custom_call_target="tpu_custom_call" | custom-call | flops 3221225472 | bytes 7620672 | tf_op jit(solution)/shard_map/pallas_call | solution.py:467
  12.3 0.3 collective-permute-start
  12.7 2.1 %collective-permute-start.1 = (bf16[128,512]{1,0:T(8,128)(2,1)}, bf16[128,512]{1,0:T(8,128)(2,1)S(1)}, u32[]{:S(2)}, u32[]{:S(2)}) collective-permute-start(bf16[128,512]{1,0:T(8,128)(2,1)} %get-tuple-element.53), channel_id=1, source_target_pairs={{0,24},{8,0},{16,8},{24,16},{1,25},{9,1},{17,9},{25,17},{2,26},{10... | collective-permute-start | bytes 393224 | tf_op jit(solution)/shard_map/ppermute | solution.py:560
  14.8 0.1 copy.18
  14.8 0.1 reshape.52
  14.9 0.1 slice.10
  15.0 0.1 add_xor_fusion.routes_ref
  15.1 0.1 add_convert_fusion.info_ref
  15.2 1.0 %copy-done.1 = bf16[512,512]{1,0:T(8,128)(2,1)S(1)} copy-done((bf16[512,512]{1,0:T(8,128)(2,1)S(1)}, bf16[512,512]{1,0:T(8,128)(2,1)}, u32[]{:S(2)}) %copy-start.1) | copy-done | bytes 524312
  16.2 6.2 %shard_map.155 = (bf16[512,1536]{1,0:T(8,128)(2,1)S(1)}, f32[512,512]{1,0:T(8,128)S(1)}, f32[512,512]{1,0:T(8,128)S(1)}, f32[512,512]{1,0:T(8,128)S(1)}, f32[4,1...) custom-call(s32[2]{0:T(128)S(1)} %add_convert_fusion.info_ref, ...), custom_call_target="tpu_custom_call" | custom-call | flops 805306368 | bytes 8945736 | tf_op jit(solution)/shard_map/pallas_call | solution.py:467
  22.4 0.0 copy-start
  22.4 0.0 copy-start.4
  22.4 0.0 collective-permute-done.from_left_ref
  22.5 0.0 collective-permute-done.1.from_right_ref
  22.5 0.0 collective-permute-done.3.out_second
  22.5 0.2 shard_map.158
  22.7 0.3 collective-permute-start.6
  23.0 0.1 collective-permute-start.7
  23.1 0.4 copy-done
  23.5 4.3 %shard_map.156 = (bf16[512,512]{1,0:T(8,128)(2,1)S(1)}, bf16[128,512]{1,0:T(8,128)(2,1)S(1)}, bf16[128,512]{1,0:T(8,128)(2,1)S(1)}, bf16[128,512]{1,0:T(8,128)(2...) custom-call(s32[2]{0:T(128)S(1)} %add_convert_fusion.info_ref, ...), custom_call_target="tpu_custom_call" | custom-call | flops 1073741824 | bytes 9717768 | tf_op jit(solution)/shard_map/pallas_call | solution.py:467
  27.8 2.4 %collective-permute-start.4 = (bf16[128,512]{1,0:T(8,128)(2,1)S(1)}, bf16[128,512]{1,0:T(8,128)(2,1)S(1)}, u32[]{:S(2)}, u32[]{:S(2)}) collective-permute-start(bf16[128,512]{1,0:T(8,128)(2,1)S(1)} %get-tuple-element.64), channel_id=1, source_target_pairs={{0,4},{1,5},{2,6},{3,7},{4,0},{5,1},{6,2},{7,3},{8,12},{9,13},{10,... | collective-permute-start | bytes 393224 | tf_op jit(solution)/shard_map/ppermute | solution.py:484
  30.2 2.0 %collective-permute-start.5 = (bf16[128,512]{1,0:T(8,128)(2,1)S(1)}, bf16[128,512]{1,0:T(8,128)(2,1)S(1)}, u32[]{:S(2)}, u32[]{:S(2)}) collective-permute-start(bf16[128,512]{1,0:T(8,128)(2,1)S(1)} %get-tuple-element.65), channel_id=1, source_target_pairs={{0,5},{1,4},{2,7},{3,6},{4,1},{5,0},{6,3},{7,2},{8,13},{9,12},{10,... | collective-permute-start | bytes 393224 | tf_op jit(solution)/shard_map/ppermute | solution.py:484
  32.2 2.3 %collective-permute-done.4.refs_0_ = bf16[128,512]{1,0:T(8,128)(2,1)S(1)} collective-permute-done((bf16[128,512]{1,0:T(8,128)(2,1)S(1)}, bf16[128,512]{1,0:T(8,128)(2,1)S(1)}, u32[]{:S(2)}, u32[]{:S(2)}) %collective-permute-start.4) | collective-permute-done | bytes 131104 | tf_op jit(solution)/shard_map/ppermute | solution.py:484
  34.5 7.9 %collective-permute-done.5.refs_1_ = bf16[128,512]{1,0:T(8,128)(2,1)S(1)} collective-permute-done((bf16[128,512]{1,0:T(8,128)(2,1)S(1)}, bf16[128,512]{1,0:T(8,128)(2,1)S(1)}, u32[]{:S(2)}, u32[]{:S(2)}) %collective-permute-start.5) | collective-permute-done | bytes 131104 | tf_op jit(solution)/shard_map/ppermute | solution.py:484
  42.4 3.4 %collective-permute-start.16 = (bf16[128,512]{1,0:T(8,128)(2,1)S(1)}, bf16[128,512]{1,0:T(8,128)(2,1)S(1)}, u32[]{:S(2)}, u32[]{:S(2)}) collective-permute-start(bf16[128,512]{1,0:T(8,128)(2,1)S(1)} %get-tuple-element.91), channel_id=1, source_target_pairs={{0,6},{1,7},{2,4},{3,5},{4,2},{5,3},{6,0},{7,1},{8,14},{9,15},{10,... | collective-permute-start | bytes 393224 | tf_op jit(solution)/shard_map/ppermute | solution.py:484
  45.8 0.0 collective-permute-start.17
  45.8 0.0 collective-permute-done.6.refs_3_
  45.8 1.6 %shard_map.159 = (bf16[128,512]{1,0:T(8,128)(2,1)S(1)}, bf16[128,512]{1,0:T(8,128)(2,1)S(1)}) custom-call(bf16[128,512]{1,0:T(8,128)(2,1)S(1)} %collective-permute-done.4.refs_0_, bf16[128,512]{1,0:T(8,128)(2,1)S(1)} %collective-permute-done.5.refs_1_, bf16[2,512,512]{2,1,0:T(8,128)(2,1)S(1)} %get-tuple-element.73.refs_2_, ...), custom_call_target="tpu_custom_call" | custom-call | flops 1073741824 | bytes 4718592 | tf_op jit(solution)/shard_map/pallas_call | solution.py:467
  47.4 2.8 %collective-permute-start.8 = (bf16[128,512]{1,0:T(8,128)(2,1)S(1)}, bf16[128,512]{1,0:T(8,128)(2,1)S(1)}, u32[]{:S(2)}, u32[]{:S(2)}) collective-permute-start(bf16[128,512]{1,0:T(8,128)(2,1)S(1)} %get-tuple-element.82), channel_id=1, source_target_pairs={{0,1},{1,0},{2,3},{3,2},{4,5},{5,4},{6,7},{7,6},{8,9},{9,8},{10,11... | collective-permute-start | bytes 393224 | tf_op jit(solution)/shard_map/ppermute | solution.py:484
  50.2 1.3 %collective-permute-start.10 = (bf16[128,512]{1,0:T(8,128)(2,1)S(1)}, bf16[128,512]{1,0:T(8,128)(2,1)S(1)}, u32[]{:S(2)}, u32[]{:S(2)}) collective-permute-start(bf16[128,512]{1,0:T(8,128)(2,1)S(1)} %get-tuple-element.85), channel_id=1, source_target_pairs={{0,2},{1,3},{2,0},{3,1},{4,6},{5,7},{6,4},{7,5},{8,10},{9,11},{10,... | collective-permute-start | bytes 393224 | tf_op jit(solution)/shard_map/ppermute | solution.py:484
  51.5 0.4 collective-permute-start.11
  51.9 2.3 %collective-permute-start.14 = (bf16[128,512]{1,0:T(8,128)(2,1)S(1)}, bf16[128,512]{1,0:T(8,128)(2,1)S(1)}, u32[]{:S(2)}, u32[]{:S(2)}) collective-permute-start(bf16[128,512]{1,0:T(8,128)(2,1)S(1)} %get-tuple-element.89), channel_id=1, source_target_pairs={{0,4},{1,5},{2,6},{3,7},{4,0},{5,1},{6,2},{7,3},{8,12},{9,13},{10,... | collective-permute-start | bytes 393224 | tf_op jit(solution)/shard_map/ppermute | solution.py:484
  54.3 2.2 %collective-permute-start.15 = (bf16[128,512]{1,0:T(8,128)(2,1)S(1)}, bf16[128,512]{1,0:T(8,128)(2,1)S(1)}, u32[]{:S(2)}, u32[]{:S(2)}) collective-permute-start(bf16[128,512]{1,0:T(8,128)(2,1)S(1)} %get-tuple-element.90), channel_id=1, source_target_pairs={{0,5},{1,4},{2,7},{3,6},{4,1},{5,0},{6,3},{7,2},{8,13},{9,12},{10,... | collective-permute-start | bytes 393224 | tf_op jit(solution)/shard_map/ppermute | solution.py:484
  56.5 1.6 %shard_map.162 = (bf16[128,512]{1,0:T(8,128)(2,1)S(1)}, bf16[128,512]{1,0:T(8,128)(2,1)S(1)}) custom-call(bf16[128,512]{1,0:T(8,128)(2,1)S(1)} %collective-permute-done.16.refs_0_, bf16[128,512]{1,0:T(8,128)(2,1)S(1)} %collective-permute-done.17.refs_1_, bf16[2,512,512]{2,1,0:T(8,128)(2,1)S(1)} %get-tuple-element.73.refs_2_, ...), custom_call_target="tpu_custom_call" | custom-call | flops 1073741824 | bytes 4718592 | tf_op jit(solution)/shard_map/pallas_call | solution.py:467
  58.1 1.5 %collective-permute-start.18 = (bf16[128,512]{1,0:T(8,128)(2,1)S(1)}, bf16[128,512]{1,0:T(8,128)(2,1)S(1)}, u32[]{:S(2)}, u32[]{:S(2)}) collective-permute-start(bf16[128,512]{1,0:T(8,128)(2,1)S(1)} %get-tuple-element.93), channel_id=1, source_target_pairs={{0,6},{1,7},{2,4},{3,5},{4,2},{5,3},{6,0},{7,1},{8,14},{9,15},{10,... | collective-permute-start | bytes 393224 | tf_op jit(solution)/shard_map/ppermute | solution.py:484
  59.6 1.6 %shard_map.160 = (bf16[128,512]{1,0:T(8,128)(2,1)S(1)}, bf16[128,512]{1,0:T(8,128)(2,1)S(1)}) custom-call(bf16[128,512]{1,0:T(8,128)(2,1)S(1)} %get-tuple-element.81.refs_0_, bf16[128,512]{1,0:T(8,128)(2,1)S(1)} %collective-permute-done.8.refs_1_, bf16[2,512,512]{2,1,0:T(8,128)(2,1)S(1)} %get-tuple-element.73.refs_2_, ...), custom_call_target="tpu_custom_call" | custom-call | flops 1073741824 | bytes 4718592 | tf_op jit(solution)/shard_map/pallas_call | solution.py:467
  61.3 2.2 %collective-permute-start.19 = (bf16[128,512]{1,0:T(8,128)(2,1)S(1)}, bf16[128,512]{1,0:T(8,128)(2,1)S(1)}, u32[]{:S(2)}, u32[]{:S(2)}) collective-permute-start(bf16[128,512]{1,0:T(8,128)(2,1)S(1)} %get-tuple-element.94), channel_id=1, source_target_pairs={{0,7},{1,6},{2,5},{3,4},{4,3},{5,2},{6,1},{7,0},{8,15},{9,14},{10,... | collective-permute-start | bytes 393224 | tf_op jit(solution)/shard_map/ppermute | solution.py:484
  63.4 0.1 collective-permute-start.9
  63.5 1.6 %shard_map.161 = (bf16[128,512]{1,0:T(8,128)(2,1)S(1)}, bf16[128,512]{1,0:T(8,128)(2,1)S(1)}) custom-call(bf16[128,512]{1,0:T(8,128)(2,1)S(1)} %collective-permute-done.10.refs_0_, bf16[128,512]{1,0:T(8,128)(2,1)S(1)} %collective-permute-done.11.refs_1_, bf16[2,512,512]{2,1,0:T(8,128)(2,1)S(1)} %get-tuple-element.73.refs_2_, ...), custom_call_target="tpu_custom_call" | custom-call | flops 1073741824 | bytes 4718592 | tf_op jit(solution)/shard_map/pallas_call | solution.py:467
  65.1 0.1 collective-permute-start.12
  65.2 7.8 %collective-permute-done.15.rest_5_ = bf16[128,512]{1,0:T(8,128)(2,1)S(1)} collective-permute-done((bf16[128,512]{1,0:T(8,128)(2,1)S(1)}, bf16[128,512]{1,0:T(8,128)(2,1)S(1)}, u32[]{:S(2)}, u32[]{:S(2)}) %collective-permute-start.15) | collective-permute-done | bytes 131104 | tf_op jit(solution)/shard_map/ppermute | solution.py:484
  73.0 0.9 %collective-permute-start.13 = (bf16[128,512]{1,0:T(8,128)(2,1)S(1)}, bf16[128,512]{1,0:T(8,128)(2,1)S(1)}, u32[]{:S(2)}, u32[]{:S(2)}) collective-permute-start(bf16[128,512]{1,0:T(8,128)(2,1)S(1)} %get-tuple-element.88), channel_id=1, source_target_pairs={{0,3},{1,2},{2,1},{3,0},{4,7},{5,6},{6,5},{7,4},{8,11},{9,10},{10,... | collective-permute-start | bytes 393224 | tf_op jit(solution)/shard_map/ppermute | solution.py:484
  73.9 0.4 shard_map.157.slot_col_ref
  74.3 1.3 %collective-permute-done.12.rest_2_ = bf16[128,512]{1,0:T(8,128)(2,1)S(1)} collective-permute-done((bf16[128,512]{1,0:T(8,128)(2,1)S(1)}, bf16[128,512]{1,0:T(8,128)(2,1)S(1)}, u32[]{:S(2)}, u32[]{:S(2)}) %collective-permute-start.12) | collective-permute-done | bytes 131104 | tf_op jit(solution)/shard_map/ppermute | solution.py:484
  75.6 2.6 %collective-permute-done.13.rest_3_ = bf16[128,512]{1,0:T(8,128)(2,1)S(1)} collective-permute-done((bf16[128,512]{1,0:T(8,128)(2,1)S(1)}, bf16[128,512]{1,0:T(8,128)(2,1)S(1)}, u32[]{:S(2)}, u32[]{:S(2)}) %collective-permute-start.13) | collective-permute-done | bytes 131104 | tf_op jit(solution)/shard_map/ppermute | solution.py:484
  78.2 1.9 %shard_map.163 = bf16[512,512]{1,0:T(8,128)(2,1)} custom-call(bf16[512,512]{1,0:T(8,128)(2,1)S(1)} %get-tuple-element.63.third_ref, s32[512,128]{1,0:T(8,128)S(1)} %shard_map.157.slot_col_ref, f32[1,512]{1,0:T(1,128)S(1)} %bitcast.21, bf16[128,512]{1,0:T(8,128)(2,1)S(1)} %get-tuple-element.83.rest_0_, bf16[128,512]{1,0:T(8,128)(2,1)S(1)} %collective-permute-done.9.rest_1_, ...), custom_call_target="tpu_custom_call" | custom-call | flops 536870912 | bytes 2361344 | tf_op jit(solution)/shard_map/pallas_call | solution.py:467
  (24 shorter events, 0.1 us)
Async XLA Ops:
  0.0 22.5 %collective-permute-start.2 = (bf16[512,512]{1,0:T(8,128)(2,1)}, bf16[512,512]{1,0:T(8,128)(2,1)S(1)}, u32[]{:S(2)}, u32[]{:S(2)}) collective-permute-start(bf16[512,512]{1,0:T(8,128)(2,1)} %bitcast.16), channel_id=1, source_target_pairs={{0,8},{8,0},{16,24},{24,16},{1,9},{9,1},{17,25},{25,17},{2,10},{10... | collective-permute-start | bytes 1572872 | tf_op jit(solution)/shard_map/ppermute | solution.py:484
  2.0 20.4 %collective-permute-start.3 = (bf16[512,512]{1,0:T(8,128)(2,1)}, bf16[512,512]{1,0:T(8,128)(2,1)S(1)}, u32[]{:S(2)}, u32[]{:S(2)}) collective-permute-start(bf16[512,512]{1,0:T(8,128)(2,1)} %bitcast.18), channel_id=1, source_target_pairs={{0,16},{8,24},{16,0},{24,8},{1,17},{9,25},{17,1},{25,9},{2,18},{10... | collective-permute-start | bytes 1572872 | tf_op jit(solution)/shard_map/ppermute | solution.py:484
  3.3 11.5 %copy-start.7 = (s32[1,1,32,16,1]{2,4,3,1,0:T(1,128)S(1)}, s32[1,1,32,16,1]{2,4,3,1,0:T(1,128)}, u32[]{:S(2)}) copy-start(s32[1,1,32,16,1]{2,4,3,1,0:T(1,128)} %param.17) | copy-start | bytes 6148
  3.3 11.9 %copy-start.6 = (f32[225,16]{0,1:T(8,128)S(1)}, f32[225,16]{0,1:T(8,128)}, u32[]{:S(2)}) copy-start(f32[225,16]{0,1:T(8,128)} %param.27) | copy-start | bytes 43204
  3.3 19.2 %copy-start.2 = (bf16[1,512,512]{2,1,0:T(8,128)(2,1)S(1)}, bf16[1,512,512]{2,1,0:T(8,128)(2,1)}, u32[]{:S(2)}) copy-start(bf16[1,512,512]{2,1,0:T(8,128)(2,1)} %param.29) | copy-start | bytes 1572868
  3.3 19.2 %copy-start.3 = (bf16[1,512,512]{2,1,0:T(8,128)(2,1)S(1)}, bf16[1,512,512]{2,1,0:T(8,128)(2,1)}, u32[]{:S(2)}) copy-start(bf16[1,512,512]{2,1,0:T(8,128)(2,1)} %param.30) | copy-start | bytes 1572868
  12.3 10.1 %collective-permute-start = (bf16[128,512]{1,0:T(8,128)(2,1)}, bf16[128,512]{1,0:T(8,128)(2,1)S(1)}, u32[]{:S(2)}, u32[]{:S(2)}) collective-permute-start(bf16[128,512]{1,0:T(8,128)(2,1)} %get-tuple-element.52), channel_id=1, source_target_pairs={{0,8},{8,16},{16,24},{24,0},{1,9},{9,17},{17,25},{25,1},{2,10},{10... | collective-permute-start | bytes 393224 | tf_op jit(solution)/shard_map/ppermute | solution.py:561
  12.7 9.8 %collective-permute-start.1 = (bf16[128,512]{1,0:T(8,128)(2,1)}, bf16[128,512]{1,0:T(8,128)(2,1)S(1)}, u32[]{:S(2)}, u32[]{:S(2)}) collective-permute-start(bf16[128,512]{1,0:T(8,128)(2,1)} %get-tuple-element.53), channel_id=1, source_target_pairs={{0,24},{8,0},{16,8},{24,16},{1,25},{9,1},{17,9},{25,17},{2,26},{10... | collective-permute-start | bytes 393224 | tf_op jit(solution)/shard_map/ppermute | solution.py:560
  15.2 1.0 %copy-start.1 = (bf16[512,512]{1,0:T(8,128)(2,1)S(1)}, bf16[512,512]{1,0:T(8,128)(2,1)}, u32[]{:S(2)}) copy-start(bf16[512,512]{1,0:T(8,128)(2,1)} %get-tuple-element.50.x_any.x_ref) | copy-start | bytes 1572868
  22.4 1.0 %copy-start = (bf16[512,512]{1,0:T(8,128)(2,1)S(1)}, bf16[512,512]{1,0:T(8,128)(2,1)}, u32[]{:S(2)}) copy-start(bf16[512,512]{1,0:T(8,128)(2,1)} %wproj_hbm.3) | copy-start | bytes 1572868
  22.4 1.0 %copy-start.4 = (f32[512]{0:T(512)S(1)}, f32[512]{0:T(512)}, u32[]{:S(2)}) copy-start(f32[512]{0:T(512)} %param.28) | copy-start | bytes 6148
  22.7 23.1 %collective-permute-start.6 = (bf16[2,512,512]{2,1,0:T(8,128)(2,1)S(1)}, bf16[2,512,512]{2,1,0:T(8,128)(2,1)S(1)}, u32[]{:S(2)}, u32[]{:S(2)}) collective-permute-start(bf16[2,512,512]{2,1,0:T(8,128)(2,1)S(1)} %get-tuple-element.73.refs_2_), channel_id=1, source_target_pairs={{0,16},{8,24},{16,0},{24,8},{1,17},{9,25},{17,1},{25,9},{2,18},{10... | collective-permute-start | bytes 3145736 | tf_op jit(solution)/shard_map/ppermute | solution.py:484
  23.0 22.8 %collective-permute-start.7 = (bf16[2,512,512]{2,1,0:T(8,128)(2,1)S(1)}, bf16[2,512,512]{2,1,0:T(8,128)(2,1)S(1)}, u32[]{:S(2)}, u32[]{:S(2)}) collective-permute-start(bf16[2,512,512]{2,1,0:T(8,128)(2,1)S(1)} %get-tuple-element.74.refs_4_), channel_id=1, source_target_pairs={{0,8},{8,0},{16,24},{24,16},{1,9},{9,1},{17,25},{25,17},{2,10},{10... | collective-permute-start | bytes 3145736 | tf_op jit(solution)/shard_map/ppermute | solution.py:484
  27.8 6.7 %collective-permute-start.4 = (bf16[128,512]{1,0:T(8,128)(2,1)S(1)}, bf16[128,512]{1,0:T(8,128)(2,1)S(1)}, u32[]{:S(2)}, u32[]{:S(2)}) collective-permute-start(bf16[128,512]{1,0:T(8,128)(2,1)S(1)} %get-tuple-element.64), channel_id=1, source_target_pairs={{0,4},{1,5},{2,6},{3,7},{4,0},{5,1},{6,2},{7,3},{8,12},{9,13},{10,... | collective-permute-start | bytes 393224 | tf_op jit(solution)/shard_map/ppermute | solution.py:484
  30.2 12.2 %collective-permute-start.5 = (bf16[128,512]{1,0:T(8,128)(2,1)S(1)}, bf16[128,512]{1,0:T(8,128)(2,1)S(1)}, u32[]{:S(2)}, u32[]{:S(2)}) collective-permute-start(bf16[128,512]{1,0:T(8,128)(2,1)S(1)} %get-tuple-element.65), channel_id=1, source_target_pairs={{0,5},{1,4},{2,7},{3,6},{4,1},{5,0},{6,3},{7,2},{8,13},{9,12},{10,... | collective-permute-start | bytes 393224 | tf_op jit(solution)/shard_map/ppermute | solution.py:484
  42.4 9.5 %collective-permute-start.16 = (bf16[128,512]{1,0:T(8,128)(2,1)S(1)}, bf16[128,512]{1,0:T(8,128)(2,1)S(1)}, u32[]{:S(2)}, u32[]{:S(2)}) collective-permute-start(bf16[128,512]{1,0:T(8,128)(2,1)S(1)} %get-tuple-element.91), channel_id=1, source_target_pairs={{0,6},{1,7},{2,4},{3,5},{4,2},{5,3},{6,0},{7,1},{8,14},{9,15},{10,... | collective-permute-start | bytes 393224 | tf_op jit(solution)/shard_map/ppermute | solution.py:484
  45.8 8.5 %collective-permute-start.17 = (bf16[128,512]{1,0:T(8,128)(2,1)S(1)}, bf16[128,512]{1,0:T(8,128)(2,1)S(1)}, u32[]{:S(2)}, u32[]{:S(2)}) collective-permute-start(bf16[128,512]{1,0:T(8,128)(2,1)S(1)} %get-tuple-element.92), channel_id=1, source_target_pairs={{0,7},{1,6},{2,5},{3,4},{4,3},{5,2},{6,1},{7,0},{8,15},{9,14},{10,... | collective-permute-start | bytes 393224 | tf_op jit(solution)/shard_map/ppermute | solution.py:484
  47.4 10.7 %collective-permute-start.8 = (bf16[128,512]{1,0:T(8,128)(2,1)S(1)}, bf16[128,512]{1,0:T(8,128)(2,1)S(1)}, u32[]{:S(2)}, u32[]{:S(2)}) collective-permute-start(bf16[128,512]{1,0:T(8,128)(2,1)S(1)} %get-tuple-element.82), channel_id=1, source_target_pairs={{0,1},{1,0},{2,3},{3,2},{4,5},{5,4},{6,7},{7,6},{8,9},{9,8},{10,11... | collective-permute-start | bytes 393224 | tf_op jit(solution)/shard_map/ppermute | solution.py:484
  50.2 11.0 %collective-permute-start.10 = (bf16[128,512]{1,0:T(8,128)(2,1)S(1)}, bf16[128,512]{1,0:T(8,128)(2,1)S(1)}, u32[]{:S(2)}, u32[]{:S(2)}) collective-permute-start(bf16[128,512]{1,0:T(8,128)(2,1)S(1)} %get-tuple-element.85), channel_id=1, source_target_pairs={{0,2},{1,3},{2,0},{3,1},{4,6},{5,7},{6,4},{7,5},{8,10},{9,11},{10,... | collective-permute-start | bytes 393224 | tf_op jit(solution)/shard_map/ppermute | solution.py:484
  51.5 11.9 %collective-permute-start.11 = (bf16[128,512]{1,0:T(8,128)(2,1)S(1)}, bf16[128,512]{1,0:T(8,128)(2,1)S(1)}, u32[]{:S(2)}, u32[]{:S(2)}) collective-permute-start(bf16[128,512]{1,0:T(8,128)(2,1)S(1)} %get-tuple-element.86), channel_id=1, source_target_pairs={{0,3},{1,2},{2,1},{3,0},{4,7},{5,6},{6,5},{7,4},{8,11},{9,10},{10,... | collective-permute-start | bytes 393224 | tf_op jit(solution)/shard_map/ppermute | solution.py:484
  51.9 13.2 %collective-permute-start.14 = (bf16[128,512]{1,0:T(8,128)(2,1)S(1)}, bf16[128,512]{1,0:T(8,128)(2,1)S(1)}, u32[]{:S(2)}, u32[]{:S(2)}) collective-permute-start(bf16[128,512]{1,0:T(8,128)(2,1)S(1)} %get-tuple-element.89), channel_id=1, source_target_pairs={{0,4},{1,5},{2,6},{3,7},{4,0},{5,1},{6,2},{7,3},{8,12},{9,13},{10,... | collective-permute-start | bytes 393224 | tf_op jit(solution)/shard_map/ppermute | solution.py:484
  54.3 18.7 %collective-permute-start.15 = (bf16[128,512]{1,0:T(8,128)(2,1)S(1)}, bf16[128,512]{1,0:T(8,128)(2,1)S(1)}, u32[]{:S(2)}, u32[]{:S(2)}) collective-permute-start(bf16[128,512]{1,0:T(8,128)(2,1)S(1)} %get-tuple-element.90), channel_id=1, source_target_pairs={{0,5},{1,4},{2,7},{3,6},{4,1},{5,0},{6,3},{7,2},{8,13},{9,12},{10,... | collective-permute-start | bytes 393224 | tf_op jit(solution)/shard_map/ppermute | solution.py:484
  58.1 16.2 %collective-permute-start.18 = (bf16[128,512]{1,0:T(8,128)(2,1)S(1)}, bf16[128,512]{1,0:T(8,128)(2,1)S(1)}, u32[]{:S(2)}, u32[]{:S(2)}) collective-permute-start(bf16[128,512]{1,0:T(8,128)(2,1)S(1)} %get-tuple-element.93), channel_id=1, source_target_pairs={{0,6},{1,7},{2,4},{3,5},{4,2},{5,3},{6,0},{7,1},{8,14},{9,15},{10,... | collective-permute-start | bytes 393224 | tf_op jit(solution)/shard_map/ppermute | solution.py:484
  61.3 13.0 %collective-permute-start.19 = (bf16[128,512]{1,0:T(8,128)(2,1)S(1)}, bf16[128,512]{1,0:T(8,128)(2,1)S(1)}, u32[]{:S(2)}, u32[]{:S(2)}) collective-permute-start(bf16[128,512]{1,0:T(8,128)(2,1)S(1)} %get-tuple-element.94), channel_id=1, source_target_pairs={{0,7},{1,6},{2,5},{3,4},{4,3},{5,2},{6,1},{7,0},{8,15},{9,14},{10,... | collective-permute-start | bytes 393224 | tf_op jit(solution)/shard_map/ppermute | solution.py:484
  63.4 14.8 %copy-start.5 = (f32[512]{0:T(512)S(1)}, f32[512]{0:T(512)}, u32[]{:S(2)}) copy-start(f32[512]{0:T(512)} %param.31) | copy-start | bytes 6148
  63.4 10.8 %collective-permute-start.9 = (bf16[128,512]{1,0:T(8,128)(2,1)S(1)}, bf16[128,512]{1,0:T(8,128)(2,1)S(1)}, u32[]{:S(2)}, u32[]{:S(2)}) collective-permute-start(bf16[128,512]{1,0:T(8,128)(2,1)S(1)} %get-tuple-element.84), channel_id=1, source_target_pairs={{0,1},{1,0},{2,3},{3,2},{4,5},{5,4},{6,7},{7,6},{8,9},{9,8},{10,11... | collective-permute-start | bytes 393224 | tf_op jit(solution)/shard_map/ppermute | solution.py:484
  65.1 10.5 %collective-permute-start.12 = (bf16[128,512]{1,0:T(8,128)(2,1)S(1)}, bf16[128,512]{1,0:T(8,128)(2,1)S(1)}, u32[]{:S(2)}, u32[]{:S(2)}) collective-permute-start(bf16[128,512]{1,0:T(8,128)(2,1)S(1)} %get-tuple-element.87), channel_id=1, source_target_pairs={{0,2},{1,3},{2,0},{3,1},{4,6},{5,7},{6,4},{7,5},{8,10},{9,11},{10,... | collective-permute-start | bytes 393224 | tf_op jit(solution)/shard_map/ppermute | solution.py:484
  73.0 5.2 %collective-permute-start.13 = (bf16[128,512]{1,0:T(8,128)(2,1)S(1)}, bf16[128,512]{1,0:T(8,128)(2,1)S(1)}, u32[]{:S(2)}, u32[]{:S(2)}) collective-permute-start(bf16[128,512]{1,0:T(8,128)(2,1)S(1)} %get-tuple-element.88), channel_id=1, source_target_pairs={{0,3},{1,2},{2,1},{3,0},{4,7},{5,6},{6,5},{7,4},{8,11},{9,10},{10,... | collective-permute-start | bytes 393224 | tf_op jit(solution)/shard_map/ppermute | solution.py:484

commit v4 on v3

--- a/solution.py
+++ b/solution.py
@@ -341,7 +341,7 @@
     capacity,
     info_ref,
     qkv_ref,
-    x_ref,
+    x_any,
     from_left_ref,
     from_right_ref,
     wqkv_ref,
@@ -354,8 +354,8 @@
     gain_hbm,
     *rest,
 ):
-    third_ref, *out_refs, halo_kv, heads, wproj_ref, gain_ref, sems = rest
-    copies = fetch(sems, (wproj_hbm, wproj_ref), (gain_hbm, gain_ref))
+    third_ref, *out_refs, halo_kv, heads, wproj_ref, gain_ref, x_ref, sems = rest
+    copies = fetch(sems, (wproj_hbm, wproj_ref), (gain_hbm, gain_ref), (x_any, x_ref))
     rows, width = x_ref.shape
     strip = WIN * band_width
     side = WIN * HALF
@@ -617,13 +617,14 @@
             proj_shifted,
             gain_shifted.reshape(1, width),
         ],
-        "svvvvvvvvvvhh",
+        "svavvvvvvvvhh",
         [
             pltpu.VMEM((2 * sent, 2 * width), BF),
             pltpu.VMEM((rows, width), BF),
             pltpu.VMEM((width, width), BF),
             pltpu.VMEM((1, width), F32),
-            pltpu.SemaphoreType.DMA((2,)),
+            pltpu.VMEM((rows, width), BF),
+            pltpu.SemaphoreType.DMA((3,)),
         ],
         flops=2 * rows * width * 4 * width,
     )

time: 80.6 us -> 80.5 us (level)
  no operation moved by 1% of the time
where the time goes in v4:
time: 80.5 us; the launch traced here: 80.3 us
  Pallas kernels  28.5 us (35%)
  starting transfers between devices  27.5 us (34%)
  waiting for transfers between devices  22.1 us (27%)
  local copies, waits for them, and re-layouts  1.72 us (2%)
    pallas_call x10, Pallas kernels, call(): pl.pallas_call(kernel, out_shape=outs, in_specs=[pl.BlockSpec(memory_spac...  28.5 us
    ppermute x18, starting transfers between devices, swap(): lax.ppermute(block, axis, [(i, i ^ bits) for i in range(lax.axis_size(axi...  25.1 us
    ppermute x18, waiting for transfers between devices, swap(): lax.ppermute(block, axis, [(i, i ^ bits) for i in range(lax.axis_size(axi...  22.1 us
    ppermute x1, starting transfers between devices, local(): lax.ppermute(to_left, 'band', [(i, (i - 1) % band_count) for i in ring])  2.1 us
  transfers between devices with their start and end apart: 20, of which 5 were waited for; matrix products, arithmetic and copies ran while one was open for 0% of the time, Pallas kernels for 33%

profile of v4, /device:TPU:1, one launch (start us, length us, event | category | flops | bytes accessed | tf_op | source)
XLA Modules:
  0.0 80.3 jit_solution(1046068034555296897)
XLA Ops:
  0.0 2.0 %collective-permute-start.2 = (bf16[512,512]{1,0:T(8,128)(2,1)}, bf16[512,512]{1,0:T(8,128)(2,1)S(1)}, u32[]{:S(2)}, u32[]{:S(2)}) collective-permute-start(bf16[512,512]{1,0:T(8,128)(2,1)} %bitcast.16), channel_id=1, source_target_pairs={{0,8},{8,0},{16,24},{24,16},{1,9},{9,1},{17,25},{25,17},{2,10},{10... | collective-permute-start | bytes 1572872 | tf_op jit(solution)/shard_map/ppermute | solution.py:484
  2.0 1.2 %collective-permute-start.3 = (bf16[512,512]{1,0:T(8,128)(2,1)}, bf16[512,512]{1,0:T(8,128)(2,1)S(1)}, u32[]{:S(2)}, u32[]{:S(2)}) collective-permute-start(bf16[512,512]{1,0:T(8,128)(2,1)} %bitcast.18), channel_id=1, source_target_pairs={{0,16},{8,24},{16,0},{24,8},{1,17},{9,25},{17,1},{25,9},{2,18},{10... | collective-permute-start | bytes 1572872 | tf_op jit(solution)/shard_map/ppermute | solution.py:484
  3.3 9.0 %shard_map.154 = (bf16[512,512]{1,0:T(8,128)(2,1)}, bf16[128,512]{1,0:T(8,128)(2,1)}, bf16[128,512]{1,0:T(8,128)(2,1)}) custom-call(f32[16,225]{1,0:T(8,128)} %bitcast.24, bf16[512,512]{1,0:T(8,128)(2,1)} %bitcast.23, bf16[512,1536]{1,0:T(8,128)(2,1)} %wqkv_hbm.2, bf16[512,512]{1,0:T(8,128)(2,1)} %wproj_hbm.2, f32[1,512]{1,0:T(1,128)} %bitcast.25, ...), custom_call_target="tpu_custom_call" | custom-call | flops 3221225472 | bytes 7620672 | tf_op jit(solution)/shard_map/pallas_call | solution.py:467
  12.3 0.3 collective-permute-start
  12.7 2.1 %collective-permute-start.1 = (bf16[128,512]{1,0:T(8,128)(2,1)}, bf16[128,512]{1,0:T(8,128)(2,1)S(1)}, u32[]{:S(2)}, u32[]{:S(2)}) collective-permute-start(bf16[128,512]{1,0:T(8,128)(2,1)} %get-tuple-element.53), channel_id=1, source_target_pairs={{0,24},{8,0},{16,8},{24,16},{1,25},{9,1},{17,9},{25,17},{2,26},{10... | collective-permute-start | bytes 393224 | tf_op jit(solution)/shard_map/ppermute | solution.py:560
  14.8 0.1 copy.18
  14.8 0.1 reshape.52
  14.9 0.1 slice.10
  15.0 0.1 add_xor_fusion.routes_ref
  15.1 0.1 add_convert_fusion.info_ref
  15.2 1.0 %copy-done.1 = bf16[512,512]{1,0:T(8,128)(2,1)S(1)} copy-done((bf16[512,512]{1,0:T(8,128)(2,1)S(1)}, bf16[512,512]{1,0:T(8,128)(2,1)}, u32[]{:S(2)}) %copy-start.1) | copy-done | bytes 524312
  16.2 6.2 %shard_map.155 = (bf16[512,1536]{1,0:T(8,128)(2,1)S(1)}, f32[512,512]{1,0:T(8,128)S(1)}, f32[512,512]{1,0:T(8,128)S(1)}, f32[512,512]{1,0:T(8,128)S(1)}, f32[4,1...) custom-call(s32[2]{0:T(128)S(1)} %add_convert_fusion.info_ref, ...), custom_call_target="tpu_custom_call" | custom-call | flops 805306368 | bytes 8945736 | tf_op jit(solution)/shard_map/pallas_call | solution.py:467
  22.4 0.0 copy-start
  22.4 0.0 copy-start.4
  22.4 0.0 collective-permute-done.from_left_ref
  22.5 0.0 collective-permute-done.1.from_right_ref
  22.5 0.0 collective-permute-done.3.out_second
  22.5 0.2 shard_map.158
  22.7 0.3 collective-permute-start.6
  23.0 0.1 collective-permute-start.7
  23.1 0.4 copy-done
  23.5 4.3 %shard_map.156 = (bf16[512,512]{1,0:T(8,128)(2,1)S(1)}, bf16[128,512]{1,0:T(8,128)(2,1)S(1)}, bf16[128,512]{1,0:T(8,128)(2,1)S(1)}, bf16[128,512]{1,0:T(8,128)(2...) custom-call(s32[2]{0:T(128)S(1)} %add_convert_fusion.info_ref, ...), custom_call_target="tpu_custom_call" | custom-call | flops 1073741824 | bytes 9717768 | tf_op jit(solution)/shard_map/pallas_call | solution.py:467
  27.8 2.4 %collective-permute-start.4 = (bf16[128,512]{1,0:T(8,128)(2,1)S(1)}, bf16[128,512]{1,0:T(8,128)(2,1)S(1)}, u32[]{:S(2)}, u32[]{:S(2)}) collective-permute-start(bf16[128,512]{1,0:T(8,128)(2,1)S(1)} %get-tuple-element.64), channel_id=1, source_target_pairs={{0,4},{1,5},{2,6},{3,7},{4,0},{5,1},{6,2},{7,3},{8,12},{9,13},{10,... | collective-permute-start | bytes 393224 | tf_op jit(solution)/shard_map/ppermute | solution.py:484
  30.2 2.0 %collective-permute-start.5 = (bf16[128,512]{1,0:T(8,128)(2,1)S(1)}, bf16[128,512]{1,0:T(8,128)(2,1)S(1)}, u32[]{:S(2)}, u32[]{:S(2)}) collective-permute-start(bf16[128,512]{1,0:T(8,128)(2,1)S(1)} %get-tuple-element.65), channel_id=1, source_target_pairs={{0,5},{1,4},{2,7},{3,6},{4,1},{5,0},{6,3},{7,2},{8,13},{9,12},{10,... | collective-permute-start | bytes 393224 | tf_op jit(solution)/shard_map/ppermute | solution.py:484
  32.2 2.3 %collective-permute-done.4.refs_0_ = bf16[128,512]{1,0:T(8,128)(2,1)S(1)} collective-permute-done((bf16[128,512]{1,0:T(8,128)(2,1)S(1)}, bf16[128,512]{1,0:T(8,128)(2,1)S(1)}, u32[]{:S(2)}, u32[]{:S(2)}) %collective-permute-start.4) | collective-permute-done | bytes 131104 | tf_op jit(solution)/shard_map/ppermute | solution.py:484
  34.5 7.9 %collective-permute-done.5.refs_1_ = bf16[128,512]{1,0:T(8,128)(2,1)S(1)} collective-permute-done((bf16[128,512]{1,0:T(8,128)(2,1)S(1)}, bf16[128,512]{1,0:T(8,128)(2,1)S(1)}, u32[]{:S(2)}, u32[]{:S(2)}) %collective-permute-start.5) | collective-permute-done | bytes 131104 | tf_op jit(solution)/shard_map/ppermute | solution.py:484
  42.4 3.4 %collective-permute-start.16 = (bf16[128,512]{1,0:T(8,128)(2,1)S(1)}, bf16[128,512]{1,0:T(8,128)(2,1)S(1)}, u32[]{:S(2)}, u32[]{:S(2)}) collective-permute-start(bf16[128,512]{1,0:T(8,128)(2,1)S(1)} %get-tuple-element.91), channel_id=1, source_target_pairs={{0,6},{1,7},{2,4},{3,5},{4,2},{5,3},{6,0},{7,1},{8,14},{9,15},{10,... | collective-permute-start | bytes 393224 | tf_op jit(solution)/shard_map/ppermute | solution.py:484
  45.9 1.6 %shard_map.159 = (bf16[128,512]{1,0:T(8,128)(2,1)S(1)}, bf16[128,512]{1,0:T(8,128)(2,1)S(1)}) custom-call(bf16[128,512]{1,0:T(8,128)(2,1)S(1)} %collective-permute-done.4.refs_0_, bf16[128,512]{1,0:T(8,128)(2,1)S(1)} %collective-permute-done.5.refs_1_, bf16[2,512,512]{2,1,0:T(8,128)(2,1)S(1)} %get-tuple-element.73.refs_2_, ...), custom_call_target="tpu_custom_call" | custom-call | flops 1073741824 | bytes 4718592 | tf_op jit(solution)/shard_map/pallas_call | solution.py:467
  47.5 2.8 %collective-permute-start.8 = (bf16[128,512]{1,0:T(8,128)(2,1)S(1)}, bf16[128,512]{1,0:T(8,128)(2,1)S(1)}, u32[]{:S(2)}, u32[]{:S(2)}) collective-permute-start(bf16[128,512]{1,0:T(8,128)(2,1)S(1)} %get-tuple-element.82), channel_id=1, source_target_pairs={{0,1},{1,0},{2,3},{3,2},{4,5},{5,4},{6,7},{7,6},{8,9},{9,8},{10,11... | collective-permute-start | bytes 393224 | tf_op jit(solution)/shard_map/ppermute | solution.py:484
  50.2 1.3 %collective-permute-start.10 = (bf16[128,512]{1,0:T(8,128)(2,1)S(1)}, bf16[128,512]{1,0:T(8,128)(2,1)S(1)}, u32[]{:S(2)}, u32[]{:S(2)}) collective-permute-start(bf16[128,512]{1,0:T(8,128)(2,1)S(1)} %get-tuple-element.85), channel_id=1, source_target_pairs={{0,2},{1,3},{2,0},{3,1},{4,6},{5,7},{6,4},{7,5},{8,10},{9,11},{10,... | collective-permute-start | bytes 393224 | tf_op jit(solution)/shard_map/ppermute | solution.py:484
  51.5 0.4 collective-permute-start.11
  51.9 2.3 %collective-permute-start.14 = (bf16[128,512]{1,0:T(8,128)(2,1)S(1)}, bf16[128,512]{1,0:T(8,128)(2,1)S(1)}, u32[]{:S(2)}, u32[]{:S(2)}) collective-permute-start(bf16[128,512]{1,0:T(8,128)(2,1)S(1)} %get-tuple-element.89), channel_id=1, source_target_pairs={{0,4},{1,5},{2,6},{3,7},{4,0},{5,1},{6,2},{7,3},{8,12},{9,13},{10,... | collective-permute-start | bytes 393224 | tf_op jit(solution)/shard_map/ppermute | solution.py:484
  54.3 2.3 %collective-permute-start.15 = (bf16[128,512]{1,0:T(8,128)(2,1)S(1)}, bf16[128,512]{1,0:T(8,128)(2,1)S(1)}, u32[]{:S(2)}, u32[]{:S(2)}) collective-permute-start(bf16[128,512]{1,0:T(8,128)(2,1)S(1)} %get-tuple-element.90), channel_id=1, source_target_pairs={{0,5},{1,4},{2,7},{3,6},{4,1},{5,0},{6,3},{7,2},{8,13},{9,12},{10,... | collective-permute-start | bytes 393224 | tf_op jit(solution)/shard_map/ppermute | solution.py:484
  56.5 1.6 %shard_map.162 = (bf16[128,512]{1,0:T(8,128)(2,1)S(1)}, bf16[128,512]{1,0:T(8,128)(2,1)S(1)}) custom-call(bf16[128,512]{1,0:T(8,128)(2,1)S(1)} %collective-permute-done.16.refs_0_, bf16[128,512]{1,0:T(8,128)(2,1)S(1)} %collective-permute-done.17.refs_1_, bf16[2,512,512]{2,1,0:T(8,128)(2,1)S(1)} %get-tuple-element.73.refs_2_, ...), custom_call_target="tpu_custom_call" | custom-call | flops 1073741824 | bytes 4718592 | tf_op jit(solution)/shard_map/pallas_call | solution.py:467
  58.1 0.0 collective-permute-done.8.refs_1_
  58.1 1.5 %collective-permute-start.18 = (bf16[128,512]{1,0:T(8,128)(2,1)S(1)}, bf16[128,512]{1,0:T(8,128)(2,1)S(1)}, u32[]{:S(2)}, u32[]{:S(2)}) collective-permute-start(bf16[128,512]{1,0:T(8,128)(2,1)S(1)} %get-tuple-element.93), channel_id=1, source_target_pairs={{0,6},{1,7},{2,4},{3,5},{4,2},{5,3},{6,0},{7,1},{8,14},{9,15},{10,... | collective-permute-start | bytes 393224 | tf_op jit(solution)/shard_map/ppermute | solution.py:484
  59.6 1.6 %shard_map.160 = (bf16[128,512]{1,0:T(8,128)(2,1)S(1)}, bf16[128,512]{1,0:T(8,128)(2,1)S(1)}) custom-call(bf16[128,512]{1,0:T(8,128)(2,1)S(1)} %get-tuple-element.81.refs_0_, bf16[128,512]{1,0:T(8,128)(2,1)S(1)} %collective-permute-done.8.refs_1_, bf16[2,512,512]{2,1,0:T(8,128)(2,1)S(1)} %get-tuple-element.73.refs_2_, ...), custom_call_target="tpu_custom_call" | custom-call | flops 1073741824 | bytes 4718592 | tf_op jit(solution)/shard_map/pallas_call | solution.py:467
  61.3 2.2 %collective-permute-start.19 = (bf16[128,512]{1,0:T(8,128)(2,1)S(1)}, bf16[128,512]{1,0:T(8,128)(2,1)S(1)}, u32[]{:S(2)}, u32[]{:S(2)}) collective-permute-start(bf16[128,512]{1,0:T(8,128)(2,1)S(1)} %get-tuple-element.94), channel_id=1, source_target_pairs={{0,7},{1,6},{2,5},{3,4},{4,3},{5,2},{6,1},{7,0},{8,15},{9,14},{10,... | collective-permute-start | bytes 393224 | tf_op jit(solution)/shard_map/ppermute | solution.py:484
  63.5 0.0 collective-permute-done.11.refs_1_
  63.5 0.1 collective-permute-start.9
  63.5 1.6 %shard_map.161 = (bf16[128,512]{1,0:T(8,128)(2,1)S(1)}, bf16[128,512]{1,0:T(8,128)(2,1)S(1)}) custom-call(bf16[128,512]{1,0:T(8,128)(2,1)S(1)} %collective-permute-done.10.refs_0_, bf16[128,512]{1,0:T(8,128)(2,1)S(1)} %collective-permute-done.11.refs_1_, bf16[2,512,512]{2,1,0:T(8,128)(2,1)S(1)} %get-tuple-element.73.refs_2_, ...), custom_call_target="tpu_custom_call" | custom-call | flops 1073741824 | bytes 4718592 | tf_op jit(solution)/shard_map/pallas_call | solution.py:467
  65.2 0.1 collective-permute-start.12
  65.2 7.9 %collective-permute-done.15.rest_5_ = bf16[128,512]{1,0:T(8,128)(2,1)S(1)} collective-permute-done((bf16[128,512]{1,0:T(8,128)(2,1)S(1)}, bf16[128,512]{1,0:T(8,128)(2,1)S(1)}, u32[]{:S(2)}, u32[]{:S(2)}) %collective-permute-start.15) | collective-permute-done | bytes 131104 | tf_op jit(solution)/shard_map/ppermute | solution.py:484
  73.1 0.8 collective-permute-start.13
  73.9 0.4 shard_map.157.slot_col_ref
  74.3 1.3 %collective-permute-done.12.rest_2_ = bf16[128,512]{1,0:T(8,128)(2,1)S(1)} collective-permute-done((bf16[128,512]{1,0:T(8,128)(2,1)S(1)}, bf16[128,512]{1,0:T(8,128)(2,1)S(1)}, u32[]{:S(2)}, u32[]{:S(2)}) %collective-permute-start.12) | collective-permute-done | bytes 131104 | tf_op jit(solution)/shard_map/ppermute | solution.py:484
  75.6 2.6 %collective-permute-done.13.rest_3_ = bf16[128,512]{1,0:T(8,128)(2,1)S(1)} collective-permute-done((bf16[128,512]{1,0:T(8,128)(2,1)S(1)}, bf16[128,512]{1,0:T(8,128)(2,1)S(1)}, u32[]{:S(2)}, u32[]{:S(2)}) %collective-permute-start.13) | collective-permute-done | bytes 131104 | tf_op jit(solution)/shard_map/ppermute | solution.py:484
  78.3 1.9 %shard_map.163 = bf16[512,512]{1,0:T(8,128)(2,1)} custom-call(bf16[512,512]{1,0:T(8,128)(2,1)S(1)} %get-tuple-element.63.third_ref, s32[512,128]{1,0:T(8,128)S(1)} %shard_map.157.slot_col_ref, f32[1,512]{1,0:T(1,128)S(1)} %bitcast.21, bf16[128,512]{1,0:T(8,128)(2,1)S(1)} %get-tuple-element.83.rest_0_, bf16[128,512]{1,0:T(8,128)(2,1)S(1)} %collective-permute-done.9.rest_1_, ...), custom_call_target="tpu_custom_call" | custom-call | flops 536870912 | bytes 2361344 | tf_op jit(solution)/shard_map/pallas_call | solution.py:467
  (24 shorter events, 0.1 us)
Async XLA Ops:
  0.0 22.5 %collective-permute-start.2 = (bf16[512,512]{1,0:T(8,128)(2,1)}, bf16[512,512]{1,0:T(8,128)(2,1)S(1)}, u32[]{:S(2)}, u32[]{:S(2)}) collective-permute-start(bf16[512,512]{1,0:T(8,128)(2,1)} %bitcast.16), channel_id=1, source_target_pairs={{0,8},{8,0},{16,24},{24,16},{1,9},{9,1},{17,25},{25,17},{2,10},{10... | collective-permute-start | bytes 1572872 | tf_op jit(solution)/shard_map/ppermute | solution.py:484
  2.0 20.4 %collective-permute-start.3 = (bf16[512,512]{1,0:T(8,128)(2,1)}, bf16[512,512]{1,0:T(8,128)(2,1)S(1)}, u32[]{:S(2)}, u32[]{:S(2)}) collective-permute-start(bf16[512,512]{1,0:T(8,128)(2,1)} %bitcast.18), channel_id=1, source_target_pairs={{0,16},{8,24},{16,0},{24,8},{1,17},{9,25},{17,1},{25,9},{2,18},{10... | collective-permute-start | bytes 1572872 | tf_op jit(solution)/shard_map/ppermute | solution.py:484
  3.3 11.5 %copy-start.7 = (s32[1,1,32,16,1]{2,4,3,1,0:T(1,128)S(1)}, s32[1,1,32,16,1]{2,4,3,1,0:T(1,128)}, u32[]{:S(2)}) copy-start(s32[1,1,32,16,1]{2,4,3,1,0:T(1,128)} %param.17) | copy-start | bytes 6148
  3.3 11.9 %copy-start.6 = (f32[225,16]{0,1:T(8,128)S(1)}, f32[225,16]{0,1:T(8,128)}, u32[]{:S(2)}) copy-start(f32[225,16]{0,1:T(8,128)} %param.27) | copy-start | bytes 43204
  3.3 19.2 %copy-start.2 = (bf16[1,512,512]{2,1,0:T(8,128)(2,1)S(1)}, bf16[1,512,512]{2,1,0:T(8,128)(2,1)}, u32[]{:S(2)}) copy-start(bf16[1,512,512]{2,1,0:T(8,128)(2,1)} %param.29) | copy-start | bytes 1572868
  3.3 19.2 %copy-start.3 = (bf16[1,512,512]{2,1,0:T(8,128)(2,1)S(1)}, bf16[1,512,512]{2,1,0:T(8,128)(2,1)}, u32[]{:S(2)}) copy-start(bf16[1,512,512]{2,1,0:T(8,128)(2,1)} %param.30) | copy-start | bytes 1572868
  12.3 10.1 %collective-permute-start = (bf16[128,512]{1,0:T(8,128)(2,1)}, bf16[128,512]{1,0:T(8,128)(2,1)S(1)}, u32[]{:S(2)}, u32[]{:S(2)}) collective-permute-start(bf16[128,512]{1,0:T(8,128)(2,1)} %get-tuple-element.52), channel_id=1, source_target_pairs={{0,8},{8,16},{16,24},{24,0},{1,9},{9,17},{17,25},{25,1},{2,10},{10... | collective-permute-start | bytes 393224 | tf_op jit(solution)/shard_map/ppermute | solution.py:561
  12.7 9.8 %collective-permute-start.1 = (bf16[128,512]{1,0:T(8,128)(2,1)}, bf16[128,512]{1,0:T(8,128)(2,1)S(1)}, u32[]{:S(2)}, u32[]{:S(2)}) collective-permute-start(bf16[128,512]{1,0:T(8,128)(2,1)} %get-tuple-element.53), channel_id=1, source_target_pairs={{0,24},{8,0},{16,8},{24,16},{1,25},{9,1},{17,9},{25,17},{2,26},{10... | collective-permute-start | bytes 393224 | tf_op jit(solution)/shard_map/ppermute | solution.py:560
  15.2 1.0 %copy-start.1 = (bf16[512,512]{1,0:T(8,128)(2,1)S(1)}, bf16[512,512]{1,0:T(8,128)(2,1)}, u32[]{:S(2)}) copy-start(bf16[512,512]{1,0:T(8,128)(2,1)} %get-tuple-element.50.x_any) | copy-start | bytes 1572868
  22.4 1.0 %copy-start = (bf16[512,512]{1,0:T(8,128)(2,1)S(1)}, bf16[512,512]{1,0:T(8,128)(2,1)}, u32[]{:S(2)}) copy-start(bf16[512,512]{1,0:T(8,128)(2,1)} %wproj_hbm.3) | copy-start | bytes 1572868
  22.4 1.0 %copy-start.4 = (f32[512]{0:T(512)S(1)}, f32[512]{0:T(512)}, u32[]{:S(2)}) copy-start(f32[512]{0:T(512)} %param.28) | copy-start | bytes 6148
  22.7 23.1 %collective-permute-start.6 = (bf16[2,512,512]{2,1,0:T(8,128)(2,1)S(1)}, bf16[2,512,512]{2,1,0:T(8,128)(2,1)S(1)}, u32[]{:S(2)}, u32[]{:S(2)}) collective-permute-start(bf16[2,512,512]{2,1,0:T(8,128)(2,1)S(1)} %get-tuple-element.73.refs_2_), channel_id=1, source_target_pairs={{0,16},{8,24},{16,0},{24,8},{1,17},{9,25},{17,1},{25,9},{2,18},{10... | collective-permute-start | bytes 3145736 | tf_op jit(solution)/shard_map/ppermute | solution.py:484
  23.0 22.9 %collective-permute-start.7 = (bf16[2,512,512]{2,1,0:T(8,128)(2,1)S(1)}, bf16[2,512,512]{2,1,0:T(8,128)(2,1)S(1)}, u32[]{:S(2)}, u32[]{:S(2)}) collective-permute-start(bf16[2,512,512]{2,1,0:T(8,128)(2,1)S(1)} %get-tuple-element.74.refs_4_), channel_id=1, source_target_pairs={{0,8},{8,0},{16,24},{24,16},{1,9},{9,1},{17,25},{25,17},{2,10},{10... | collective-permute-start | bytes 3145736 | tf_op jit(solution)/shard_map/ppermute | solution.py:484
  27.8 6.7 %collective-permute-start.4 = (bf16[128,512]{1,0:T(8,128)(2,1)S(1)}, bf16[128,512]{1,0:T(8,128)(2,1)S(1)}, u32[]{:S(2)}, u32[]{:S(2)}) collective-permute-start(bf16[128,512]{1,0:T(8,128)(2,1)S(1)} %get-tuple-element.64), channel_id=1, source_target_pairs={{0,4},{1,5},{2,6},{3,7},{4,0},{5,1},{6,2},{7,3},{8,12},{9,13},{10,... | collective-permute-start | bytes 393224 | tf_op jit(solution)/shard_map/ppermute | solution.py:484
  30.2 12.2 %collective-permute-start.5 = (bf16[128,512]{1,0:T(8,128)(2,1)S(1)}, bf16[128,512]{1,0:T(8,128)(2,1)S(1)}, u32[]{:S(2)}, u32[]{:S(2)}) collective-permute-start(bf16[128,512]{1,0:T(8,128)(2,1)S(1)} %get-tuple-element.65), channel_id=1, source_target_pairs={{0,5},{1,4},{2,7},{3,6},{4,1},{5,0},{6,3},{7,2},{8,13},{9,12},{10,... | collective-permute-start | bytes 393224 | tf_op jit(solution)/shard_map/ppermute | solution.py:484
  42.4 9.5 %collective-permute-start.16 = (bf16[128,512]{1,0:T(8,128)(2,1)S(1)}, bf16[128,512]{1,0:T(8,128)(2,1)S(1)}, u32[]{:S(2)}, u32[]{:S(2)}) collective-permute-start(bf16[128,512]{1,0:T(8,128)(2,1)S(1)} %get-tuple-element.91), channel_id=1, source_target_pairs={{0,6},{1,7},{2,4},{3,5},{4,2},{5,3},{6,0},{7,1},{8,14},{9,15},{10,... | collective-permute-start | bytes 393224 | tf_op jit(solution)/shard_map/ppermute | solution.py:484
  45.8 8.4 %collective-permute-start.17 = (bf16[128,512]{1,0:T(8,128)(2,1)S(1)}, bf16[128,512]{1,0:T(8,128)(2,1)S(1)}, u32[]{:S(2)}, u32[]{:S(2)}) collective-permute-start(bf16[128,512]{1,0:T(8,128)(2,1)S(1)} %get-tuple-element.92), channel_id=1, source_target_pairs={{0,7},{1,6},{2,5},{3,4},{4,3},{5,2},{6,1},{7,0},{8,15},{9,14},{10,... | collective-permute-start | bytes 393224 | tf_op jit(solution)/shard_map/ppermute | solution.py:484
  47.5 10.7 %collective-permute-start.8 = (bf16[128,512]{1,0:T(8,128)(2,1)S(1)}, bf16[128,512]{1,0:T(8,128)(2,1)S(1)}, u32[]{:S(2)}, u32[]{:S(2)}) collective-permute-start(bf16[128,512]{1,0:T(8,128)(2,1)S(1)} %get-tuple-element.82), channel_id=1, source_target_pairs={{0,1},{1,0},{2,3},{3,2},{4,5},{5,4},{6,7},{7,6},{8,9},{9,8},{10,11... | collective-permute-start | bytes 393224 | tf_op jit(solution)/shard_map/ppermute | solution.py:484
  50.2 11.0 %collective-permute-start.10 = (bf16[128,512]{1,0:T(8,128)(2,1)S(1)}, bf16[128,512]{1,0:T(8,128)(2,1)S(1)}, u32[]{:S(2)}, u32[]{:S(2)}) collective-permute-start(bf16[128,512]{1,0:T(8,128)(2,1)S(1)} %get-tuple-element.85), channel_id=1, source_target_pairs={{0,2},{1,3},{2,0},{3,1},{4,6},{5,7},{6,4},{7,5},{8,10},{9,11},{10,... | collective-permute-start | bytes 393224 | tf_op jit(solution)/shard_map/ppermute | solution.py:484
  51.5 11.9 %collective-permute-start.11 = (bf16[128,512]{1,0:T(8,128)(2,1)S(1)}, bf16[128,512]{1,0:T(8,128)(2,1)S(1)}, u32[]{:S(2)}, u32[]{:S(2)}) collective-permute-start(bf16[128,512]{1,0:T(8,128)(2,1)S(1)} %get-tuple-element.86), channel_id=1, source_target_pairs={{0,3},{1,2},{2,1},{3,0},{4,7},{5,6},{6,5},{7,4},{8,11},{9,10},{10,... | collective-permute-start | bytes 393224 | tf_op jit(solution)/shard_map/ppermute | solution.py:484
  51.9 13.2 %collective-permute-start.14 = (bf16[128,512]{1,0:T(8,128)(2,1)S(1)}, bf16[128,512]{1,0:T(8,128)(2,1)S(1)}, u32[]{:S(2)}, u32[]{:S(2)}) collective-permute-start(bf16[128,512]{1,0:T(8,128)(2,1)S(1)} %get-tuple-element.89), channel_id=1, source_target_pairs={{0,4},{1,5},{2,6},{3,7},{4,0},{5,1},{6,2},{7,3},{8,12},{9,13},{10,... | collective-permute-start | bytes 393224 | tf_op jit(solution)/shard_map/ppermute | solution.py:484
  54.3 18.8 %collective-permute-start.15 = (bf16[128,512]{1,0:T(8,128)(2,1)S(1)}, bf16[128,512]{1,0:T(8,128)(2,1)S(1)}, u32[]{:S(2)}, u32[]{:S(2)}) collective-permute-start(bf16[128,512]{1,0:T(8,128)(2,1)S(1)} %get-tuple-element.90), channel_id=1, source_target_pairs={{0,5},{1,4},{2,7},{3,6},{4,1},{5,0},{6,3},{7,2},{8,13},{9,12},{10,... | collective-permute-start | bytes 393224 | tf_op jit(solution)/shard_map/ppermute | solution.py:484
  58.1 16.1 %collective-permute-start.18 = (bf16[128,512]{1,0:T(8,128)(2,1)S(1)}, bf16[128,512]{1,0:T(8,128)(2,1)S(1)}, u32[]{:S(2)}, u32[]{:S(2)}) collective-permute-start(bf16[128,512]{1,0:T(8,128)(2,1)S(1)} %get-tuple-element.93), channel_id=1, source_target_pairs={{0,6},{1,7},{2,4},{3,5},{4,2},{5,3},{6,0},{7,1},{8,14},{9,15},{10,... | collective-permute-start | bytes 393224 | tf_op jit(solution)/shard_map/ppermute | solution.py:484
  61.3 13.0 %collective-permute-start.19 = (bf16[128,512]{1,0:T(8,128)(2,1)S(1)}, bf16[128,512]{1,0:T(8,128)(2,1)S(1)}, u32[]{:S(2)}, u32[]{:S(2)}) collective-permute-start(bf16[128,512]{1,0:T(8,128)(2,1)S(1)} %get-tuple-element.94), channel_id=1, source_target_pairs={{0,7},{1,6},{2,5},{3,4},{4,3},{5,2},{6,1},{7,0},{8,15},{9,14},{10,... | collective-permute-start | bytes 393224 | tf_op jit(solution)/shard_map/ppermute | solution.py:484
  63.5 14.8 %copy-start.5 = (f32[512]{0:T(512)S(1)}, f32[512]{0:T(512)}, u32[]{:S(2)}) copy-start(f32[512]{0:T(512)} %param.31) | copy-start | bytes 6148
  63.5 10.8 %collective-permute-start.9 = (bf16[128,512]{1,0:T(8,128)(2,1)S(1)}, bf16[128,512]{1,0:T(8,128)(2,1)S(1)}, u32[]{:S(2)}, u32[]{:S(2)}) collective-permute-start(bf16[128,512]{1,0:T(8,128)(2,1)S(1)} %get-tuple-element.84), channel_id=1, source_target_pairs={{0,1},{1,0},{2,3},{3,2},{4,5},{5,4},{6,7},{7,6},{8,9},{9,8},{10,11... | collective-permute-start | bytes 393224 | tf_op jit(solution)/shard_map/ppermute | solution.py:484
  65.2 10.5 %collective-permute-start.12 = (bf16[128,512]{1,0:T(8,128)(2,1)S(1)}, bf16[128,512]{1,0:T(8,128)(2,1)S(1)}, u32[]{:S(2)}, u32[]{:S(2)}) collective-permute-start(bf16[128,512]{1,0:T(8,128)(2,1)S(1)} %get-tuple-element.87), channel_id=1, source_target_pairs={{0,2},{1,3},{2,0},{3,1},{4,6},{5,7},{6,4},{7,5},{8,10},{9,11},{10,... | collective-permute-start | bytes 393224 | tf_op jit(solution)/shard_map/ppermute | solution.py:484
  73.1 5.2 %collective-permute-start.13 = (bf16[128,512]{1,0:T(8,128)(2,1)S(1)}, bf16[128,512]{1,0:T(8,128)(2,1)S(1)}, u32[]{:S(2)}, u32[]{:S(2)}) collective-permute-start(bf16[128,512]{1,0:T(8,128)(2,1)S(1)} %get-tuple-element.88), channel_id=1, source_target_pairs={{0,3},{1,2},{2,1},{3,0},{4,7},{5,6},{6,5},{7,4},{8,11},{9,10},{10,... | collective-permute-start | bytes 393224 | tf_op jit(solution)/shard_map/ppermute | solution.py:484
